TPU v7x, 32 devices: a whole 2x2x4 slice. The times are simulated.
32 devices in a mesh: groups: 2 (over x), tile: 16 (over z, y, core).
Axes of the slice: x: 2, y: 2, z: 4, core: 2. Of those that a mesh axis runs over, the one named last changes fastest.
Arguments:
- coarse_solution: bfloat16 [32, 2, 4096], P(('groups', 'tile')), parts along dimension 0, may hold values from -6 to 6
- geometry: int32 [32, 4096], P(('groups', 'tile')), parts along dimension 0, may hold values 0 or 1
- fine_fields: bfloat16 [32, 3, 2, 2, 256, 256], P('groups', None, None, None, 'tile'), parts along dimension 0, may hold values from -6 to 6
- cotangent: bfloat16 [32, 3, 2, 2, 256, 256], P('groups', None, None, None, 'tile'), parts along dimension 0, may hold values from -0.046875 to 0.046875
- sample_ids: int32 [32], P('groups'), parts along dimension 0, may hold values from 0 to 15, each once
- first_weight: bfloat16 [3, 3, 3, 128], replicated, may hold values from -1.25 to 1.25
- dilated_weight: bfloat16 [3, 3, 128, 128], replicated, may hold values from -0.1875 to 0.1875
- project_weight: bfloat16 [128, 128], replicated, may hold values from -0.5 to 0.5
- down_weight: bfloat16 [3, 4, 4, 128], replicated, may hold values from -0.875 to 0.875
- up_weight: bfloat16 [4, 4, 6, 128], replicated, may hold values from -0.25 to 0.25
Outputs:
- prediction: bfloat16 [32, 3, 2, 2, 256, 256], P('groups', None, None, None, 'tile'), parts along dimension 0
- first_grad: float32 [6, 3, 3, 128], P('groups'), parts along dimension 0
- dilated_grad: float32 [6, 3, 128, 128], P('groups'), parts along dimension 0
- project_grad: float32 [256, 128], P('groups'), parts along dimension 0
- down_grad: float32 [6, 4, 4, 128], P('groups'), parts along dimension 0
- up_grad: float32 [8, 4, 6, 128], P('groups'), parts along dimension 0
There are 2 independent parts, one for each index of `groups`. A program takes and returns all parts, laid end to end along the dimension named above; an argument that names none is the same for every part. Nothing has to cross between parts.
Inputs may be any that keep to these rules, and one draw needn't show every extreme that they name: `sample_ids`: every sample is named by exactly one of the 16 slots.
All inputs are finite; a program needn't handle non-finite values. No bound on the sum of `geometry` on one device may be relied on, other than what follows from the above.
Results may differ from a plain program's by a relative error of at most 0.0064.
Values may be sent and summed in bfloat16 or wider, within the bound.
No kernel may reach another device: no remote copies, remote signals or barrier semaphores. Data moves between devices by JAX's collectives and lax.ppermute only.
A program may use at most 256 MiB of HBM per device.

v0:
```python
import math

import jax
import jax.numpy as jnp
from jax import lax
from jax.sharding import PartitionSpec as P

CIN = 2
FIN = 3
CG = 64
FG = 512


tap_table = ((-1, 1), (0, 0), (0, 1), (1, 0))


def extended(value, sides, width):
    for axis, dim in sides:
        peers, length = (lax.axis_size(axis), value.shape[dim])
        up = [(i, (i + 1) % peers) for i in range(peers - 1)]
        down = [(j, i) for i, j in up]
        last = lax.slice_in_dim(value, length - width, length, axis=dim)
        initial = lax.slice_in_dim(value, 0, width, axis=dim)
        before = lax.ppermute(last, axis, up)
        after = lax.ppermute(initial, axis, down)
        value = jnp.concatenate([before, value, after], axis=dim)
    return value


def as_sent(value):
    return jax.tree.map(lambda a: a.astype(jnp.bfloat16) if a.dtype == jnp.float32 else a, value)


def prefix(value, axis, combine, identity, reverse):
    peers, position = (lax.axis_size(axis), lax.axis_index(axis))
    everything = lax.all_gather(value, axis)
    start = jnp.broadcast_to(jnp.asarray(identity, value.dtype), value.shape)

    def turn(k, before):
        at = peers - 1 - k if reverse else k
        reached = at > position if reverse else at < position
        new = combine(before, everything[at])
        return jnp.where(reached, new, before)

    return lax.fori_loop(0, peers, turn, start)


def gelu_slope(pre_act, upstream):
    unused, pull_back = jax.vjp(jax.nn.gelu, pre_act)
    return pull_back(upstream)[0]


def coarse_inputs(coarse_solution, geometry):
    samples = coarse_solution.shape[0]
    fields = coarse_solution.reshape(samples, CIN, CG, CG)
    metal = geometry.reshape(samples, 1, CG, CG).astype(jnp.bfloat16)
    return jnp.concatenate([fields, metal], axis=1)


def first_conv(inputs, first_weight):
    samples, channels = (inputs.shape[0], inputs.shape[1])
    padded = jnp.pad(inputs, ((0, 0), (0, 0), (2, 2), (2, 2)))
    pieces = [
        padded[:, :, 2 * row_tap : 2 * row_tap + CG, 2 * col_tap : 2 * col_tap + CG]
        for row_tap in range(3)
        for col_tap in range(3)
    ]
    patches = jnp.swapaxes(jnp.stack(pieces, 0), 1, 2).reshape(9 * channels, samples, CG * CG)
    weight_mat = jnp.transpose(first_weight, (1, 2, 0, 3)).reshape(
        9 * channels, first_weight.shape[3]
    )
    first_pre = lax.dot_general(
        patches, weight_mat, (((0,), (0,)), ((), ())), preferred_element_type=jnp.float32
    )
    return (first_pre.reshape(samples, CG, CG, first_weight.shape[3]), patches)


def first_back(patches, d_first, first_weight):
    samples = d_first.shape[0]
    flat = d_first.reshape(samples, CG * CG, d_first.shape[3])
    matrix = lax.dot_general(
        patches, flat, (((1, 2), (0, 1)), ((), ())), preferred_element_type=jnp.float32
    )
    return jnp.transpose(
        matrix.reshape(3, 3, first_weight.shape[0], first_weight.shape[3]), (2, 0, 1, 3)
    )


def second_conv(first_hidden, dilated_weight):
    padded = jnp.pad(first_hidden, ((0, 0), (4, 4), (4, 4), (0, 0)))
    summed = jnp.zeros(first_hidden.shape[:3] + (dilated_weight.shape[3],), jnp.float32)
    for row_tap in range(3):
        for col_tap in range(3):
            window = padded[:, 4 * row_tap : 4 * row_tap + CG, 4 * col_tap : 4 * col_tap + CG, :]
            summed = summed + lax.dot_general(
                window,
                dilated_weight[row_tap, col_tap],
                (((3,), (0,)), ((), ())),
                preferred_element_type=jnp.float32,
            )
    return summed


def second_back(first_hidden, d_second, dilated_weight):
    padded = jnp.pad(first_hidden, ((0, 0), (4, 4), (4, 4), (0, 0)))
    d_padded = jnp.zeros(padded.shape, jnp.float32)
    gradients = []
    for row_tap in range(3):
        for col_tap in range(3):
            window = padded[:, 4 * row_tap : 4 * row_tap + CG, 4 * col_tap : 4 * col_tap + CG, :]
            gradients.append(
                lax.dot_general(
                    window,
                    d_second,
                    (((0, 1, 2), (0, 1, 2)), ((), ())),
                    preferred_element_type=jnp.float32,
                )
            )
            back_term = lax.dot_general(
                d_second,
                dilated_weight[row_tap, col_tap],
                (((3,), (1,)), ((), ())),
                preferred_element_type=jnp.float32,
            )
            d_padded = d_padded.at[
                :, 4 * row_tap : 4 * row_tap + CG, 4 * col_tap : 4 * col_tap + CG, :
            ].add(back_term)
    dilated_grad = jnp.stack(gradients, 0).reshape(dilated_weight.shape)
    return (dilated_grad, d_padded[:, 4 : 4 + CG, 4 : 4 + CG, :])


def column_shift(array, shift):
    if shift == 0:
        return array
    width = array.shape[-1]
    edges = [(0, 0)] * (array.ndim - 1)
    if shift > 0:
        return jnp.pad(array[..., shift:], edges + [(0, shift)])
    return jnp.pad(array[..., : width + shift], edges + [(-shift, 0)])


def phase_patches(wide):
    rows = wide.shape[4] - 2
    pieces = []
    for row_tap in range(4):
        row_move, row_phase = tap_table[row_tap]
        for col_tap in range(4):
            col_move, col_phase = tap_table[col_tap]
            block = column_shift(
                wide[:, :, row_phase, col_phase, 1 + row_move : 1 + row_move + rows, :], col_move
            )
            for channel in range(wide.shape[1]):
                pieces.append(block[:, channel])
    return jnp.stack(pieces, 0)


def down_conv(wide, down_weight):
    patches = phase_patches(wide)
    weight_mat = jnp.transpose(down_weight, (1, 2, 0, 3)).reshape(
        patches.shape[0], down_weight.shape[3]
    )
    down_pre = lax.dot_general(
        patches, weight_mat, (((0,), (0,)), ((), ())), preferred_element_type=jnp.float32
    )
    return (down_pre, patches)


def down_layout(matrix, down_weight):
    shaped = matrix.reshape(4, 4, down_weight.shape[0], down_weight.shape[3])
    return jnp.transpose(shaped, (2, 0, 1, 3))


def add_coarse(down_pre, coarse_part):
    samples, fine_rows, fine_cols, channels = down_pre.shape
    coarse_rows, coarse_cols = (coarse_part.shape[1], coarse_part.shape[2])
    shaped = down_pre.reshape(
        samples,
        coarse_rows,
        fine_rows // coarse_rows,
        coarse_cols,
        fine_cols // coarse_cols,
        channels,
    )
    return (shaped + coarse_part[:, :, None, :, None, :]).reshape(down_pre.shape)


def pool_cells(grad_pre, coarse_rows, coarse_cols):
    samples, fine_rows, fine_cols, channels = grad_pre.shape
    shaped = grad_pre.reshape(
        samples,
        coarse_rows,
        fine_rows // coarse_rows,
        coarse_cols,
        fine_cols // coarse_cols,
        channels,
    )
    return jnp.sum(shaped, axis=(2, 4), dtype=jnp.float32)


def up_phase(hidden, up_weight):
    samples, rows_in, cols_in, channels = hidden.shape
    outputs = up_weight.shape[2]
    weight_mat = up_weight.reshape(16 * outputs, channels)
    taps = lax.dot_general(
        weight_mat, hidden, (((1,), (3,)), ((), ())), preferred_element_type=jnp.float32
    )
    taps = taps.reshape(4, 4, outputs, samples, rows_in, cols_in)
    row_groups = []
    for row_phase in range(2):
        col_groups = []
        for col_phase in range(2):
            summed = jnp.zeros((outputs, samples, rows_in + 2, cols_in), jnp.float32)
            for row_tap in range(4):
                row_move, tap_row_phase = tap_table[row_tap]
                for col_tap in range(4):
                    col_move, tap_col_phase = tap_table[col_tap]
                    if tap_row_phase == row_phase and tap_col_phase == col_phase:
                        piece = column_shift(taps[row_tap, col_tap], -col_move)
                        summed = summed + jnp.pad(
                            piece, ((0, 0), (0, 0), (1 + row_move, 1 - row_move), (0, 0))
                        )
            col_groups.append(summed)
        row_groups.append(jnp.stack(col_groups, 0))
    layout = jnp.stack(row_groups, 0)
    return jnp.transpose(layout, (3, 2, 0, 1, 4, 5))


def earlier_rows(flux):
    paired = flux[:, :, 0] + flux[:, :, 1]
    inclusive = jnp.cumsum(paired, axis=3)
    exclusive = inclusive - paired
    return (jnp.stack([exclusive + flux[:, :, 0], inclusive], axis=2), inclusive[:, :, :, -1])


def later_rows(upstream):
    paired = upstream[:, :, 0] + upstream[:, :, 1]
    inclusive = jnp.flip(jnp.cumsum(jnp.flip(paired, 3), axis=3), 3)
    exclusive = inclusive - paired
    return (jnp.stack([inclusive, exclusive + upstream[:, :, 1]], axis=2), inclusive[:, :, :, 0])


def add_pair(earlier, later):
    return earlier + later


def by_blocks(function, arrays):
    samples = arrays[0].shape[0]
    block_size = 8 if samples % 8 == 0 else samples
    grouped = tuple(
        (
            member.reshape((samples // block_size, block_size) + member.shape[1:])
            for member in arrays
        )
    )
    return lax.map(lambda portion: function(*portion), grouped)


def merge_blocks(stacked):
    return stacked.reshape((stacked.shape[0] * stacked.shape[1],) + stacked.shape[2:])


def local(
    coarse_solution,
    geometry,
    fine_fields,
    cotangent,
    sample_ids,
    first_weight,
    dilated_weight,
    project_weight,
    down_weight,
    up_weight,
):
    root_scale = 1.0 / math.sqrt(FG)
    inputs = coarse_inputs(coarse_solution, geometry)
    first_pre, first_patches = first_conv(inputs, first_weight)
    first_hidden = jax.nn.gelu(first_pre).astype(jnp.bfloat16)
    second_pre = second_conv(first_hidden, dilated_weight)
    feature = jax.nn.gelu(second_pre).astype(jnp.bfloat16)
    moved = lax.all_to_all(feature, "tile", split_axis=1, concat_axis=0, tiled=True)
    slot_feature = jnp.take(moved, sample_ids, axis=0)
    projected = lax.dot_general(
        slot_feature, project_weight, (((3,), (0,)), ((), ())), preferred_element_type=jnp.float32
    )
    fine_wide = extended(fine_fields, (("tile", 4),), 1)
    rows_here = fine_fields.shape[4]

    def forward_block(fine_part, coarse_part):
        down_pre, unused = down_conv(fine_part, down_weight)
        return jax.nn.gelu(add_coarse(down_pre, coarse_part)).astype(jnp.bfloat16)

    hidden = merge_blocks(by_blocks(forward_block, (fine_wide, projected)))
    hidden_wide = extended(as_sent(hidden), (("tile", 1),), 1).astype(hidden.dtype)

    def upward_wide(hidden_part):
        return up_phase(hidden_part, up_weight)[:, :, :, :, 2 : 2 + rows_here]

    out_field = merge_blocks(by_blocks(upward_wide, (hidden_wide,)))
    running, totals = earlier_rows(out_field[:, FIN:])
    before = prefix(totals, "tile", add_pair, jnp.zeros_like(totals), False)
    prediction = (
        out_field[:, :FIN] + (running + before[:, :, None, :, None, :]) * root_scale
    ).astype(jnp.bfloat16)
    upstream = cotangent.astype(jnp.float32)
    behind, leading = later_rows(upstream)
    later_sum = prefix(leading, "tile", add_pair, jnp.zeros_like(leading), True)
    slope_rows = jnp.concatenate(
        [upstream, (behind + later_sum[:, :, None, :, None, :]) * root_scale], axis=1
    ).astype(jnp.bfloat16)
    slope_wide = extended(slope_rows, (("tile", 4),), 1)
    up_mat = up_weight.reshape(16 * up_weight.shape[2], up_weight.shape[3])

    def backward_block(fine_part, coarse_part, hidden_part, slope_part):
        down_pre, patches = down_conv(fine_part, down_weight)
        third_pre = add_coarse(down_pre, coarse_part)
        slope_patches = phase_patches(slope_part)
        d_hidden = lax.dot_general(
            slope_patches, up_mat, (((0,), (0,)), ((), ())), preferred_element_type=jnp.float32
        )
        up_part = lax.dot_general(
            slope_patches,
            hidden_part,
            (((1, 2, 3), (0, 1, 2)), ((), ())),
            preferred_element_type=jnp.float32,
        )
        d_third = gelu_slope(third_pre, d_hidden).astype(jnp.bfloat16)
        down_part = lax.dot_general(
            patches, d_third, (((1, 2, 3), (0, 1, 2)), ((), ())), preferred_element_type=jnp.float32
        )
        pooled = pool_cells(d_third, coarse_part.shape[1], coarse_part.shape[2]).astype(
            jnp.bfloat16
        )
        return (pooled, up_part, down_part)

    pooled_parts, up_parts, down_parts = by_blocks(
        backward_block, (fine_wide, projected, hidden, slope_wide)
    )
    d_project = merge_blocks(pooled_parts)
    up_grad = jnp.sum(up_parts, axis=0).reshape(up_weight.shape)
    down_grad = down_layout(jnp.sum(down_parts, axis=0), down_weight)
    project_grad = lax.dot_general(
        slot_feature,
        d_project,
        (((0, 1, 2), (0, 1, 2)), ((), ())),
        preferred_element_type=jnp.float32,
    )
    d_slot = lax.dot_general(
        d_project, project_weight, (((3,), (1,)), ((), ())), preferred_element_type=jnp.float32
    ).astype(jnp.bfloat16)
    positions = jnp.arange(sample_ids.shape[0], dtype=jnp.int32)
    inverse = jnp.zeros_like(sample_ids).at[sample_ids].set(positions)
    d_sample = jnp.take(d_slot, inverse, axis=0)
    d_feature = lax.all_to_all(d_sample, "tile", split_axis=0, concat_axis=1, tiled=True)
    d_second = gelu_slope(second_pre, d_feature.astype(jnp.float32)).astype(jnp.bfloat16)
    dilated_grad, d_first_hidden = second_back(first_hidden, d_second, dilated_weight)
    d_first = gelu_slope(first_pre, d_first_hidden).astype(jnp.bfloat16)
    first_grad = first_back(first_patches, d_first, first_weight)
    first_grad, dilated_grad, project_grad, down_grad, up_grad = lax.psum(
        (first_grad, dilated_grad, project_grad, down_grad, up_grad), "tile"
    )
    return (prediction, first_grad, dilated_grad, project_grad, down_grad, up_grad)


def solution(mesh):
    in_specs = (
        P(("groups", "tile"), None, None),
        P(("groups", "tile"), None),
        P("groups", None, None, None, "tile", None),
        P("groups", None, None, None, "tile", None),
        P("groups"),
        P(),
        P(),
        P(),
        P(),
        P(),
    )
    out_specs = (
        P("groups", None, None, None, "tile", None),
        P("groups", None, None, None),
        P("groups", None, None, None),
        P("groups", None),
        P("groups", None, None, None),
        P("groups", None, None, None),
    )
    return jax.shard_map(local, mesh=mesh, in_specs=in_specs, out_specs=out_specs, check_vma=False)
```

profile of v0, /device:TPU:0, one launch (start us, length us, event | category | flops | bytes accessed | tf_op | source)
XLA Modules:
  0.0 1162.4 jit_solution(6077645174202747988)
XLA Ops:
  62.4 118.4 %while.81 = (s32[]{:T(128)}, bf16[2,8,16,256,128]{4,3,2,1,0:T(8,128)(2,1)}, bf16[2,8,3,2,2,18,256]{6,1,0,5,4,3,2:T(8,128)(2,1)S(1)}, bf16[3,4,4,128]{3,0,2,1:T(4...) while((s32[]{:T(128)}, bf16[2,8,16,256,128]{4,3,2,1,0:T(8,128)(2,1)}, ...), condition=%wide.region_1.3_spmd, body=%wide.region_0.2_spmd.sunk | while | flops 444596224 | bytes 135754880 | solution.py:255
  75.6 9.7 convolution_add_fusion.4
  85.3 20.6 %copy.6656 = f32[8,4,4,64,4,128]{5,0,4,3,2,1:T(8,128)S(1)} copy(f32[8,4,4,64,4,128]{5,3,4,2,1,0:T(8,128)S(1)} %convolution_add_fusion.4) | data formatting | bytes 33554432 | tf_op jit(solution)/shard_map/while/body/eval_jaxpr/add | solution.py:184
  134.6 9.6 convolution_add_fusion.4
  144.2 20.6 %copy.6656 = f32[8,4,4,64,4,128]{5,0,4,3,2,1:T(8,128)S(1)} copy(f32[8,4,4,64,4,128]{5,3,4,2,1,0:T(8,128)S(1)} %convolution_add_fusion.4) | data formatting | bytes 33554432 | tf_op jit(solution)/shard_map/while/body/eval_jaxpr/add | solution.py:184
  191.1 39.7 %while.84 = (s32[]{:T(128)}, f32[16,3,2,256]{3,2,1,0:T(2,128)}, s32[]{:T(128)}, f32[16,16,3,2,256]{4,1,0,3,2:T(8,128)}, s32[]{:T(128)}, /*index=5*/s32[]{:T(128)}, s32[]{:T(128)}, s32[]{:T(128)}) while((s32[]{:T(128)}, f32[16,3,2,256]{3,2,1,0:T(2,128)}, s32[]{:T(128)}, f32[16,16,3,2,256]{4,1,0,3,2:T(8,128)}, s32[]{:T(128)}, ...), condition=%wide.region_9.11_spmd.clone, body=%wide.region_8.10_spmd.clone.sunk | while | flops 73736 | bytes 491675 | solution.py:45
  238.3 15.2 %pad_maximum_fusion = bf16[2,8,18,256,128]{4,3,2,1,0:T(8,128)(2,1)} fusion(bf16[2,8,1,256,128]{4,3,2,1,0:T(8,128)(2,1)} %bitcast.320, bf16[2,8,16,256,128]{4,3,2,1,0:T(8,128)(2,1)} %get-tuple-element.2699, bf16[2,8,1,256,128]{4,3,2,1,0:T(8,128)(2,1)} %bitcast.318), kind=kLoop, calls=%fused_computation.448 | loop fusion | flops 18874368 | bytes 37748736 | tf_op jit(solution)/shard_map/concatenate | solution.py:26
  255.6 488.6 %while.82 = (s32[]{:T(128)}, bf16[2,8,4,64,128]{4,3,2,1,0:T(8,128)(2,1)}, f32[2,96,128]{2,1,0:T(8,128)}, f32[2,48,128]{2,1,0:T(8,128)}, bf16[2,8,6,2,2,18,256]{6...) while((s32[]{:T(128)}, ...), condition=%wide.region_12.14_spmd, body=%wide.region_10.13_spmd.sunk | while | flops 2507931648 | bytes 269321600 | solution.py:255
  326.0 45.4 %stack.175 = bf16[96,8,16,256]{3,0,2,1:T(8,128)(2,1)} concatenate(bf16[1,8,16,256]{3,0,2,1:T(2,128)(2,1)} %copy.6710, bf16[1,8,16,256]{3,0,2,1:T(2,128)(2,1)} %copy.6711, bf16[1,8,16,256]{3,0,2,1:T(2,128)(2,1)} %copy.6712, bf16[1,8,16,256]{3,0,2,1:T(2,128)(2,1)} %copy.6713, bf16[1,8,16,256]{3,0,2,1:T(2,128)(2,1)} %copy.6714, bf16[1,8,16,256]{3,0,2,1:T(2,128)(2,1)} %copy.6715, ...), dimensions={0} | concatenate | bytes 12582912 | tf_op jit(solution)/shard_map/while/body/eval_jaxpr/stack | solution.py:154
  408.2 17.8 %stack.174 = bf16[48,8,16,256]{3,0,2,1:T(8,128)(2,1)S(1)} concatenate(bf16[1,8,16,256]{3,0,2,1:T(2,128)(2,1)} %copy.6659, bf16[1,8,16,256]{3,0,2,1:T(2,128)(2,1)} %copy.6660, bf16[1,8,16,256]{3,0,2,1:T(2,128)(2,1)} %copy.6661, bf16[1,8,16,256]{3,0,2,1:T(2,128)(2,1)} %copy.6662, bf16[1,8,16,256]{3,0,2,1:T(2,128)(2,1)} %copy.6663, bf16[1,8,16,256]{3,0,2,1:T(2,128)(2,1)} %copy.6664, ...), dimensions={0} | concatenate | bytes 6291456 | tf_op jit(solution)/shard_map/while/body/eval_jaxpr/stack | solution.py:154
  434.9 10.0 convolution_add_fusion.5
  444.8 12.0 %copy.6708 = f32[8,4,4,64,4,128]{5,4,3,2,1,0:T(4,128)} copy(f32[8,4,4,64,4,128]{5,3,4,2,1,0:T(8,128)S(1)} %convolution_add_fusion.5) | data formatting | bytes 33554432 | tf_op jit(solution)/shard_map/while/body/eval_jaxpr/add | solution.py:184
  456.8 16.6 %fusion.387 = bf16[8,16,256,128]{3,2,1,0:T(8,128)(2,1)S(1)} fusion(f32[8,16,256,128]{3,2,1,0:T(8,128)} %bitcast.1225, bf16[96,8,16,256]{3,0,2,1:T(8,128)(2,1)} %stack.175, bf16[96,128]{1,0:T(8,128)(2,1)S(1)} %get-tuple-element.2719), kind=kOutput, calls=%fused_computation.191.clone.1 | convolution fusion | flops 889192448 | bytes 31481856 | tf_op jit(solution)/shard_map/while/body/eval_jaxpr/dot_general | solution.py:317
  564.7 45.2 %stack.175 = bf16[96,8,16,256]{3,0,2,1:T(8,128)(2,1)} concatenate(bf16[1,8,16,256]{3,0,2,1:T(2,128)(2,1)} %copy.6710, bf16[1,8,16,256]{3,0,2,1:T(2,128)(2,1)} %copy.6711, bf16[1,8,16,256]{3,0,2,1:T(2,128)(2,1)} %copy.6712, bf16[1,8,16,256]{3,0,2,1:T(2,128)(2,1)} %copy.6713, bf16[1,8,16,256]{3,0,2,1:T(2,128)(2,1)} %copy.6714, bf16[1,8,16,256]{3,0,2,1:T(2,128)(2,1)} %copy.6715, ...), dimensions={0} | concatenate | bytes 12582912 | tf_op jit(solution)/shard_map/while/body/eval_jaxpr/stack | solution.py:154
  646.7 17.8 %stack.174 = bf16[48,8,16,256]{3,0,2,1:T(8,128)(2,1)S(1)} concatenate(bf16[1,8,16,256]{3,0,2,1:T(2,128)(2,1)} %copy.6659, bf16[1,8,16,256]{3,0,2,1:T(2,128)(2,1)} %copy.6660, bf16[1,8,16,256]{3,0,2,1:T(2,128)(2,1)} %copy.6661, bf16[1,8,16,256]{3,0,2,1:T(2,128)(2,1)} %copy.6662, bf16[1,8,16,256]{3,0,2,1:T(2,128)(2,1)} %copy.6663, bf16[1,8,16,256]{3,0,2,1:T(2,128)(2,1)} %copy.6664, ...), dimensions={0} | concatenate | bytes 6291456 | tf_op jit(solution)/shard_map/while/body/eval_jaxpr/stack | solution.py:154
  673.4 10.2 convolution_add_fusion.5
  683.6 12.0 %copy.6708 = f32[8,4,4,64,4,128]{5,4,3,2,1,0:T(4,128)} copy(f32[8,4,4,64,4,128]{5,3,4,2,1,0:T(8,128)S(1)} %convolution_add_fusion.5) | data formatting | bytes 33554432 | tf_op jit(solution)/shard_map/while/body/eval_jaxpr/add | solution.py:184
  695.6 16.6 %fusion.387 = bf16[8,16,256,128]{3,2,1,0:T(8,128)(2,1)S(1)} fusion(f32[8,16,256,128]{3,2,1,0:T(8,128)} %bitcast.1225, bf16[96,8,16,256]{3,0,2,1:T(8,128)(2,1)} %stack.175, bf16[96,128]{1,0:T(8,128)(2,1)S(1)} %get-tuple-element.2719), kind=kOutput, calls=%fused_computation.191.clone.1 | convolution fusion | flops 889192448 | bytes 31481856 | tf_op jit(solution)/shard_map/while/body/eval_jaxpr/dot_general | solution.py:317
  748.1 9.9 all-to-all-start.1
  758.0 100.9 %while.85 = (s32[]{:T(128)}, f32[2,8,6,2,2,16,256]{6,1,0,4,2,5,3:T(8,128)}, bf16[2,8,18,256,128]{4,3,2,1,0:T(8,128)(2,1)}, bf16[4,4,6,128]{3,2,1,0:T(8,128)(2,1)...) while((s32[]{:T(128)}, f32[2,8,6,2,2,16,256]{6,1,0,4,2,5,3:T(8,128)}, ...), condition=%wide.wide.region_3.5_spmd, body=%wide.wide.region_2.4_spmd.sunk | while | flops 910884864 | bytes 159223136 | solution.py:255
  758.0 11.8 %fusion.392 = f32[96,8,18,256]{3,0,2,1:T(8,128)} fusion(bf16[2,8,18,256,128]{4,3,2,1,0:T(8,128)(2,1)} %get-tuple-element.2644, s32[]{:T(128)} %get-tuple-element.2636, bf16[96,128,1,1]{1,0,2,3:T(8,128)(2,1)S(1)} %get-tuple-element.2646), kind=kOutput, calls=%fused_computation.143.clone.clone.1 | convolution fusion | flops 905969664 | bytes 23618048 | tf_op jit(solution)/shard_map/while/body/eval_jaxpr/dot_general | solution.py:204
  769.9 18.2 %copy.6809 = f32[96,8,18,256]{3,1,2,0:T(8,128)} copy(f32[96,8,18,256]{3,0,2,1:T(8,128)} %fusion.392) | data formatting | bytes 28311552 | tf_op jit(solution)/shard_map/while/body/eval_jaxpr/dot_general | solution.py:204
  808.4 11.8 %fusion.392 = f32[96,8,18,256]{3,0,2,1:T(8,128)} fusion(bf16[2,8,18,256,128]{4,3,2,1,0:T(8,128)(2,1)} %get-tuple-element.2644, s32[]{:T(128)} %get-tuple-element.2636, bf16[96,128,1,1]{1,0,2,3:T(8,128)(2,1)S(1)} %get-tuple-element.2646), kind=kOutput, calls=%fused_computation.143.clone.clone.1 | convolution fusion | flops 905969664 | bytes 23618048 | tf_op jit(solution)/shard_map/while/body/eval_jaxpr/dot_general | solution.py:204
  820.2 18.2 %copy.6809 = f32[96,8,18,256]{3,1,2,0:T(8,128)} copy(f32[96,8,18,256]{3,0,2,1:T(8,128)} %fusion.392) | data formatting | bytes 28311552 | tf_op jit(solution)/shard_map/while/body/eval_jaxpr/dot_general | solution.py:204
  868.1 11.0 scatter-add.31
  883.7 10.9 scatter-add.34
  898.2 9.8 scatter-add.36
  912.0 9.8 scatter-add.41
  941.4 73.0 %all-reduce.56.cloned.1.call-done = (f32[3,3,3,128]{3,0,2,1:T(4,128)}, f32[3,4,4,128]{3,0,2,1:T(4,128)}, f32[4,4,6,128]{3,2,1,0:T(8,128)}) async-done(((f32[3,3,3,128]{3,0,2,1:T(4,128)}, f32[3,4,4,128]{3,0,2,1:T(4,128)}, f32[4,4,6,128]{3,2,1,0:T(8,128)}), (f32[3,3,3,128]{3,0,2,1:T(4,128)}, f32[3,4,4,128]{3,0,2,1:T(4,128)}, f32[4,4,6,128]{3,2,1,0:T(8,128)})) %all-reduce.56.cloned.1.call-update) | async-done | bytes 87568 | tf_op jit(solution)/shard_map/psum | solution.py:358
  1018.6 39.6 %all-gather.5.cloned.1.call-done = f32[256,3,2,1,256]{4,0,2,1,3:T(8,128)} async-done(((f32[16,3,2,1,256]{4,0,2,1,3:T(8,128)}), f32[256,3,2,1,256]{4,0,2,1,3:T(8,128)}) %all-gather.5.cloned.1.call-update) | async-done | bytes 1572880 | tf_op jit(solution)/shard_map/all_gather | solution.py:36
  1058.2 16.6 %while.83 = (s32[]{:T(128)}, f32[16,3,2,256]{3,2,1,0:T(2,128)S(1)}, s32[]{:T(128)}, f32[16,16,3,2,256]{4,1,0,3,2:T(8,128)}, s32[]{:T(128)}, /*index=5*/s32[]{:T(128)}) while((s32[]{:T(128)}, f32[16,3,2,256]{3,2,1,0:T(2,128)S(1)}, s32[]{:T(128)}, f32[16,16,3,2,256]{4,1,0,3,2:T(8,128)}, s32[]{:T(128)}, /*index=5*/s32[]{:T(128)}) %tuple.677), condition=%wide.region_6.8_spmd.clone, body=%wide.region_5.7_spmd.clone.sunk | while | flops 73732 | bytes 491613 | solution.py:45
  1080.0 72.0 %all-reduce.58.cloned.1.call-done = (f32[3,3,128,128]{3,2,1,0:T(8,128)}, f32[128,128]{1,0:T(8,128)}) async-done(((f32[3,3,128,128]{3,2,1,0:T(8,128)}, f32[128,128]{1,0:T(8,128)}), (f32[3,3,128,128]{3,2,1,0:T(8,128)}, f32[128,128]{1,0:T(8,128)})) %all-reduce.58.cloned.1.call-update) | async-done | bytes 655376 | tf_op jit(solution)/shard_map/psum | solution.py:358
  (888 shorter events, 557.0 us)
Async XLA Ops:
  7.2 53.3 %copy-start = (bf16[128,128]{1,0:T(8,128)(2,1)S(1)}, bf16[128,128]{1,0:T(8,128)(2,1)}, u32[]{:S(2)}) copy-start(bf16[128,128]{1,0:T(8,128)(2,1)} %param.47) | copy-start | bytes 98308
  18.3 9.3 copy-start.38
  20.0 13.1 %copy-start.23 = (bf16[16,3,2,2,16,256]{5,4,3,2,1,0:T(8,128)(2,1)S(1)}, bf16[16,3,2,2,16,256]{5,4,3,2,1,0:T(8,128)(2,1)}, u32[]{:S(2)}) copy-start(bf16[16,3,2,2,16,256]{5,4,3,2,1,0:T(8,128)(2,1)} %param.43) | copy-start | bytes 4718596
  20.0 38.5 %all-to-all-start = ((bf16[1,64,64,128]{3,2,0,1:T(8,128)(2,1)}), bf16[1,64,64,128]{3,2,0,1:T(8,128)(2,1)}, u32[]{:S(2)}, u32[]{:S(2)}) async-start(bf16[1,64,64,128]{3,2,0,1:T(8,128)(2,1)} %fusion.193), calls=%async_computation | async-start | bytes 2097152 | tf_op jit(solution)/shard_map/all_to_all | solution.py:280
  27.6 163.5 %all-gather.7.cloned.1.call-start = ((), (), s32[]{:S(2)}) async-start(), calls=%async_computation.3 | async-start | bytes 1671168 | tf_op jit(solution)/shard_map/all_gather | solution.py:36
  29.3 29.0 %collective-permute-start = (bf16[16,3,2,2,1,256]{5,0,4,3,2,1:T(8,128)(2,1)}, bf16[16,3,2,2,1,256]{5,0,4,3,2,1:T(8,128)(2,1)S(1)}, u32[]{:S(2)}, u32[]{:S(2)}) collective-permute-start(bf16[16,3,2,2,1,256]{5,0,4,3,2,1:T(8,128)(2,1)} %get-tuple-element.2003), channel_id=1, source_target_pairs={{0,1},{1,2},{2,3},{3,4},{4,5},{5,6},{6,7},{7,8},{8,9},{9,10},{10,1... | collective-permute-start | bytes 294920 | tf_op jit(solution)/shard_map/ppermute | solution.py:24
  31.6 26.7 %collective-permute-start.1 = (bf16[16,3,2,2,1,256]{5,0,4,3,2,1:T(8,128)(2,1)S(1)}, bf16[16,3,2,2,1,256]{5,0,4,3,2,1:T(8,128)(2,1)S(1)}, u32[]{:S(2)}, u32[]{:S(2)}) collective-permute-start(bf16[16,3,2,2,1,256]{5,0,4,3,2,1:T(8,128)(2,1)S(1)} %get-tuple-element.2004), channel_id=1, source_target_pairs={{1,0},{2,1},{3,2},{4,3},{5,4},{6,5},{7,6},{8,7},{9,8},{10,9},{11,1... | collective-permute-start | bytes 294920 | tf_op jit(solution)/shard_map/ppermute | solution.py:25
  40.2 10.7 copy-start.59
  47.8 9.8 copy-start.47
  181.4 50.4 %copy-start.32 = (f32[16,3,1,2,16,256]{5,0,3,1,4,2:T(8,128)S(1)}, f32[16,3,1,2,16,256]{5,0,3,1,4,2:T(8,128)}, u32[]{:S(2)}) copy-start(f32[16,3,1,2,16,256]{5,0,3,1,4,2:T(8,128)} %get-tuple-element.1999) | copy-start | bytes 4718596
  184.6 53.7 %collective-permute-start.2 = (bf16[16,1,256,128]{3,2,1,0:T(8,128)(2,1)}, bf16[16,1,256,128]{3,2,1,0:T(8,128)(2,1)}, u32[]{:S(2)}, u32[]{:S(2)}) collective-permute-start(bf16[16,1,256,128]{3,2,1,0:T(8,128)(2,1)} %get-tuple-element.1995), channel_id=1, source_target_pairs={{0,1},{1,2},{2,3},{3,4},{4,5},{5,6},{6,7},{7,8},{8,9},{9,10},{10,1... | collective-permute-start | bytes 3145736 | tf_op jit(solution)/shard_map/ppermute | solution.py:24
  189.8 48.5 %collective-permute-start.3 = (bf16[16,1,256,128]{3,2,1,0:T(8,128)(2,1)}, bf16[16,1,256,128]{3,2,1,0:T(8,128)(2,1)}, u32[]{:S(2)}, u32[]{:S(2)}) collective-permute-start(bf16[16,1,256,128]{3,2,1,0:T(8,128)(2,1)} %get-tuple-element.1996), channel_id=1, source_target_pairs={{1,0},{2,1},{3,2},{4,3},{5,4},{6,5},{7,6},{8,7},{9,8},{10,9},{11,1... | collective-permute-start | bytes 3145736 | tf_op jit(solution)/shard_map/ppermute | solution.py:25
  233.7 19.8 %collective-permute-start.4 = (bf16[16,6,2,2,1,256]{5,0,3,1,4,2:T(8,128)(2,1)S(1)}, bf16[16,6,2,2,1,256]{5,0,3,1,4,2:T(8,128)(2,1)S(1)}, u32[]{:S(2)}, u32[]{:S(2)}) collective-permute-start(bf16[16,6,2,2,1,256]{5,0,3,1,4,2:T(8,128)(2,1)S(1)} %get-tuple-element.1997), channel_id=1, source_target_pairs={{0,1},{1,2},{2,3},{3,4},{4,5},{5,6},{6,7},{7,8},{8,9},{9,10},{10,1... | collective-permute-start | bytes 589832 | tf_op jit(solution)/shard_map/ppermute | solution.py:24
  237.0 16.5 %collective-permute-start.5 = (bf16[16,6,2,2,1,256]{5,0,3,1,4,2:T(8,128)(2,1)S(1)}, bf16[16,6,2,2,1,256]{5,0,3,1,4,2:T(8,128)(2,1)S(1)}, u32[]{:S(2)}, u32[]{:S(2)}) collective-permute-start(bf16[16,6,2,2,1,256]{5,0,3,1,4,2:T(8,128)(2,1)S(1)} %get-tuple-element.1998), channel_id=1, source_target_pairs={{1,0},{2,1},{3,2},{4,3},{5,4},{6,5},{7,6},{8,7},{9,8},{10,9},{11,1... | collective-permute-start | bytes 589832 | tf_op jit(solution)/shard_map/ppermute | solution.py:25
  255.8 115.6 %copy-start.19 = (bf16[2,8,3,2,2,18,256]{6,1,0,5,4,3,2:T(8,128)(2,1)}, bf16[2,8,3,2,2,18,256]{6,1,0,5,4,3,2:T(8,128)(2,1)S(1)}, u32[]{:S(2)}) copy-start(bf16[2,8,3,2,2,18,256]{6,1,0,5,4,3,2:T(8,128)(2,1)S(1)} %get-tuple-element.2720) | copy-start | bytes 5308420 | tf_op jit(solution)/shard_map/while
  456.8 16.7 %copy-start.52 = (f32[2,48,128]{2,1,0:T(8,128)S(1)}, f32[2,48,128]{2,1,0:T(8,128)}, u32[]{:S(2)}) copy-start(f32[2,48,128]{2,1,0:T(8,128)} %get-tuple-element.2705) | copy-start | bytes 147460 | tf_op jit(solution)/shard_map/while
  476.6 9.1 copy-start.53
  476.7 9.1 copy-start.43
  476.7 9.2 copy-start.49
  494.5 115.4 %copy-start.19 = (bf16[2,8,3,2,2,18,256]{6,1,0,5,4,3,2:T(8,128)(2,1)}, bf16[2,8,3,2,2,18,256]{6,1,0,5,4,3,2:T(8,128)(2,1)S(1)}, u32[]{:S(2)}) copy-start(bf16[2,8,3,2,2,18,256]{6,1,0,5,4,3,2:T(8,128)(2,1)S(1)} %get-tuple-element.2720) | copy-start | bytes 5308420 | tf_op jit(solution)/shard_map/while
  695.6 16.6 %copy-start.52 = (f32[2,48,128]{2,1,0:T(8,128)S(1)}, f32[2,48,128]{2,1,0:T(8,128)}, u32[]{:S(2)}) copy-start(f32[2,48,128]{2,1,0:T(8,128)} %get-tuple-element.2705) | copy-start | bytes 147460 | tf_op jit(solution)/shard_map/while
  715.4 9.1 copy-start.53
  715.4 9.1 copy-start.43
  715.4 9.2 copy-start.49
  745.9 12.1 %copy-start.45 = (bf16[96,128,1,1]{1,0,2,3:T(8,128)(2,1)S(1)}, bf16[96,128,1,1]{1,0,2,3:T(8,128)(2,1)}, u32[]{:S(2)}) copy-start(bf16[96,128,1,1]{1,0,2,3:T(8,128)(2,1)} %reshape.956) | copy-start | bytes 73732
  748.1 112.2 %all-to-all-start.1 = ((bf16[16,4,64,128]{3,2,1,0:T(8,128)(2,1)}), bf16[16,4,64,128]{3,2,1,0:T(8,128)(2,1)}, u32[]{:S(2)}, u32[]{:S(2)}) async-start(bf16[16,4,64,128]{3,2,1,0:T(8,128)(2,1)} %broadcast_select_fusion), calls=%async_computation.1 | async-start | bytes 2097152 | tf_op jit(solution)/shard_map/all_to_all | solution.py:353
  757.9 256.5 %all-reduce.56.cloned.1.call-start = ((), (), s32[]{:S(2)}) async-start(), calls=%async_computation.4 | async-start | bytes 233472 | tf_op jit(solution)/shard_map/psum | solution.py:358
  758.0 100.9 %copy-start.51 = (f32[2,96,128]{2,1,0:T(8,128)S(1)}, f32[2,96,128]{2,1,0:T(8,128)}, u32[]{:S(2)}) copy-start(f32[2,96,128]{2,1,0:T(8,128)} %get-tuple-element.584) | copy-start | bytes 294916
  758.0 101.6 %copy-start.54 = (f32[2,48,128]{2,1,0:T(8,128)S(1)}, f32[2,48,128]{2,1,0:T(8,128)}, u32[]{:S(2)}) copy-start(f32[2,48,128]{2,1,0:T(8,128)} %get-tuple-element.583) | copy-start | bytes 147460
  926.3 131.9 %all-gather.5.cloned.1.call-start = ((), (), s32[]{:S(2)}) async-start(), calls=%async_computation.2 | async-start | bytes 1671168 | tf_op jit(solution)/shard_map/all_gather | solution.py:36
  933.0 219.1 %all-reduce.58.cloned.1.call-start = ((), (), s32[]{:S(2)}) async-start(), calls=%async_computation.5 | async-start | bytes 1310720 | tf_op jit(solution)/shard_map/psum | solution.py:358
  941.3 133.5 %copy-start.30 = (f32[16,3,2,16,256]{4,0,2,1,3:T(8,128)S(1)}, f32[16,3,2,16,256]{4,0,2,1,3:T(8,128)}, u32[]{:S(2)}) copy-start(f32[16,3,2,16,256]{4,0,2,1,3:T(8,128)} %copy-done.29) | copy-start | bytes 4718596
  (63 other events, 210.6 us)
Sparse Core Ops, SparseCore 0:
  43.8 43.1 all-gather.6
  926.4 87.9 all-reduce.55
  1016.6 41.5 all-gather.4
  1062.1 89.9 all-reduce.57
where the time goes:
time: 1180 us; the launch traced here: 1160 us
  local copies, waits for them, and re-layouts  651 us (55%)
  waiting for transfers between devices  185 us (16%)
  matrix products  149 us (13%)
  other arithmetic  114 us (10%)
  starting transfers between devices  32.6 us (3%)
  loops' own time  15.2 us (1%)
  between operations  15.1 us (1%)
    squeeze x336, local copies, waits for them, and re-layouts, phase_patches(): return jnp.stack(pieces, 0)  201 us
    psum x2, waiting for transfers between devices, local(): lax.psum((first_grad, dilated_grad, project_grad, down_grad, up_grad), 't...  145 us
    another operation x6, local copies, waits for them, and re-layouts, phase_patches(): return jnp.stack(pieces, 0)  126 us
    add x8, local copies, waits for them, and re-layouts, add_coarse(): shaped + coarse_part[:, :, None, :, None, :]  72.4 us
    scatter-add x5, local copies, waits for them, and re-layouts, second_back(): d_padded = d_padded.at[:, 4 * row_tap:4 * row_tap + CG, 4 * col_tap:4 * c...  41.7 us
    all_gather x2, waiting for transfers between devices, prefix(): everything = lax.all_gather(value, axis)  39.6 us
    dot_general x4, matrix products, down_conv(): lax.dot_general(patches, weight_mat, (((0,), (0,)), ((), ())), preferred_...  39.4 us
    dot_general x2, local copies, waits for them, and re-layouts, up_phase(): lax.dot_general(weight_mat, hidden, (((1,), (3,)), ((), ())), preferred_e...  36.4 us
  transfers between devices with their start and end apart: 12, of which 3 were waited for; matrix products, arithmetic and copies ran while one was open for 29% of the time, Pallas kernels for 0%

commit v1 on v0

v1 whole, which is shorter than its diff:
```python
import math

import jax
import jax.numpy as jnp
import numpy as np
from jax import lax
from jax.experimental import pallas as pl
from jax.experimental.pallas import tpu as pltpu
from jax.sharding import PartitionSpec as P

CG = 64
FG = 512
HALF = FG // 2
SCALE = 1.0 / math.sqrt(FG)
GELU_A = math.sqrt(2.0 / math.pi)
GELU_B = GELU_A * 0.044715
BF = jnp.bfloat16
F32 = jnp.float32

AUX = 48
GRAD_ROWS = 1536
UP_AT, DOWN_AT, FIRST_AT, PROJECT_AT = 1280, 1376, 1424, 1152


def nn(a, b):
    return lax.dot_general(a, b, (((1,), (0,)), ((), ())), preferred_element_type=F32)


def nt(a, b):
    return lax.dot_general(a, b, (((1,), (1,)), ((), ())), preferred_element_type=F32)


def exact(a, b):
    return lax.dot_general(
        a, b, (((1,), (0,)), ((), ())), precision=lax.Precision.HIGHEST, preferred_element_type=F32
    )


def row_at(tap, r):
    if tap == 0:
        return 8 if r == 0 else 4 + r - 1
    if tap == 1:
        return r
    if tap == 2:
        return 4 + r
    return 9 if r == 3 else r + 1


def fine_row(block, index):
    if index == 8:
        return 8 * block - 1
    if index == 9:
        return 8 * block + 8
    return 8 * block + 2 * (index % 4) + index // 4


COL_GROUP = (2, 0, 1, 3)


def constants(rows):
    blocks = rows // 4
    last = 2 * rows
    width = 12 * rows + AUX

    def held(ch, q, o):
        return ((ch * 2 + o % 2) * 2 + q) * rows + o // 2

    sel_x = np.zeros((blocks, 2, 32, width), np.float32)
    sel_s = np.zeros((blocks, 2, 64, width), np.float32)
    sel_o = np.zeros((12 * rows + 32, blocks, 2, 64), np.float32)
    base = 12 * rows
    for b in range(blocks):
        for q in range(2):
            for ch in range(3):
                for index in range(10):
                    o = fine_row(b, index)
                    at = ch * 10 + index
                    if o == -1:
                        sel_x[b, q, at, base + ch * 2 + q] = 1
                        sel_s[b, q, at, base + 6 + ch * 2 + q] = 1
                        sel_s[b, q, 32 + at, base + 6 + ch * 2 + q] = 1
                    elif o == last:
                        sel_x[b, q, at, base + 16 + ch * 2 + q] = 1
                        sel_s[b, q, at, base + 22 + ch * 2 + q] = 1
                    else:
                        sel_x[b, q, at, held(ch, q, o)] = 1
                        sel_s[b, q, at, held(ch, q, o)] = 1
                    for later in range(max(o, 0), last):
                        sel_s[b, q, 32 + at, held(ch, q, later)] = 1
                    sel_s[b, q, 32 + at, base + 32 + ch * 2 + q] = 1
                    sel_s[b, q, 32 + at, base + 40 + ch * 2 + q] = 1
                    for target in range(max(o, 0), last):
                        if target == o:
                            sel_o[held(ch, q, target), b, q, at] = 1
                        if o >= 0:
                            sel_o[held(ch, q, target), b, q, 32 + at] = 1
                    if o == -1:
                        sel_o[base + ch * 2 + q, b, q, at] = 1
                        sel_o[base + 6 + ch * 2 + q, b, q, 32 + at] = 1
                    else:
                        sel_o[base + 18 + ch * 2 + q, b, q, 32 + at] = 1
                    if o == last:
                        sel_o[base + 12 + ch * 2 + q, b, q, at] = 1
    sel_s_first = sel_s.copy()
    for q in range(2):
        for ch in range(3):
            sel_s_first[0, q, 32 + ch * 10 + 8] = 0
    ex = np.zeros((4, 128, 48), np.float32)
    eu = np.zeros((4, 256, 96), np.float32)
    for r in range(4):
        for i in range(4):
            for j in range(4):
                for ch in range(3):
                    ex[r, COL_GROUP[j] * 32 + ch * 10 + row_at(i, r), (ch * 4 + i) * 4 + j] = 1
                for k in range(6):
                    at = COL_GROUP[j] * 64 + (k // 3) * 32 + (k % 3) * 10 + row_at(i, r)
                    eu[r, at, (i * 4 + j) * 6 + k] = 1
    ef = np.zeros((80, 32), np.float32)
    for ch in range(3):
        for tap in range(9):
            ef[tap * 8 + ch, ch * 9 + tap] = 1
    pool = np.zeros((CG, HALF), np.float32)
    for c in range(HALF):
        pool[c // 4, c] = 1
    spread = np.zeros((blocks, CG, blocks, HALF), np.float32)
    for a in range(blocks):
        spread[a, :, a, :] = pool
    return dict(
        sel_x=sel_x.reshape(blocks * 64, width),
        sel_s=sel_s.reshape(blocks * 128, width),
        sel_s_first=sel_s_first.reshape(blocks * 128, width),
        sel_o=sel_o.reshape(12 * rows + 32, blocks * 128),
        ex=ex.reshape(512, 48),
        eu=eu.reshape(1024, 96),
        ext=np.concatenate(list(np.swapaxes(ex, 1, 2)), 0),
        eut=np.concatenate(list(np.swapaxes(eu, 1, 2)), 0),
        ef=ef,
        eft=ef.T,
        pool=pool,
        spread=spread.reshape(blocks * CG, blocks * HALF),
    )


def gelu_both(pre):
    square = pre * pre
    t = jnp.tanh(pre * (GELU_B * square + GELU_A))
    gate = 0.5 + 0.5 * t
    value = pre * gate
    slope = gate + (value * (1.0 - gate)) * (6.0 * GELU_B * square + 2.0 * GELU_A)
    return value, slope


def moved(value, shift, lane, keep):
    width = value.shape[1]
    return jnp.where(keep(lane), pltpu.roll(value, shift % width, 1), 0.0)


def slot_kernel(
    blocks,
    ids_ref,
    tile_ref,
    coarse_ref,
    fine_ref,
    cot_ref,
    before_ref,
    after_ref,
    later_ref,
    sel_x_ref,
    sel_s_ref,
    sel_o_ref,
    ex_ref,
    eu_ref,
    ext_ref,
    eut_ref,
    ef_ref,
    eft_ref,
    pool_ref,
    spread_ref,
    first_t_ref,
    second_t_ref,
    second_ref,
    project_ref,
    project_t_ref,
    down_t_ref,
    up_t_ref,
    up_ref,
    pred_ref,
    edge_ref,
    out_ref,
    grad_ref,
    w_ref,
    u_ref,
    ut_ref,
    w1_ref,
    gu_ref,
    gd_ref,
    fg_ref,
):
    step = pl.program_id(0)
    cells = blocks * CG
    tile = tile_ref[0]

    @pl.when(step == 0)
    def _():
        for r in range(4):
            rows = slice(r * 128, (r + 1) * 128)
            w_ref[rows, 0:128] = nt(down_t_ref[...], ex_ref[rows, :]).astype(BF)
            w_ref[rows, 128:256] = project_t_ref[...]
            taps = eu_ref[r * 256 : (r + 1) * 256, :]
            u_ref[rows, :] = nt(up_t_ref[...], taps).astype(BF)
            ut_ref[:, rows] = nn(taps, up_ref[...]).astype(BF)
        w1_ref[...] = nt(first_t_ref[...], ef_ref[...]).astype(BF)
        gu_ref[...] = jnp.zeros_like(gu_ref)
        gd_ref[...] = jnp.zeros_like(gd_ref)
        fg_ref[...] = jnp.zeros_like(fg_ref)
        grad_ref[...] = jnp.zeros_like(grad_ref)

    inputs = jnp.concatenate([coarse_ref[0], jnp.zeros((5, coarse_ref.shape[2]), F32)], axis=0)
    lane_in = lax.broadcasted_iota(jnp.int32, inputs.shape, 1) % CG
    by_col = (
        moved(inputs, 2, lane_in, lambda x: x >= 2),
        inputs,
        moved(inputs, -2, lane_in, lambda x: x < CG - 2),
    )
    above = jnp.where(tile * blocks >= 4, 1.0, 0.0)
    below = jnp.where(tile * blocks + 4 <= CG - blocks, 1.0, 0.0)
    windows = []
    for window in range(3):
        pieces = []
        for row_tap in range(3):
            for col_tap in range(3):
                start = (4 * window + 2 * row_tap) * CG
                pieces.append(by_col[col_tap][:, start : start + cells])
        pieces.append(jnp.zeros((8, cells), F32))
        stacked = jnp.concatenate(pieces, axis=0)
        if window == 0:
            stacked = stacked * above
        if window == 2:
            stacked = stacked * below
        windows.append(stacked)
    patches = jnp.concatenate(windows, axis=1).astype(BF)
    first_value, first_slope = gelu_both(nn(w1_ref[...], patches))
    lane_h = lax.broadcasted_iota(jnp.int32, first_value.shape, 1) % CG
    first_value = first_value.astype(BF).astype(F32)
    hidden_by_col = (
        moved(first_value, 4, lane_h, lambda x: x >= 4).astype(BF),
        first_value.astype(BF),
        moved(first_value, -4, lane_h, lambda x: x < CG - 4).astype(BF),
    )
    columns = jnp.concatenate(
        [
            hidden_by_col[col_tap][:, window * cells : (window + 1) * cells]
            for window in range(3)
            for col_tap in range(3)
        ],
        axis=0,
    )
    second_value, second_slope = gelu_both(nn(second_t_ref[...], columns))
    feature = second_value.astype(BF)
    feature_wide = nn(feature, spread_ref[...]).astype(BF)

    later = later_ref[0]
    later_high = later.astype(BF).astype(F32)
    later_both = jnp.concatenate([later_high, later - later_high], axis=0).astype(BF)
    aux = [before_ref[0], after_ref[0], later_both]
    fine_all = nn(sel_x_ref[...], jnp.concatenate([fine_ref[0]] + aux, axis=0))
    slope_all = nn(sel_s_ref[...], jnp.concatenate([cot_ref[0]] + aux, axis=0))
    row = lax.broadcasted_iota(jnp.int32, (64, HALF), 0)
    flux_scale = jnp.where(row >= 32, SCALE, 1.0)
    lane32 = lax.broadcasted_iota(jnp.int32, (32, HALF), 1)
    lane64 = lax.broadcasted_iota(jnp.int32, (64, HALF), 1)
    not_first = lambda x: x >= 1
    not_last = lambda x: x < HALF - 1

    def enter(b):
        x0 = fine_all[b * 64 : b * 64 + 32]
        x1 = fine_all[b * 64 + 32 : b * 64 + 64]
        x_taps = jnp.concatenate(
            [x0, x1, moved(x1, 1, lane32, not_first), moved(x0, -1, lane32, not_last)], axis=0
        ).astype(BF)
        s0 = slope_all[b * 128 : b * 128 + 64] * flux_scale
        s1 = slope_all[b * 128 + 64 : b * 128 + 128] * flux_scale
        s_taps = jnp.concatenate(
            [s0, s1, moved(s1, 1, lane64, not_first), moved(s0, -1, lane64, not_last)], axis=0
        ).astype(BF)
        third = nn(
            w_ref[...],
            jnp.concatenate([x_taps, feature_wide[:, b * HALF : (b + 1) * HALF]], axis=0),
        )
        return x_taps, s_taps, third, nn(u_ref[...], s_taps)

    def middle(entered):
        x_taps, s_taps, third, d_hidden = entered
        value, slope = gelu_both(third)
        return x_taps, s_taps, value.astype(BF), (d_hidden * slope).astype(BF)

    def leave(held):
        x_taps, s_taps, hidden, d_third = held
        taps = nn(ut_ref[...], hidden)
        c0 = taps[0:64] + moved(taps[192:256], 1, lane64, not_first)
        c1 = taps[64:128] + moved(taps[128:192], -1, lane64, not_last)
        gu_ref[...] += nt(s_taps, hidden)
        both = nt(jnp.concatenate([x_taps, pool_ref[...]], axis=0), d_third)
        gd_ref[...] += both[0:128]
        per_row = both[128:192]
        cells_sum = (per_row[:, 0:128] + per_row[:, 128:256]) + (
            per_row[:, 256:384] + per_row[:, 384:512]
        )
        return [c0 * flux_scale, c1 * flux_scale], cells_sum

    combined = []
    pooled = []
    entered = {}
    held = {}
    for turn in range(blocks + 2):
        if turn < blocks:
            entered[turn] = enter(turn)
        if 0 <= turn - 1 < blocks:
            held[turn - 1] = middle(entered.pop(turn - 1))
        if turn - 2 >= 0:
            pair, cells_sum = leave(held.pop(turn - 2))
            combined += pair
            pooled.append(cells_sum)

    out = jnp.concatenate(combined, axis=0)
    out_high = out.astype(BF)
    out_low = (out - out_high.astype(F32)).astype(BF)
    placed = nn(sel_o_ref[...], out_high) + nn(sel_o_ref[...], out_low)
    main = pred_ref.shape[1]
    pred_ref[0] = placed[0:main]
    edge_ref[0] = placed[main : main + 32]

    d_project = jnp.concatenate(pooled, axis=0).astype(BF)
    grad_ref[PROJECT_AT : PROJECT_AT + 128, :] += nn(feature, d_project)
    d_feature = nt(project_ref[...], d_project).astype(BF).astype(F32)
    d_second = (d_feature * second_slope).astype(BF)
    grad_ref[0:1152, :] += nt(columns, d_second)
    back = nn(second_ref[...], d_second)
    lane_c = lax.broadcasted_iota(jnp.int32, (128, cells), 1) % CG
    parts = []
    for window in range(3):
        at = window * 384
        parts.append(
            back[at + 128 : at + 256]
            + moved(back[at : at + 128], -4, lane_c, lambda x: x < CG - 4)
            + moved(back[at + 256 : at + 384], 4, lane_c, lambda x: x >= 4)
        )
    d_first = (jnp.concatenate(parts, axis=1) * first_slope).astype(BF)
    fg_ref[...] += nt(patches, d_first)

    @pl.when(step == pl.num_programs(0) - 1)
    def _():
        up = jnp.zeros((96, 128), F32)
        down = jnp.zeros((48, 128), F32)
        for r in range(4):
            lanes = slice(r * 128, (r + 1) * 128)
            up = up + exact(eut_ref[r * 96 : (r + 1) * 96, :], gu_ref[:, lanes])
            down = down + exact(ext_ref[r * 48 : (r + 1) * 48, :], gd_ref[:, lanes])
        grad_ref[UP_AT : UP_AT + 96, :] = up
        grad_ref[DOWN_AT : DOWN_AT + 48, :] = down
        grad_ref[FIRST_AT : FIRST_AT + 32, :] = exact(eft_ref[...], fg_ref[...])
        out_ref[...] = grad_ref[...].astype(BF)


def run_slots(ids, tile, coarse, fine, cot, before, after, later, fixed, weights):
    slots, main, width = fine.shape
    blocks = main // 48

    def whole(array):
        return pl.BlockSpec(array.shape, lambda n, ids, tile: (0,) * array.ndim)

    def per_slot(array):
        return pl.BlockSpec((1,) + array.shape[1:], lambda n, ids, tile: (n, 0, 0))

    in_specs = [
        pl.BlockSpec((1,) + coarse.shape[1:], lambda n, ids, tile: (ids[n], 0, 0)),
        per_slot(fine),
        per_slot(cot),
        per_slot(before),
        per_slot(after),
        per_slot(later),
    ] + [whole(a) for a in fixed + weights]
    grid_spec = pltpu.PrefetchScalarGridSpec(
        num_scalar_prefetch=2,
        grid=(slots,),
        in_specs=in_specs,
        out_specs=[
            pl.BlockSpec((1, main, width), lambda n, ids, tile: (n, 0, 0)),
            pl.BlockSpec((1, 32, width), lambda n, ids, tile: (n, 0, 0)),
            pl.BlockSpec((GRAD_ROWS, 128), lambda n, ids, tile: (0, 0)),
        ],
        scratch_shapes=[
            pltpu.VMEM((GRAD_ROWS, 128), F32),
            pltpu.VMEM((512, 256), BF),
            pltpu.VMEM((512, 256), BF),
            pltpu.VMEM((256, 512), BF),
            pltpu.VMEM((128, 80), BF),
            pltpu.VMEM((256, 512), F32),
            pltpu.VMEM((128, 512), F32),
            pltpu.VMEM((80, 128), F32),
        ],
    )

    def body(*refs):
        slot_kernel(blocks, *refs)

    return pl.pallas_call(
        body,
        grid_spec=grid_spec,
        out_shape=[
            jax.ShapeDtypeStruct((slots, main, width), F32),
            jax.ShapeDtypeStruct((slots, 32, width), F32),
            jax.ShapeDtypeStruct((GRAD_ROWS, 128), BF),
        ],
        compiler_params=pltpu.CompilerParams(vmem_limit_bytes=52 * 1024 * 1024),
        cost_estimate=pl.CostEstimate(
            flops=slots * blocks * 500_000_000, bytes_accessed=16_000_000, transcendentals=0
        ),
    )(ids, tile, coarse, fine, cot, before, after, later, *fixed, *weights)


def exchanged(value):
    return lax.all_to_all(value, "tile", split_axis=0, concat_axis=0, tiled=True)


def local(
    coarse_solution,
    geometry,
    fine_fields,
    cotangent,
    sample_ids,
    first_weight,
    dilated_weight,
    project_weight,
    down_weight,
    up_weight,
):
    peers = lax.axis_size("tile")
    position = lax.axis_index("tile")
    slots, rows = fine_fields.shape[0], fine_fields.shape[4]
    blocks = rows // 4
    up = [(i, i + 1) for i in range(peers - 1)]
    down = [(i + 1, i) for i in range(peers - 1)]

    totals = jnp.sum(cotangent.astype(F32), axis=(2, 4)).reshape(slots, 6, HALF)
    totals = jnp.pad(totals, ((0, 0), (0, 2), (0, 0)))
    mine = coarse_solution.shape[0]
    inputs = jnp.concatenate([coarse_solution.astype(F32), geometry.astype(F32)[:, None]], axis=1)
    padded = jnp.pad(inputs, ((0, 0), (0, 0), (6 * CG, 6 * CG)))
    span = (blocks + 12) * CG
    windows = jnp.stack(
        [padded[:, :, t * blocks * CG : t * blocks * CG + span] for t in range(peers)], 0
    )
    sent = jnp.concatenate(
        [
            windows.reshape(peers, mine * 3 * span),
            totals.reshape(peers, (slots // peers) * 8 * HALF),
        ],
        axis=1,
    )
    got = exchanged(sent)
    coarse = got[:, : mine * 3 * span].reshape(peers * mine, 3, span)
    sums = got[:, mine * 3 * span :]
    order = lax.broadcasted_iota(jnp.int32, (peers, peers), 0)
    other = lax.broadcasted_iota(jnp.int32, (peers, peers), 1)
    behind = jnp.sum(jnp.where((other > order)[:, :, None], sums[None], 0.0), axis=1)
    later = exchanged(behind).reshape(slots, 8, HALF)

    blank = jnp.zeros((slots, 4, HALF), BF)
    edge_last = jnp.concatenate(
        [
            fine_fields[:, :, 1, :, -1].reshape(slots, 6, HALF),
            cotangent[:, :, 1, :, -1].reshape(slots, 6, HALF),
            blank,
        ],
        axis=1,
    )
    edge_first = jnp.concatenate(
        [
            fine_fields[:, :, 0, :, 0].reshape(slots, 6, HALF),
            cotangent[:, :, 0, :, 0].reshape(slots, 6, HALF),
            blank,
        ],
        axis=1,
    )
    from_before = lax.ppermute(edge_last, "tile", up)
    from_after = lax.ppermute(edge_first, "tile", down)

    made = constants(rows)
    sel_s = jnp.where(
        position == 0, jnp.asarray(made["sel_s_first"], BF), jnp.asarray(made["sel_s"], BF)
    )
    fixed = [
        jnp.asarray(made["sel_x"], BF),
        sel_s,
        jnp.asarray(made["sel_o"], BF),
        jnp.asarray(made["ex"], BF),
        jnp.asarray(made["eu"], BF),
        jnp.asarray(made["ext"], F32),
        jnp.asarray(made["eut"], F32),
        jnp.asarray(made["ef"], BF),
        jnp.asarray(made["eft"], F32),
        jnp.asarray(made["pool"], BF),
        jnp.asarray(made["spread"], BF),
    ]
    second = dilated_weight.reshape(1152, 128)
    up_flat = up_weight.reshape(96, 128)
    weights = [
        jnp.pad(first_weight.reshape(27, 128), ((0, 5), (0, 0))).T,
        second.T,
        second,
        project_weight,
        project_weight.T,
        down_weight.reshape(48, 128).T,
        up_flat.T,
        up_flat,
    ]
    pred_local, edges, grads = run_slots(
        sample_ids,
        position.reshape(1).astype(jnp.int32),
        coarse,
        fine_fields.reshape(slots, 12 * rows, HALF),
        cotangent.reshape(slots, 12 * rows, HALF),
        from_before,
        from_after,
        later,
        fixed,
        weights,
    )

    before_flux = jnp.where(position >= 1, edges[:, 6:12], 0.0)
    flux = edges[:, 18:24] + before_flux
    chunk = GRAD_ROWS // peers
    extra = (slots // peers) * 12

    def halves(value):
        high = lax.reduce_precision(value, 8, 7)
        return [high.astype(BF), (value - high).astype(BF)]

    sent = jnp.concatenate(
        [grads.reshape(peers, chunk, 128)] + halves(flux.reshape(peers, extra, 128)), axis=1
    )
    got = exchanged(sent).astype(F32)
    to_first = lax.ppermute(edges[:, 12:18], "tile", up)
    to_last = lax.ppermute(edges[:, 0:6] + edges[:, 6:12], "tile", down)
    reduced = jnp.sum(got[:, :chunk], axis=0).astype(BF)
    sums = got[:, chunk : chunk + extra] + got[:, chunk + extra :]
    ahead = jnp.sum(jnp.where((other < order)[:, :, None, None], sums[None], 0.0), axis=1)
    reduced, to_first, to_last = lax.optimization_barrier((reduced, to_first, to_last))
    back = exchanged(
        jnp.concatenate(
            [jnp.broadcast_to(reduced, (peers, chunk, 128))] + halves(ahead), axis=1
        )
    )
    total = back[:, :chunk].reshape(GRAD_ROWS, 128).astype(F32)
    ahead = back[:, chunk : chunk + extra].astype(F32) + back[:, chunk + extra :].astype(F32)
    base = ahead.reshape(slots, 6, HALF) + before_flux

    shape = (slots, 3, 2, 2, rows, HALF)
    half_row = lax.broadcasted_iota(jnp.int32, shape, 2)
    fine_row_at = lax.broadcasted_iota(jnp.int32, shape, 4)

    def over_rows(value):
        return value.reshape(slots, 3, 1, 2, 1, HALF)

    prediction = (
        pred_local.reshape(shape)
        + over_rows(base)
        + jnp.where((half_row == 0) & (fine_row_at == 0), over_rows(to_first), 0.0)
        + jnp.where((half_row == 1) & (fine_row_at == rows - 1), over_rows(to_last), 0.0)
    ).astype(BF)
    return (
        prediction,
        total[FIRST_AT : FIRST_AT + 27].reshape(first_weight.shape),
        total[0:1152].reshape(dilated_weight.shape),
        total[PROJECT_AT : PROJECT_AT + 128],
        total[DOWN_AT : DOWN_AT + 48].reshape(down_weight.shape),
        total[UP_AT : UP_AT + 96].reshape(up_weight.shape),
    )


def solution(mesh):
    in_specs = (
        P(("groups", "tile"), None, None),
        P(("groups", "tile"), None),
        P("groups", None, None, None, "tile", None),
        P("groups", None, None, None, "tile", None),
        P("groups"),
        P(),
        P(),
        P(),
        P(),
        P(),
    )
    out_specs = (
        P("groups", None, None, None, "tile", None),
        P("groups", None, None, None),
        P("groups", None, None, None),
        P("groups", None),
        P("groups", None, None, None),
        P("groups", None, None, None),
    )
    return jax.shard_map(local, mesh=mesh, in_specs=in_specs, out_specs=out_specs, check_vma=False)
```

time: 1180 us -> 159 us (0.13); the launches traced: 1160 us -> 158 us
  local copies, waits for them, and re-layouts: 651 us -> 12.9 us
  waiting for transfers between devices: 185 us -> 31 us
  matrix products: 149 us -> 0 us
  other arithmetic: 114 us -> 16 us
  Pallas kernels: 0 us -> 68.4 us
  loops' own time: 15.2 us -> 0 us
  between operations: 15.1 us -> 1.49 us
    squeeze x344 -> x0, local copies, waits for them, and re-layouts: 222 us -> none  [the longest x336 201 us: phase_patches(): return jnp.stack(pieces, 0)]
    dot_general x44 -> x0, matrix products: 149 us -> none  [the longest x4 39.4 us: down_conv(): lax.dot_general(patches, weight_mat, (((0,), (0,)), ((), ())), preferred_...]
    psum x2 -> x0, waiting for transfers between devices: 145 us -> none  [local(): lax.psum((first_grad, dilated_grad, project_grad, down_grad, up_grad), 't...]
    another operation x10 -> x5, local copies, waits for them, and re-layouts: 128 us -> 0.38 us  [the longest x1 0.3 us: local(): jnp.stack([padded[:, :, t * blocks * CG:t * blocks * CG + span] for t in...]
    add x8 -> x3, local copies, waits for them, and re-layouts: 72.4 us -> 0.15 us  [the longest x1 0.08 us: local(): pred_local.reshape(shape) + over_rows(base)]
    pallas_call x0 -> x1, Pallas kernels: none -> 68.4 us  [run_slots(): pl.pallas_call(body, grid_spec=grid_spec, out_shape=[jax.ShapeDtypeStruct...]
    dot_general x7 -> x0, local copies, waits for them, and re-layouts: 67.4 us -> none  [the longest x2 36.4 us: up_phase(): lax.dot_general(weight_mat, hidden, (((1,), (3,)), ((), ())), preferred_e...]
    scatter-add x5 -> x0, local copies, waits for them, and re-layouts: 41.7 us -> none  [second_back(): d_padded = d_padded.at[:, 4 * row_tap:4 * row_tap + CG, 4 * col_tap:4 * c...]
  transfers between devices with their start and end apart: 12 -> 8, of which waited for: 3 -> 4; matrix products, arithmetic and copies ran while one was open for 29% -> 5% of each run, Pallas kernels for 0% -> 0%
where the time goes in v1:
time: 159 us; the launch traced here: 158 us
  Pallas kernels  68.4 us (43%)
  waiting for transfers between devices  31 us (19%)
  starting transfers between devices  27.9 us (18%)
  other arithmetic  16 us (10%)
  local copies, waits for them, and re-layouts  12.9 us (8%)
    pallas_call x1, Pallas kernels, run_slots(): pl.pallas_call(body, grid_spec=grid_spec, out_shape=[jax.ShapeDtypeStruct...  68.4 us
    all_to_all x4, waiting for transfers between devices, exchanged(): lax.all_to_all(value, 'tile', split_axis=0, concat_axis=0, tiled=True)  31 us
    all_to_all x4, starting transfers between devices, exchanged(): lax.all_to_all(value, 'tile', split_axis=0, concat_axis=0, tiled=True)  19.3 us
  transfers between devices with their start and end apart: 8, of which 4 were waited for; matrix products, arithmetic and copies ran while one was open for 5% of the time, Pallas kernels for 0%

profile of v1, /device:TPU:0, one launch (start us, length us, event | category | flops | bytes accessed | tf_op | source)
XLA Modules:
  0.0 157.7 jit_solution(7139341737238393729)
XLA Ops:
  0.6 0.7 convert_bitcast_fusion
  1.4 0.7 convert_element_type.48
  2.4 2.0 %convert_reduce_fusion = f32[16,3,2,256]{3,2,1,0:T(2,128)S(1)} fusion(bf16[16,3,2,2,16,256]{5,4,3,2,1,0:T(8,128)(2,1)} %param.25), kind=kLoop, calls=%fused_computation.1 | loop fusion | flops 1548288 | bytes 1671168 | tf_op jit(solution)/shard_map/reduce_sum | solution.py:445
  5.1 0.9 all_to_all.20
  6.0 7.4 %all-to-all-start = ((f32[16,1,5120]{2,1,0:T(1,128)}), f32[16,1,5120]{2,1,0:T(1,128)S(1)}, u32[]{:S(2)}, u32[]{:S(2)}) async-start(f32[16,1,5120]{2,1,0:T(1,128)} %all_to_all.20), calls=%async_computation | async-start | bytes 655360 | tf_op jit(solution)/shard_map/all_to_all | solution.py:423
  13.4 1.3 fusion.30
  14.9 1.3 fusion.31
  16.6 1.3 collective-permute-start.1
  17.9 3.0 %collective-permute-start = (bf16[16,16,256]{2,1,0:T(8,128)(2,1)S(1)}, bf16[16,16,256]{2,1,0:T(8,128)(2,1)S(1)}, u32[]{:S(2)}, u32[]{:S(2)}) collective-permute-start(bf16[16,16,256]{2,1,0:T(8,128)(2,1)S(1)} %get-tuple-element.70), channel_id=1, source_target_pairs={{0,1},{1,2},{2,3},{3,4},{4,5},{5,6},{6,7},{7,8},{8,9},{9,10},{10,1... | collective-permute-start | bytes 393224 | tf_op jit(solution)/shard_map/ppermute | solution.py:486
  21.0 3.6 %all-to-all-done = f32[16,1,5120]{2,1,0:T(1,128)S(1)} async-done(((f32[16,1,5120]{2,1,0:T(1,128)}), f32[16,1,5120]{2,1,0:T(1,128)S(1)}, u32[]{:S(2)}, u32[]{:S(2)}) %all-to-all-start) | async-done | bytes 327712 | tf_op jit(solution)/shard_map/all_to_all | solution.py:423
  25.3 0.8 copy.110
  26.0 3.5 %all-to-all-start.1 = ((f32[16,1,2048]{2,1,0:T(1,128)}), f32[16,1,2048]{2,1,0:T(1,128)S(1)}, u32[]{:S(2)}, u32[]{:S(2)}) async-start(f32[16,1,2048]{2,1,0:T(1,128)} %copy.110), calls=%async_computation.1 | async-start | bytes 262144 | tf_op jit(solution)/shard_map/all_to_all | solution.py:423
  30.2 0.9 copy.116.refs_20_
  31.3 6.2 %all-to-all-done.1 = f32[16,1,2048]{2,1,0:T(1,128)S(1)} async-done(((f32[16,1,2048]{2,1,0:T(1,128)}), f32[16,1,2048]{2,1,0:T(1,128)S(1)}, u32[]{:S(2)}, u32[]{:S(2)}) %all-to-all-start.1) | async-done | bytes 131104 | tf_op jit(solution)/shard_map/all_to_all | solution.py:423
  37.9 68.4 %shard_map.253 = (f32[16,192,256]{2,1,0:T(8,128)}, f32[16,32,256]{2,1,0:T(8,128)}, bf16[1536,128]{1,0:T(8,128)(2,1)}) custom-call(s32[16]{0:T(128)S(1)} %copy-done.1, s32[1]{0:T(128)} %bitcast.refs_1_, f32[16,3,1024]{2,1,0:T(4,128)S(1)} %reshape.136.refs_2_, bf16[16,192,256]{2,1,0:T(8,128)(2,1)} %bitcast.127, bf16[16,192,256]{2,1,0:T(8,128)(2,1)} %bitcast.92, ...), custom_call_target="tpu_custom_call" | custom-call | flops 32000000000 | bytes 16000000 | tf_op jit(solution)/shard_map/pallas_call | solution.py:407
  106.3 1.2 slice_add_fusion.1
  107.6 1.8 %pad_maximum_fusion = bf16[16,120,128]{2,1,0:T(8,128)(2,1)} fusion(bf16[16,12,128]{2,1,0:T(8,128)(2,1)S(1)} %get-tuple-element.52, bf16[16,12,128]{2,1,0:T(8,128)(2,1)S(1)} %get-tuple-element.51, bf16[16,96,128]{2,1,0:T(8,128)(2,1)} %bitcast.104), kind=kLoop, calls=%fused_computation.5 | loop fusion | flops 1474560 | bytes 983040 | tf_op jit(solution)/shard_map/concatenate | solution.py:540
  109.4 3.6 %all-to-all-start.2 = ((bf16[16,120,128]{2,1,0:T(8,128)(2,1)}), bf16[16,120,128]{2,1,0:T(8,128)(2,1)S(1)}, u32[]{:S(2)}, u32[]{:S(2)}) async-start(bf16[16,120,128]{2,1,0:T(8,128)(2,1)} %pad_maximum_fusion), calls=%async_computation.2 | async-start | bytes 983040 | tf_op jit(solution)/shard_map/all_to_all | solution.py:423
  113.0 1.3 collective-permute-start.3
  114.3 3.0 %collective-permute-start.2 = (f32[16,6,256]{2,1,0:T(8,128)S(1)}, f32[16,6,256]{2,1,0:T(8,128)S(1)}, u32[]{:S(2)}, u32[]{:S(2)}) collective-permute-start(f32[16,6,256]{2,1,0:T(8,128)S(1)} %get-tuple-element.47), channel_id=1, source_target_pairs={{0,1},{1,2},{2,3},{3,4},{4,5},{5,6},{6,7},{7,8},{8,9},{9,10},{10,1... | collective-permute-start | bytes 294920 | tf_op jit(solution)/shard_map/ppermute | solution.py:544
  117.4 9.4 %all-to-all-done.2 = bf16[16,120,128]{2,1,0:T(8,128)(2,1)S(1)} async-done(((bf16[16,120,128]{2,1,0:T(8,128)(2,1)}), bf16[16,120,128]{2,1,0:T(8,128)(2,1)S(1)}, u32[]{:S(2)}, u32[]{:S(2)}) %all-to-all-start.2) | async-done | bytes 491552 | tf_op jit(solution)/shard_map/all_to_all | solution.py:423
  127.4 0.8 pad_maximum_fusion.1
  128.3 4.8 %all-to-all-start.3 = ((bf16[16,120,128]{2,1,0:T(8,128)(2,1)}), bf16[16,120,128]{2,1,0:T(8,128)(2,1)}, u32[]{:S(2)}, u32[]{:S(2)}) async-start(bf16[16,120,128]{2,1,0:T(8,128)(2,1)} %pad_maximum_fusion.1), calls=%async_computation.3 | async-start | bytes 983040 | tf_op jit(solution)/shard_map/all_to_all | solution.py:423
  134.3 0.7 copy.123
  135.1 11.9 %all-to-all-done.3 = bf16[16,120,128]{2,1,0:T(8,128)(2,1)} async-done(((bf16[16,120,128]{2,1,0:T(8,128)(2,1)}), bf16[16,120,128]{2,1,0:T(8,128)(2,1)}, u32[]{:S(2)}, u32[]{:S(2)}) %all-to-all-start.3) | async-done | bytes 491552 | tf_op jit(solution)/shard_map/all_to_all | solution.py:423
  146.9 1.1 slice_convert_fusion
  149.2 0.6 slice.196
  149.9 0.9 slice.195
  150.7 0.9 convert_add_fusion
  151.7 1.0 select_add_fusion
  152.8 1.3 reshape.148
  154.8 2.9 %add_convert_fusion = bf16[16,3,2,2,16,256]{5,4,3,2,1,0:T(8,128)(2,1)} fusion(f32[16,3,2,2,16,256]{5,4,3,2,1,0:T(8,128)S(1)} %bitcast.87, f32[16,3,2,256]{3,2,1,0:T(2,128)} %copy.123, f32[16,3,2,256]{3,2,1,0:T(2,128)S(1)} %copy.121, f32[16,3,2,256]{3,2,1,0:T(2,128)S(1)} %copy.119, pred[16]{0:T(512)(128)(4,1)} %get-tuple-element.71, ...), kind=kLoop, calls=%fused_computation | loop fusion | flops 6291456 | bytes 5013540 | tf_op jit(solution)/shard_map/convert_element_type | solution.py:571
  (113 shorter events, 6.8 us)
Async XLA Ops:
  6.0 18.5 %all-to-all-start = ((f32[16,1,5120]{2,1,0:T(1,128)}), f32[16,1,5120]{2,1,0:T(1,128)S(1)}, u32[]{:S(2)}, u32[]{:S(2)}) async-start(f32[16,1,5120]{2,1,0:T(1,128)} %all_to_all.20), calls=%async_computation | async-start | bytes 655360 | tf_op jit(solution)/shard_map/all_to_all | solution.py:423
  13.4 16.1 %copy-start.11 = (bf16[512,240]{1,0:T(8,128)(2,1)S(1)}, bf16[512,240]{1,0:T(8,128)(2,1)}, u32[]{:S(2)}) copy-start(bf16[512,240]{1,0:T(8,128)(2,1)} %constant.43.clone) | copy-start | bytes 737284
  13.4 16.1 %copy-start.12 = (bf16[512,240]{1,0:T(8,128)(2,1)S(1)}, bf16[512,240]{1,0:T(8,128)(2,1)}, u32[]{:S(2)}) copy-start(bf16[512,240]{1,0:T(8,128)(2,1)} %constant.42.clone) | copy-start | bytes 737284
  14.8 14.8 %copy-start.15 = (bf16[3,3,3,128]{3,2,1,0:T(4,128)(2,1)S(1)}, bf16[3,3,3,128]{3,2,1,0:T(4,128)(2,1)}, u32[]{:S(2)}) copy-start(bf16[3,3,3,128]{3,2,1,0:T(4,128)(2,1)} %param.27) | copy-start | bytes 20740
  14.9 14.9 %copy-start.14 = (bf16[3,4,4,128]{3,2,1,0:T(4,128)(2,1)S(1)}, bf16[3,4,4,128]{3,2,1,0:T(4,128)(2,1)}, u32[]{:S(2)}) copy-start(bf16[3,4,4,128]{3,2,1,0:T(4,128)(2,1)} %param.30) | copy-start | bytes 36868
  14.9 15.0 %copy-start.13 = (bf16[4,4,6,128]{3,1,2,0:T(4,128)(2,1)S(1)}, bf16[4,4,6,128]{3,1,2,0:T(4,128)(2,1)}, u32[]{:S(2)}) copy-start(bf16[4,4,6,128]{3,1,2,0:T(4,128)(2,1)} %param.31) | copy-start | bytes 73732
  14.9 15.2 %copy-start = (bf16[128,128]{1,0:T(8,128)(2,1)S(1)}, bf16[128,128]{1,0:T(8,128)(2,1)}, u32[]{:S(2)}) copy-start(bf16[128,128]{1,0:T(8,128)(2,1)} %refs_22_.1) | copy-start | bytes 98308
  14.9 15.3 %copy-start.10 = (bf16[3,3,128,128]{3,2,1,0:T(8,128)(2,1)S(1)}, bf16[3,3,128,128]{3,2,1,0:T(8,128)(2,1)}, u32[]{:S(2)}) copy-start(bf16[3,3,128,128]{3,2,1,0:T(8,128)(2,1)} %param.28) | copy-start | bytes 884740
  16.6 21.2 %collective-permute-start.1 = (bf16[16,16,256]{2,1,0:T(8,128)(2,1)S(1)}, bf16[16,16,256]{2,1,0:T(8,128)(2,1)S(1)}, u32[]{:S(2)}, u32[]{:S(2)}) collective-permute-start(bf16[16,16,256]{2,1,0:T(8,128)(2,1)S(1)} %get-tuple-element.69), channel_id=1, source_target_pairs={{1,0},{2,1},{3,2},{4,3},{5,4},{6,5},{7,6},{8,7},{9,8},{10,9},{11,1... | collective-permute-start | bytes 393224 | tf_op jit(solution)/shard_map/ppermute | solution.py:487
  17.9 19.9 %collective-permute-start = (bf16[16,16,256]{2,1,0:T(8,128)(2,1)S(1)}, bf16[16,16,256]{2,1,0:T(8,128)(2,1)S(1)}, u32[]{:S(2)}, u32[]{:S(2)}) collective-permute-start(bf16[16,16,256]{2,1,0:T(8,128)(2,1)S(1)} %get-tuple-element.70), channel_id=1, source_target_pairs={{0,1},{1,2},{2,3},{3,4},{4,5},{5,6},{6,7},{7,8},{8,9},{9,10},{10,1... | collective-permute-start | bytes 393224 | tf_op jit(solution)/shard_map/ppermute | solution.py:486
  24.6 13.3 %copy-start.1 = (s32[16]{0:T(128)S(1)}, s32[16]{0:T(128)}, u32[]{:S(2)}) copy-start(s32[16]{0:T(128)} %refs_0_.1) | copy-start | bytes 196
  24.6 13.3 %copy-start.2 = (bf16[224,512]{1,0:T(8,128)(2,1)S(1)}, bf16[224,512]{1,0:T(8,128)(2,1)}, u32[]{:S(2)}) copy-start(bf16[224,512]{1,0:T(8,128)(2,1)} %constant.45.clone.refs_10_) | copy-start | bytes 688132
  24.6 13.3 %copy-start.3 = (bf16[512,48]{1,0:T(8,128)(2,1)S(1)}, bf16[512,48]{1,0:T(8,128)(2,1)}, u32[]{:S(2)}) copy-start(bf16[512,48]{1,0:T(8,128)(2,1)} %constant.46.clone.refs_11_) | copy-start | bytes 147460
  24.6 13.3 %copy-start.4 = (bf16[256,240]{1,0:T(8,128)(2,1)S(1)}, bf16[256,240]{1,0:T(8,128)(2,1)}, u32[]{:S(2)}) copy-start(bf16[256,240]{1,0:T(8,128)(2,1)} %constant.44.clone.refs_8_) | copy-start | bytes 368644
  24.6 13.2 %copy-start.5 = (f32[192,128]{1,0:T(8,128)S(1)}, f32[192,128]{1,0:T(8,128)}, u32[]{:S(2)}) copy-start(f32[192,128]{1,0:T(8,128)} %constant.48.clone.refs_13_) | copy-start | bytes 294916
  24.6 13.2 %copy-start.6 = (bf16[64,256]{1,0:T(8,128)(2,1)S(1)}, bf16[64,256]{1,0:T(8,128)(2,1)}, u32[]{:S(2)}) copy-start(bf16[64,256]{1,0:T(8,128)(2,1)} %constant.52.clone.refs_17_) | copy-start | bytes 98308
  24.7 13.2 %copy-start.7 = (bf16[80,32]{1,0:T(8,128)(2,1)S(1)}, bf16[80,32]{1,0:T(8,128)(2,1)}, u32[]{:S(2)}) copy-start(bf16[80,32]{1,0:T(8,128)(2,1)} %constant.50.clone.refs_15_) | copy-start | bytes 15364
  24.7 13.2 %copy-start.8 = (f32[32,80]{1,0:T(8,128)S(1)}, f32[32,80]{1,0:T(8,128)}, u32[]{:S(2)}) copy-start(f32[32,80]{1,0:T(8,128)} %constant.51.clone.refs_16_) | copy-start | bytes 30724
  26.0 11.4 %all-to-all-start.1 = ((f32[16,1,2048]{2,1,0:T(1,128)}), f32[16,1,2048]{2,1,0:T(1,128)S(1)}, u32[]{:S(2)}, u32[]{:S(2)}) async-start(f32[16,1,2048]{2,1,0:T(1,128)} %copy.110), calls=%async_computation.1 | async-start | bytes 262144 | tf_op jit(solution)/shard_map/all_to_all | solution.py:423
  109.4 17.3 %all-to-all-start.2 = ((bf16[16,120,128]{2,1,0:T(8,128)(2,1)}), bf16[16,120,128]{2,1,0:T(8,128)(2,1)S(1)}, u32[]{:S(2)}, u32[]{:S(2)}) async-start(bf16[16,120,128]{2,1,0:T(8,128)(2,1)} %pad_maximum_fusion), calls=%async_computation.2 | async-start | bytes 983040 | tf_op jit(solution)/shard_map/all_to_all | solution.py:423
  113.0 13.9 %collective-permute-start.3 = (f32[16,6,256]{2,1,0:T(8,128)S(1)}, f32[16,6,256]{2,1,0:T(8,128)S(1)}, u32[]{:S(2)}, u32[]{:S(2)}) collective-permute-start(f32[16,6,256]{2,1,0:T(8,128)S(1)} %get-tuple-element.46), channel_id=1, source_target_pairs={{1,0},{2,1},{3,2},{4,3},{5,4},{6,5},{7,6},{8,7},{9,8},{10,9},{11,1... | collective-permute-start | bytes 294920 | tf_op jit(solution)/shard_map/ppermute | solution.py:545
  114.3 12.6 %collective-permute-start.2 = (f32[16,6,256]{2,1,0:T(8,128)S(1)}, f32[16,6,256]{2,1,0:T(8,128)S(1)}, u32[]{:S(2)}, u32[]{:S(2)}) collective-permute-start(f32[16,6,256]{2,1,0:T(8,128)S(1)} %get-tuple-element.47), channel_id=1, source_target_pairs={{0,1},{1,2},{2,3},{3,4},{4,5},{5,6},{6,7},{7,8},{8,9},{9,10},{10,1... | collective-permute-start | bytes 294920 | tf_op jit(solution)/shard_map/ppermute | solution.py:544
  128.3 18.7 %all-to-all-start.3 = ((bf16[16,120,128]{2,1,0:T(8,128)(2,1)}), bf16[16,120,128]{2,1,0:T(8,128)(2,1)}, u32[]{:S(2)}, u32[]{:S(2)}) async-start(bf16[16,120,128]{2,1,0:T(8,128)(2,1)} %pad_maximum_fusion.1), calls=%async_computation.3 | async-start | bytes 983040 | tf_op jit(solution)/shard_map/all_to_all | solution.py:423
  135.1 19.7 %copy-start.9 = (f32[16,192,256]{2,1,0:T(8,128)S(1)}, f32[16,192,256]{2,1,0:T(8,128)}, u32[]{:S(2)}) copy-start(f32[16,192,256]{2,1,0:T(8,128)} %get-tuple-element.12) | copy-start | bytes 9437188

commit v2 on v1

--- a/solution.py
+++ b/solution.py
@@ -96,11 +96,11 @@
                             sel_o[held(ch, q, target), b, q, 32 + at] = 1
                     if o == -1:
                         sel_o[base + ch * 2 + q, b, q, at] = 1
-                        sel_o[base + 6 + ch * 2 + q, b, q, 32 + at] = 1
+                        sel_o[base + 8 + ch * 2 + q, b, q, 32 + at] = 1
                     else:
-                        sel_o[base + 18 + ch * 2 + q, b, q, 32 + at] = 1
+                        sel_o[base + 24 + ch * 2 + q, b, q, 32 + at] = 1
                     if o == last:
-                        sel_o[base + 12 + ch * 2 + q, b, q, at] = 1
+                        sel_o[base + 16 + ch * 2 + q, b, q, at] = 1
     sel_s_first = sel_s.copy()
     for q in range(2):
         for ch in range(3):
@@ -155,10 +155,99 @@
     return jnp.where(keep(lane), pltpu.roll(value, shift % width, 1), 0.0)
 
 
+def coarse_forward(blocks, tile, coarse_ref, w1_ref, second_t_ref, spread_ref, store, place):
+    patches_s, columns_s, first_slope_s, second_slope_s, feature_s, wide_s = store
+    cells = blocks * CG
+    inputs = jnp.concatenate([coarse_ref[0], jnp.zeros((5, coarse_ref.shape[2]), F32)], axis=0)
+    lane_in = lax.broadcasted_iota(jnp.int32, inputs.shape, 1) % CG
+    by_col = (
+        moved(inputs, 2, lane_in, lambda x: x >= 2),
+        inputs,
+        moved(inputs, -2, lane_in, lambda x: x < CG - 2),
+    )
+    above = jnp.where(tile * blocks >= 4, 1.0, 0.0)
+    below = jnp.where(tile * blocks + 4 <= CG - blocks, 1.0, 0.0)
+    windows = []
+    for window in range(3):
+        pieces = []
+        for row_tap in range(3):
+            for col_tap in range(3):
+                start = (4 * window + 2 * row_tap) * CG
+                pieces.append(by_col[col_tap][:, start : start + cells])
+        pieces.append(jnp.zeros((8, cells), F32))
+        stacked = jnp.concatenate(pieces, axis=0)
+        if window == 0:
+            stacked = stacked * above
+        if window == 2:
+            stacked = stacked * below
+        windows.append(stacked)
+    patches = jnp.concatenate(windows, axis=1).astype(BF)
+    first_value, first_slope = gelu_both(nn(w1_ref[...], patches))
+    yield
+    lane_h = lax.broadcasted_iota(jnp.int32, first_value.shape, 1) % CG
+    first_value = first_value.astype(BF).astype(F32)
+    hidden_by_col = (
+        moved(first_value, 4, lane_h, lambda x: x >= 4).astype(BF),
+        first_value.astype(BF),
+        moved(first_value, -4, lane_h, lambda x: x < CG - 4).astype(BF),
+    )
+    columns = jnp.concatenate(
+        [
+            hidden_by_col[col_tap][:, window * cells : (window + 1) * cells]
+            for window in range(3)
+            for col_tap in range(3)
+        ],
+        axis=0,
+    )
+    second_value, second_slope = gelu_both(nn(second_t_ref[...], columns))
+    yield
+    feature = second_value.astype(BF)
+    patches_s[place] = patches
+    columns_s[place] = columns
+    first_slope_s[place] = first_slope
+    second_slope_s[place] = second_slope
+    feature_s[place] = feature
+    wide_s[place] = nn(feature, spread_ref[...]).astype(BF)
+
+
+def coarse_backward(blocks, d_project, project_ref, second_ref, store, place, grad_ref, fg_ref):
+    patches_s, columns_s, first_slope_s, second_slope_s, feature_s, _ = store
+    cells = blocks * CG
+    grad_ref[PROJECT_AT : PROJECT_AT + 128, :] += nn(feature_s[place], d_project)
+    d_feature = nt(project_ref[...], d_project).astype(BF).astype(F32)
+    d_second = (d_feature * second_slope_s[place]).astype(BF)
+    yield
+    grad_ref[0:1152, :] += nt(columns_s[place], d_second)
+    back = nn(second_ref[...], d_second)
+    yield
+    lane_c = lax.broadcasted_iota(jnp.int32, (128, cells), 1) % CG
+    parts = []
+    for window in range(3):
+        at = window * 384
+        parts.append(
+            back[at + 128 : at + 256]
+            + moved(back[at : at + 128], -4, lane_c, lambda x: x < CG - 4)
+            + moved(back[at + 256 : at + 384], 4, lane_c, lambda x: x >= 4)
+        )
+    d_first = (jnp.concatenate(parts, axis=1) * first_slope_s[place]).astype(BF)
+    fg_ref[...] += nt(patches_s[place], d_first)
+
+
+def advance(stage):
+    next(stage, None)
+
+
+def finish(stage):
+    for _ in stage:
+        pass
+
+
 def slot_kernel(
     blocks,
+    peers,
     ids_ref,
     tile_ref,
+    coarse_first_ref,
     coarse_ref,
     fine_ref,
     cot_ref,
@@ -185,8 +274,10 @@
     up_t_ref,
     up_ref,
     pred_ref,
-    edge_ref,
-    out_ref,
+    to_last_ref,
+    to_first_ref,
+    own_ref,
+    sent_ref,
     grad_ref,
     w_ref,
     u_ref,
@@ -195,10 +286,24 @@
     gu_ref,
     gd_ref,
     fg_ref,
+    d_project_ref,
+    *store,
 ):
     step = pl.program_id(0)
-    cells = blocks * CG
     tile = tile_ref[0]
+    now = lax.rem(step, 3)
+    soon = lax.rem(step + 1, 3)
+    done = lax.rem(step + 2, 3)
+
+    def forward(source, place):
+        return coarse_forward(
+            blocks, tile, source, w1_ref, second_t_ref, spread_ref, store, place
+        )
+
+    def backward(place):
+        return coarse_backward(
+            blocks, d_project_ref[...], project_ref, second_ref, store, place, grad_ref, fg_ref
+        )
 
     @pl.when(step == 0)
     def _():
@@ -214,51 +319,14 @@
         gd_ref[...] = jnp.zeros_like(gd_ref)
         fg_ref[...] = jnp.zeros_like(fg_ref)
         grad_ref[...] = jnp.zeros_like(grad_ref)
-
-    inputs = jnp.concatenate([coarse_ref[0], jnp.zeros((5, coarse_ref.shape[2]), F32)], axis=0)
-    lane_in = lax.broadcasted_iota(jnp.int32, inputs.shape, 1) % CG
-    by_col = (
-        moved(inputs, 2, lane_in, lambda x: x >= 2),
-        inputs,
-        moved(inputs, -2, lane_in, lambda x: x < CG - 2),
-    )
-    above = jnp.where(tile * blocks >= 4, 1.0, 0.0)
-    below = jnp.where(tile * blocks + 4 <= CG - blocks, 1.0, 0.0)
-    windows = []
-    for window in range(3):
-        pieces = []
-        for row_tap in range(3):
-            for col_tap in range(3):
-                start = (4 * window + 2 * row_tap) * CG
-                pieces.append(by_col[col_tap][:, start : start + cells])
-        pieces.append(jnp.zeros((8, cells), F32))
-        stacked = jnp.concatenate(pieces, axis=0)
-        if window == 0:
-            stacked = stacked * above
-        if window == 2:
-            stacked = stacked * below
-        windows.append(stacked)
-    patches = jnp.concatenate(windows, axis=1).astype(BF)
-    first_value, first_slope = gelu_both(nn(w1_ref[...], patches))
-    lane_h = lax.broadcasted_iota(jnp.int32, first_value.shape, 1) % CG
-    first_value = first_value.astype(BF).astype(F32)
-    hidden_by_col = (
-        moved(first_value, 4, lane_h, lambda x: x >= 4).astype(BF),
-        first_value.astype(BF),
-        moved(first_value, -4, lane_h, lambda x: x < CG - 4).astype(BF),
-    )
-    columns = jnp.concatenate(
-        [
-            hidden_by_col[col_tap][:, window * cells : (window + 1) * cells]
-            for window in range(3)
-            for col_tap in range(3)
-        ],
-        axis=0,
-    )
-    second_value, second_slope = gelu_both(nn(second_t_ref[...], columns))
-    feature = second_value.astype(BF)
-    feature_wide = nn(feature, spread_ref[...]).astype(BF)
-
+        d_project_ref[...] = jnp.zeros_like(d_project_ref)
+        for buffer in store:
+            buffer[2] = jnp.zeros(buffer.shape[1:], buffer.dtype)
+        finish(forward(coarse_first_ref, 0))
+
+    back = backward(done)
+    ahead = forward(coarse_ref, soon)
+    advance(back)
     later = later_ref[0]
     later_high = later.astype(BF).astype(F32)
     later_both = jnp.concatenate([later_high, later - later_high], axis=0).astype(BF)
@@ -283,10 +351,8 @@
         s_taps = jnp.concatenate(
             [s0, s1, moved(s1, 1, lane64, not_first), moved(s0, -1, lane64, not_last)], axis=0
         ).astype(BF)
-        third = nn(
-            w_ref[...],
-            jnp.concatenate([x_taps, feature_wide[:, b * HALF : (b + 1) * HALF]], axis=0),
-        )
+        wide = store[5][now, :, b * HALF : (b + 1) * HALF]
+        third = nn(w_ref[...], jnp.concatenate([x_taps, wide], axis=0))
         return x_taps, s_taps, third, nn(u_ref[...], s_taps)
 
     def middle(entered):
@@ -315,8 +381,14 @@
     for turn in range(blocks + 2):
         if turn < blocks:
             entered[turn] = enter(turn)
+        if turn == 1:
+            advance(back)
+        if turn == 2:
+            finish(back)
         if 0 <= turn - 1 < blocks:
             held[turn - 1] = middle(entered.pop(turn - 1))
+        if turn >= 3:
+            advance(ahead)
         if turn - 2 >= 0:
             pair, cells_sum = leave(held.pop(turn - 2))
             combined += pair
@@ -325,31 +397,26 @@
     out = jnp.concatenate(combined, axis=0)
     out_high = out.astype(BF)
     out_low = (out - out_high.astype(F32)).astype(BF)
+    finish(ahead)
     placed = nn(sel_o_ref[...], out_high) + nn(sel_o_ref[...], out_low)
     main = pred_ref.shape[1]
     pred_ref[0] = placed[0:main]
-    edge_ref[0] = placed[main : main + 32]
-
-    d_project = jnp.concatenate(pooled, axis=0).astype(BF)
-    grad_ref[PROJECT_AT : PROJECT_AT + 128, :] += nn(feature, d_project)
-    d_feature = nt(project_ref[...], d_project).astype(BF).astype(F32)
-    d_second = (d_feature * second_slope).astype(BF)
-    grad_ref[0:1152, :] += nt(columns, d_second)
-    back = nn(second_ref[...], d_second)
-    lane_c = lax.broadcasted_iota(jnp.int32, (128, cells), 1) % CG
-    parts = []
-    for window in range(3):
-        at = window * 384
-        parts.append(
-            back[at + 128 : at + 256]
-            + moved(back[at : at + 128], -4, lane_c, lambda x: x < CG - 4)
-            + moved(back[at + 256 : at + 384], 4, lane_c, lambda x: x >= 4)
-        )
-    d_first = (jnp.concatenate(parts, axis=1) * first_slope).astype(BF)
-    fg_ref[...] += nt(patches, d_first)
+    before_flux = placed[main + 8 : main + 16]
+    own = before_flux * jnp.where(tile >= 1, 1.0, 0.0)
+    flux = placed[main + 24 : main + 32] + own
+    to_last_ref[0] = placed[main : main + 8] + before_flux
+    to_first_ref[0] = placed[main + 16 : main + 24]
+    own_ref[0] = own
+    flux = jnp.concatenate([flux[:, 0:128], flux[:, 128:256]], axis=0)
+    flux_high = flux.astype(BF)
+    chunk = GRAD_ROWS // peers
+    sent_ref[step, chunk : chunk + 16, :] = flux_high
+    sent_ref[step, chunk + 16 : chunk + 32, :] = (flux - flux_high.astype(F32)).astype(BF)
+    d_project_ref[...] = jnp.concatenate(pooled, axis=0).astype(BF)
 
     @pl.when(step == pl.num_programs(0) - 1)
     def _():
+        finish(backward(now))
         up = jnp.zeros((96, 128), F32)
         down = jnp.zeros((48, 128), F32)
         for r in range(4):
@@ -359,12 +426,15 @@
         grad_ref[UP_AT : UP_AT + 96, :] = up
         grad_ref[DOWN_AT : DOWN_AT + 48, :] = down
         grad_ref[FIRST_AT : FIRST_AT + 32, :] = exact(eft_ref[...], fg_ref[...])
-        out_ref[...] = grad_ref[...].astype(BF)
-
-
-def run_slots(ids, tile, coarse, fine, cot, before, after, later, fixed, weights):
+        for t in range(peers):
+            sent_ref[t, 0:chunk, :] = grad_ref[t * chunk : (t + 1) * chunk, :].astype(BF)
+
+
+def run_slots(peers, ids, tile, coarse, fine, cot, before, after, later, fixed, weights):
     slots, main, width = fine.shape
     blocks = main // 48
+    cells = blocks * CG
+    chunk = GRAD_ROWS // peers
 
     def whole(array):
         return pl.BlockSpec(array.shape, lambda n, ids, tile: (0,) * array.ndim)
@@ -372,23 +442,29 @@
     def per_slot(array):
         return pl.BlockSpec((1,) + array.shape[1:], lambda n, ids, tile: (n, 0, 0))
 
+    one = (1,) + coarse.shape[1:]
     in_specs = [
-        pl.BlockSpec((1,) + coarse.shape[1:], lambda n, ids, tile: (ids[n], 0, 0)),
+        pl.BlockSpec(one, lambda n, ids, tile: (ids[0], 0, 0)),
+        pl.BlockSpec(one, lambda n, ids, tile: (ids[jnp.minimum(n + 1, slots - 1)], 0, 0)),
         per_slot(fine),
         per_slot(cot),
         per_slot(before),
         per_slot(after),
         per_slot(later),
     ] + [whole(a) for a in fixed + weights]
+    edge = jax.ShapeDtypeStruct((slots, 8, width), F32)
+    out_shape = [
+        jax.ShapeDtypeStruct((slots, main, width), F32),
+        edge,
+        edge,
+        edge,
+        jax.ShapeDtypeStruct((peers, chunk + 32, 128), BF),
+    ]
     grid_spec = pltpu.PrefetchScalarGridSpec(
         num_scalar_prefetch=2,
         grid=(slots,),
         in_specs=in_specs,
-        out_specs=[
-            pl.BlockSpec((1, main, width), lambda n, ids, tile: (n, 0, 0)),
-            pl.BlockSpec((1, 32, width), lambda n, ids, tile: (n, 0, 0)),
-            pl.BlockSpec((GRAD_ROWS, 128), lambda n, ids, tile: (0, 0)),
-        ],
+        out_specs=[per_slot(a) for a in out_shape[:4]] + [whole(out_shape[4])],
         scratch_shapes=[
             pltpu.VMEM((GRAD_ROWS, 128), F32),
             pltpu.VMEM((512, 256), BF),
@@ -398,25 +474,91 @@
             pltpu.VMEM((256, 512), F32),
             pltpu.VMEM((128, 512), F32),
             pltpu.VMEM((80, 128), F32),
+            pltpu.VMEM((cells, 128), BF),
+            pltpu.VMEM((3, 80, 3 * cells), BF),
+            pltpu.VMEM((3, 1152, cells), BF),
+            pltpu.VMEM((3, 128, 3 * cells), F32),
+            pltpu.VMEM((3, 128, cells), F32),
+            pltpu.VMEM((3, 128, cells), BF),
+            pltpu.VMEM((3, 128, blocks * HALF), BF),
         ],
     )
 
     def body(*refs):
-        slot_kernel(blocks, *refs)
+        slot_kernel(blocks, peers, *refs)
 
     return pl.pallas_call(
         body,
         grid_spec=grid_spec,
-        out_shape=[
-            jax.ShapeDtypeStruct((slots, main, width), F32),
-            jax.ShapeDtypeStruct((slots, 32, width), F32),
-            jax.ShapeDtypeStruct((GRAD_ROWS, 128), BF),
-        ],
+        out_shape=out_shape,
         compiler_params=pltpu.CompilerParams(vmem_limit_bytes=52 * 1024 * 1024),
         cost_estimate=pl.CostEstimate(
             flops=slots * blocks * 500_000_000, bytes_accessed=16_000_000, transcendentals=0
         ),
-    )(ids, tile, coarse, fine, cot, before, after, later, *fixed, *weights)
+    )(ids, tile, coarse, coarse, fine, cot, before, after, later, *fixed, *weights)
+
+
+FINAL_SLOTS = 4
+PARTS = ((0, 1152), (PROJECT_AT, 128), (UP_AT, 96), (DOWN_AT, 48), (FIRST_AT, 32))
+
+
+def final_kernel(chunk, rows, back_ref, pred_ref, own_ref, first_ref, last_ref, out_ref, *grads):
+    step = pl.program_id(0)
+
+    @pl.when(step == 0)
+    def _():
+        for (start, size), grad in zip(PARTS, grads):
+            at = start
+            while at < start + size:
+                t = at // chunk
+                stop = min((t + 1) * chunk, start + size)
+                grad[at - start : stop - start, :] = back_ref[
+                    t, at - t * chunk : stop - t * chunk, :
+                ].astype(F32)
+                at = stop
+
+    row = lax.broadcasted_iota(jnp.int32, (rows, HALF), 0)
+    for s in range(out_ref.shape[0]):
+        slot = step * out_ref.shape[0] + s
+        ahead = back_ref[slot, chunk : chunk + 16, :].astype(F32)
+        ahead = ahead + back_ref[slot, chunk + 16 : chunk + 32, :].astype(F32)
+        base = jnp.concatenate([ahead[0:8], ahead[8:16]], axis=1) + own_ref[s]
+        for k in range(3):
+            for p in range(2):
+                for q in range(2):
+                    at = ((k * 2 + p) * 2 + q) * rows
+                    pick = slice(k * 2 + q, k * 2 + q + 1)
+                    edge = (first_ref if p == 0 else last_ref)[s, pick, :]
+                    reached = row == (0 if p == 0 else rows - 1)
+                    out_ref[s, at : at + rows, :] = (
+                        pred_ref[s, at : at + rows, :]
+                        + base[pick]
+                        + jnp.where(reached, edge, 0.0)
+                    ).astype(BF)
+
+
+def run_final(back, pred, own, first, last):
+    slots, main, width = pred.shape
+    chunk = back.shape[1] - 32
+    held = FINAL_SLOTS if main % 192 == 0 else 2 * FINAL_SLOTS
+
+    def per_slots(array):
+        return pl.BlockSpec((held,) + array.shape[1:], lambda n: (n, 0, 0))
+
+    def body(*refs):
+        final_kernel(chunk, main // 12, *refs)
+
+    return pl.pallas_call(
+        body,
+        grid=(slots // held,),
+        in_specs=[pl.BlockSpec(back.shape, lambda n: (0, 0, 0))]
+        + [per_slots(a) for a in (pred, own, first, last)],
+        out_specs=[per_slots(pred)]
+        + [pl.BlockSpec((size, 128), lambda n: (0, 0)) for _, size in PARTS],
+        out_shape=[jax.ShapeDtypeStruct(pred.shape, BF)]
+        + [jax.ShapeDtypeStruct((size, 128), F32) for _, size in PARTS],
+        compiler_params=pltpu.CompilerParams(vmem_limit_bytes=32 * 1024 * 1024),
+    )(back, pred, own, first, last)
 
 
 def exchanged(value):
@@ -515,7 +657,8 @@
         up_flat.T,
         up_flat,
     ]
-    pred_local, edges, grads = run_slots(
+    pred_local, last_edge, first_edge, own, sent = run_slots(
+        peers,
         sample_ids,
         position.reshape(1).astype(jnp.int32),
         coarse,
@@ -528,54 +671,35 @@
         weights,
     )
 
-    before_flux = jnp.where(position >= 1, edges[:, 6:12], 0.0)
-    flux = edges[:, 18:24] + before_flux
     chunk = GRAD_ROWS // peers
-    extra = (slots // peers) * 12
-
-    def halves(value):
-        high = lax.reduce_precision(value, 8, 7)
-        return [high.astype(BF), (value - high).astype(BF)]
-
-    sent = jnp.concatenate(
-        [grads.reshape(peers, chunk, 128)] + halves(flux.reshape(peers, extra, 128)), axis=1
-    )
     got = exchanged(sent).astype(F32)
-    to_first = lax.ppermute(edges[:, 12:18], "tile", up)
-    to_last = lax.ppermute(edges[:, 0:6] + edges[:, 6:12], "tile", down)
+    to_first = lax.ppermute(first_edge, "tile", up)
+    to_last = lax.ppermute(last_edge, "tile", down)
     reduced = jnp.sum(got[:, :chunk], axis=0).astype(BF)
-    sums = got[:, chunk : chunk + extra] + got[:, chunk + extra :]
+    sums = got[:, chunk : chunk + 16] + got[:, chunk + 16 :]
     ahead = jnp.sum(jnp.where((other < order)[:, :, None, None], sums[None], 0.0), axis=1)
+    high = lax.reduce_precision(ahead, 8, 7)
     reduced, to_first, to_last = lax.optimization_barrier((reduced, to_first, to_last))
     back = exchanged(
         jnp.concatenate(
-            [jnp.broadcast_to(reduced, (peers, chunk, 128))] + halves(ahead), axis=1
+            [
+                jnp.broadcast_to(reduced, (peers, chunk, 128)),
+                high.astype(BF),
+                (ahead - high).astype(BF),
+            ],
+            axis=1,
         )
     )
-    total = back[:, :chunk].reshape(GRAD_ROWS, 128).astype(F32)
-    ahead = back[:, chunk : chunk + extra].astype(F32) + back[:, chunk + extra :].astype(F32)
-    base = ahead.reshape(slots, 6, HALF) + before_flux
-
-    shape = (slots, 3, 2, 2, rows, HALF)
-    half_row = lax.broadcasted_iota(jnp.int32, shape, 2)
-    fine_row_at = lax.broadcasted_iota(jnp.int32, shape, 4)
-
-    def over_rows(value):
-        return value.reshape(slots, 3, 1, 2, 1, HALF)
-
-    prediction = (
-        pred_local.reshape(shape)
-        + over_rows(base)
-        + jnp.where((half_row == 0) & (fine_row_at == 0), over_rows(to_first), 0.0)
-        + jnp.where((half_row == 1) & (fine_row_at == rows - 1), over_rows(to_last), 0.0)
-    ).astype(BF)
+    prediction, dilated, project, up_grad, down_grad, first = run_final(
+        back, pred_local, own, to_first, to_last
+    )
     return (
-        prediction,
-        total[FIRST_AT : FIRST_AT + 27].reshape(first_weight.shape),
-        total[0:1152].reshape(dilated_weight.shape),
-        total[PROJECT_AT : PROJECT_AT + 128],
-        total[DOWN_AT : DOWN_AT + 48].reshape(down_weight.shape),
-        total[UP_AT : UP_AT + 96].reshape(up_weight.shape),
+        prediction.reshape(fine_fields.shape),
+        first[0:27].reshape(first_weight.shape),
+        dilated.reshape(dilated_weight.shape),
+        project,
+        down_grad.reshape(down_weight.shape),
+        up_grad.reshape(up_weight.shape),
     )
 
 

time: 159 us -> 139 us (0.87)
  blocking collectives: 0 us -> 18.7 us
  waiting for transfers between devices: 31 us -> 19.9 us
  other arithmetic: 16 us -> 5.84 us
  Pallas kernels: 68.4 us -> 62 us
  starting transfers between devices: 27.9 us -> 22.3 us
  local copies, waits for them, and re-layouts: 12.9 us -> 8.4 us
    all_to_all x0 -> x1, blocking collectives: none -> 18.7 us  [exchanged(): lax.all_to_all(value, 'tile', split_axis=0, concat_axis=0, tiled=True)]
    all_to_all x4 -> x3, waiting for transfers between devices: 31 us -> 19.9 us  [exchanged(): lax.all_to_all(value, 'tile', split_axis=0, concat_axis=0, tiled=True)]
    pallas_call x1 -> x2, Pallas kernels: 68.4 us -> 62 us  [the longest x1 59.9 us: run_slots(): pl.pallas_call(body, grid_spec=grid_spec, out_shape=out_shape, compiler_p...]
    all_to_all x4 -> x3, starting transfers between devices: 19.3 us -> 14.5 us  [exchanged(): lax.all_to_all(value, 'tile', split_axis=0, concat_axis=0, tiled=True)]
    convert_element_type x4 -> x1, other arithmetic: 3.99 us -> 0.03 us  [local(): high.astype(BF)]
    add x4 -> x1, other arithmetic: 3.14 us -> 0.02 us  [local(): sums = got[:, chunk:chunk + 16] + got[:, chunk + 16:]]
    slice x5 -> x0, local copies, waits for them, and re-layouts: 2.71 us -> none  [the longest x1 0.86 us: local(): total[0:1152].reshape(dilated_weight.shape)]
    concatenate x2 -> x1, other arithmetic: 2.68 us -> 0.04 us  [local(): jnp.concatenate([jnp.broadcast_to(reduced, (peers, chunk, 128)), high.ast...]
  transfers between devices with their start and end apart: 8 -> 7, of which waited for: 4 -> 3; matrix products, arithmetic and copies ran while one was open for 5% -> 5% of each run, Pallas kernels for 0% -> 0%
where the time goes in v2:
time: 139 us
  Pallas kernels  62 us (45%)
  starting transfers between devices  22.3 us (16%)
  waiting for transfers between devices  19.9 us (14%)
  blocking collectives  18.7 us (13%)
  local copies, waits for them, and re-layouts  8.4 us (6%)
  other arithmetic  5.84 us (4%)
    pallas_call x1, Pallas kernels, run_slots(): pl.pallas_call(body, grid_spec=grid_spec, out_shape=out_shape, compiler_p...  59.9 us
    all_to_all x3, waiting for transfers between devices, exchanged(): lax.all_to_all(value, 'tile', split_axis=0, concat_axis=0, tiled=True)  19.9 us
    all_to_all x1, blocking collectives, exchanged(): lax.all_to_all(value, 'tile', split_axis=0, concat_axis=0, tiled=True)  18.7 us
    all_to_all x3, starting transfers between devices, exchanged(): lax.all_to_all(value, 'tile', split_axis=0, concat_axis=0, tiled=True)  14.5 us
    ppermute x1, starting transfers between devices, local(): from_before = lax.ppermute(edge_last, 'tile', up)  3.04 us
  transfers between devices with their start and end apart: 7, of which 3 were waited for; matrix products, arithmetic and copies ran while one was open for 5% of the time, Pallas kernels for 0%

profile of v2, /device:TPU:0, one launch (start us, length us, event | category | flops | bytes accessed | tf_op | source)
XLA Modules:
  0.0 138.6 jit_solution(988569286139060588)
XLA Ops:
  0.6 0.7 convert_bitcast_fusion
  1.4 0.7 convert_element_type.27
  2.4 2.0 %convert_reduce_fusion = f32[16,3,2,256]{3,2,1,0:T(2,128)S(1)} fusion(bf16[16,3,2,2,16,256]{5,4,3,2,1,0:T(8,128)(2,1)} %param.25), kind=kLoop, calls=%fused_computation | loop fusion | flops 1548288 | bytes 1671168 | tf_op jit(solution)/shard_map/reduce_sum | solution.py:587
  4.7 0.3 stack.67
  5.1 0.9 all_to_all.20
  6.0 7.4 %all-to-all-start = ((f32[16,1,5120]{2,1,0:T(1,128)}), f32[16,1,5120]{2,1,0:T(1,128)S(1)}, u32[]{:S(2)}, u32[]{:S(2)}) async-start(f32[16,1,5120]{2,1,0:T(1,128)} %all_to_all.20), calls=%async_computation | async-start | bytes 655360 | tf_op jit(solution)/shard_map/all_to_all | solution.py:565
  13.4 1.3 fusion.29
  14.9 1.3 fusion.30
  16.5 0.1 maximum_maximum_fusion.1
  16.6 1.3 collective-permute-start.1
  17.9 3.0 %collective-permute-start = (bf16[16,16,256]{2,1,0:T(8,128)(2,1)S(1)}, bf16[16,16,256]{2,1,0:T(8,128)(2,1)S(1)}, u32[]{:S(2)}, u32[]{:S(2)}) collective-permute-start(bf16[16,16,256]{2,1,0:T(8,128)(2,1)S(1)} %get-tuple-element.87), channel_id=1, source_target_pairs={{0,1},{1,2},{2,3},{3,4},{4,5},{5,6},{6,7},{7,8},{8,9},{9,10},{10,1... | collective-permute-start | bytes 393224 | tf_op jit(solution)/shard_map/ppermute | solution.py:628
  21.0 3.6 %all-to-all-done = f32[16,1,5120]{2,1,0:T(1,128)S(1)} async-done(((f32[16,1,5120]{2,1,0:T(1,128)}), f32[16,1,5120]{2,1,0:T(1,128)S(1)}, u32[]{:S(2)}, u32[]{:S(2)}) %all-to-all-start) | async-done | bytes 327712 | tf_op jit(solution)/shard_map/all_to_all | solution.py:565
  24.7 0.5 select_reduce_fusion.1
  25.2 0.8 copy.93
  26.0 3.5 %all-to-all-start.1 = ((f32[16,1,2048]{2,1,0:T(1,128)}), f32[16,1,2048]{2,1,0:T(1,128)S(1)}, u32[]{:S(2)}, u32[]{:S(2)}) async-start(f32[16,1,2048]{2,1,0:T(1,128)} %copy.93), calls=%async_computation.1 | async-start | bytes 262144 | tf_op jit(solution)/shard_map/all_to_all | solution.py:565
  29.6 0.7 broadcast_select_fusion.refs_10_
  30.3 0.1 copy.94
  30.5 0.1 copy.96
  30.9 0.9 copy.99.refs_21_
  31.8 0.1 reshape.117.refs_2_.refs_3_
  32.0 5.5 %all-to-all-done.1 = f32[16,1,2048]{2,1,0:T(1,128)S(1)} async-done(((f32[16,1,2048]{2,1,0:T(1,128)}), f32[16,1,2048]{2,1,0:T(1,128)S(1)}, u32[]{:S(2)}, u32[]{:S(2)}) %all-to-all-start.1) | async-done | bytes 131104 | tf_op jit(solution)/shard_map/all_to_all | solution.py:565
  37.5 0.3 reduce
  37.9 59.9 %shard_map.253 = (f32[16,192,256]{2,1,0:T(8,128)}, f32[16,8,256]{2,1,0:T(8,128)S(1)}, f32[16,8,256]{2,1,0:T(8,128)S(1)}, f32[16,8,256]{2,1,0:T(8,128)S(1)}, bf16[16,128,128]{2,1,0:T(8,128)(2,1)}) custom-call(s32[16]{0:T(128)S(1)} %copy-done.2, s32[1]{0:T(128)} %bitcast.refs_1_, f32[16,3,1024]{2,1,0:T(4,128)S(1)} %reshape.117.refs_2_.refs_3_, ...), custom_call_target="tpu_custom_call" | custom-call | flops 32000000000 | bytes 16000000 | tf_op jit(solution)/shard_map/pallas_call | solution.py:490
  97.8 3.6 %all-to-all-start.2 = ((bf16[16,128,128]{2,1,0:T(8,128)(2,1)}), bf16[16,128,128]{2,1,0:T(8,128)(2,1)S(1)}, u32[]{:S(2)}, u32[]{:S(2)}) async-start(bf16[16,128,128]{2,1,0:T(8,128)(2,1)} %get-tuple-element.20), calls=%async_computation.2 | async-start | bytes 1048576 | tf_op jit(solution)/shard_map/all_to_all | solution.py:565
  101.4 2.2 %collective-permute-start.2 = (f32[16,8,256]{2,1,0:T(8,128)S(1)}, f32[16,8,256]{2,1,0:T(8,128)S(1)}, u32[]{:S(2)}, u32[]{:S(2)}) collective-permute-start(f32[16,8,256]{2,1,0:T(8,128)S(1)} %get-tuple-element.21), channel_id=1, source_target_pairs={{0,1},{1,2},{2,3},{3,4},{4,5},{5,6},{6,7},{7,8},{8,9},{9,10},{10,1... | collective-permute-start | bytes 393224 | tf_op jit(solution)/shard_map/ppermute | solution.py:676
  103.6 1.3 collective-permute-start.3
  104.9 10.9 %all-to-all-done.2 = bf16[16,128,128]{2,1,0:T(8,128)(2,1)S(1)} async-done(((bf16[16,128,128]{2,1,0:T(8,128)(2,1)}), bf16[16,128,128]{2,1,0:T(8,128)(2,1)S(1)}, u32[]{:S(2)}, u32[]{:S(2)}) %all-to-all-start.2) | async-done | bytes 524320 | tf_op jit(solution)/shard_map/all_to_all | solution.py:565
  116.0 0.3 select_reduce_fusion
  116.5 18.7 %all_to_all.31.refs_0_ = bf16[16,128,128]{2,1,0:T(8,128)(2,1)S(1)} all-to-all(bf16[16,128,128]{2,1,0:T(8,128)(2,1)S(1)} %pad_maximum_fusion), channel_id=1, replica_groups=mesh['groups'=2,'tile'=16] {'tile'}, dimensions={0} | all-to-all | bytes 1048576 | tf_op jit(solution)/shard_map/all_to_all | solution.py:565
  135.2 2.1 %shard_map.254 = (bf16[16,192,256]{2,1,0:T(8,128)(2,1)}, f32[1152,128]{1,0:T(8,128)}, f32[128,128]{1,0:T(8,128)}, f32[96,128]{1,0:T(8,128)S(1)}, f32[48,128]{1,0:T(8,128)}, /*index=5*/f32[32,128]{1,0:T(8,128)S(1)}) custom-call(bf16[16,128,128]{2,1,0:T(8,128)(2,1)S(1)} %all_to_all.31.refs_0_, f32[16,192,256]{2,1,0:T(8,128)S(1)} %copy-done, ...), custom_call_target="tpu_custom_call" | custom-call | tf_op jit(solution)/shard_map/pallas_call | solution.py:551
  137.3 0.6 reshape.126
  137.9 0.6 copy.100
  (90 shorter events, 1.5 us)
Async XLA Ops:
  6.0 18.5 %all-to-all-start = ((f32[16,1,5120]{2,1,0:T(1,128)}), f32[16,1,5120]{2,1,0:T(1,128)S(1)}, u32[]{:S(2)}, u32[]{:S(2)}) async-start(f32[16,1,5120]{2,1,0:T(1,128)} %all_to_all.20), calls=%async_computation | async-start | bytes 655360 | tf_op jit(solution)/shard_map/all_to_all | solution.py:565
  13.4 16.1 %copy-start.11 = (bf16[512,240]{1,0:T(8,128)(2,1)S(1)}, bf16[512,240]{1,0:T(8,128)(2,1)}, u32[]{:S(2)}) copy-start(bf16[512,240]{1,0:T(8,128)(2,1)} %constant.37.clone) | copy-start | bytes 737284
  13.4 16.1 %copy-start.12 = (bf16[512,240]{1,0:T(8,128)(2,1)S(1)}, bf16[512,240]{1,0:T(8,128)(2,1)}, u32[]{:S(2)}) copy-start(bf16[512,240]{1,0:T(8,128)(2,1)} %constant.36.clone) | copy-start | bytes 737284
  14.8 15.5 %copy-start.15 = (bf16[3,3,3,128]{3,2,1,0:T(4,128)(2,1)S(1)}, bf16[3,3,3,128]{3,2,1,0:T(4,128)(2,1)}, u32[]{:S(2)}) copy-start(bf16[3,3,3,128]{3,2,1,0:T(4,128)(2,1)} %param.27) | copy-start | bytes 20740
  14.9 15.6 %copy-start.14 = (bf16[3,4,4,128]{3,2,1,0:T(4,128)(2,1)S(1)}, bf16[3,4,4,128]{3,2,1,0:T(4,128)(2,1)}, u32[]{:S(2)}) copy-start(bf16[3,4,4,128]{3,2,1,0:T(4,128)(2,1)} %param.30) | copy-start | bytes 36868
  14.9 15.7 %copy-start.13 = (bf16[4,4,6,128]{3,1,2,0:T(4,128)(2,1)S(1)}, bf16[4,4,6,128]{3,1,2,0:T(4,128)(2,1)}, u32[]{:S(2)}) copy-start(bf16[4,4,6,128]{3,1,2,0:T(4,128)(2,1)} %param.31) | copy-start | bytes 73732
  14.9 15.8 %copy-start.1 = (bf16[128,128]{1,0:T(8,128)(2,1)S(1)}, bf16[128,128]{1,0:T(8,128)(2,1)}, u32[]{:S(2)}) copy-start(bf16[128,128]{1,0:T(8,128)(2,1)} %refs_23_.1) | copy-start | bytes 98308
  14.9 15.9 %copy-start.10 = (bf16[3,3,128,128]{3,2,1,0:T(8,128)(2,1)S(1)}, bf16[3,3,128,128]{3,2,1,0:T(8,128)(2,1)}, u32[]{:S(2)}) copy-start(bf16[3,3,128,128]{3,2,1,0:T(8,128)(2,1)} %param.28) | copy-start | bytes 884740
  16.6 21.2 %collective-permute-start.1 = (bf16[16,16,256]{2,1,0:T(8,128)(2,1)S(1)}, bf16[16,16,256]{2,1,0:T(8,128)(2,1)S(1)}, u32[]{:S(2)}, u32[]{:S(2)}) collective-permute-start(bf16[16,16,256]{2,1,0:T(8,128)(2,1)S(1)} %get-tuple-element.86), channel_id=1, source_target_pairs={{1,0},{2,1},{3,2},{4,3},{5,4},{6,5},{7,6},{8,7},{9,8},{10,9},{11,1... | collective-permute-start | bytes 393224 | tf_op jit(solution)/shard_map/ppermute | solution.py:629
  17.9 19.9 %collective-permute-start = (bf16[16,16,256]{2,1,0:T(8,128)(2,1)S(1)}, bf16[16,16,256]{2,1,0:T(8,128)(2,1)S(1)}, u32[]{:S(2)}, u32[]{:S(2)}) collective-permute-start(bf16[16,16,256]{2,1,0:T(8,128)(2,1)S(1)} %get-tuple-element.87), channel_id=1, source_target_pairs={{0,1},{1,2},{2,3},{3,4},{4,5},{5,6},{6,7},{7,8},{8,9},{9,10},{10,1... | collective-permute-start | bytes 393224 | tf_op jit(solution)/shard_map/ppermute | solution.py:628
  24.6 13.2 %copy-start.2 = (s32[16]{0:T(128)S(1)}, s32[16]{0:T(128)}, u32[]{:S(2)}) copy-start(s32[16]{0:T(128)} %refs_0_.1) | copy-start | bytes 196
  24.6 13.2 %copy-start.3 = (bf16[224,512]{1,0:T(8,128)(2,1)S(1)}, bf16[224,512]{1,0:T(8,128)(2,1)}, u32[]{:S(2)}) copy-start(bf16[224,512]{1,0:T(8,128)(2,1)} %constant.39.clone.refs_11_) | copy-start | bytes 688132
  24.6 13.2 %copy-start.4 = (bf16[512,48]{1,0:T(8,128)(2,1)S(1)}, bf16[512,48]{1,0:T(8,128)(2,1)}, u32[]{:S(2)}) copy-start(bf16[512,48]{1,0:T(8,128)(2,1)} %constant.40.clone.refs_12_) | copy-start | bytes 147460
  24.6 13.2 %copy-start.5 = (bf16[256,240]{1,0:T(8,128)(2,1)S(1)}, bf16[256,240]{1,0:T(8,128)(2,1)}, u32[]{:S(2)}) copy-start(bf16[256,240]{1,0:T(8,128)(2,1)} %constant.38.clone.refs_9_) | copy-start | bytes 368644
  24.6 13.2 %copy-start.6 = (f32[192,128]{1,0:T(8,128)S(1)}, f32[192,128]{1,0:T(8,128)}, u32[]{:S(2)}) copy-start(f32[192,128]{1,0:T(8,128)} %constant.42.clone.refs_14_) | copy-start | bytes 294916
  24.6 13.2 %copy-start.7 = (bf16[64,256]{1,0:T(8,128)(2,1)S(1)}, bf16[64,256]{1,0:T(8,128)(2,1)}, u32[]{:S(2)}) copy-start(bf16[64,256]{1,0:T(8,128)(2,1)} %constant.46.clone.refs_18_) | copy-start | bytes 98308
  24.7 13.2 %copy-start.8 = (bf16[80,32]{1,0:T(8,128)(2,1)S(1)}, bf16[80,32]{1,0:T(8,128)(2,1)}, u32[]{:S(2)}) copy-start(bf16[80,32]{1,0:T(8,128)(2,1)} %constant.44.clone.refs_16_) | copy-start | bytes 15364
  24.7 13.2 %copy-start.9 = (f32[32,80]{1,0:T(8,128)S(1)}, f32[32,80]{1,0:T(8,128)}, u32[]{:S(2)}) copy-start(f32[32,80]{1,0:T(8,128)} %constant.45.clone.refs_17_) | copy-start | bytes 30724
  26.0 11.4 %all-to-all-start.1 = ((f32[16,1,2048]{2,1,0:T(1,128)}), f32[16,1,2048]{2,1,0:T(1,128)S(1)}, u32[]{:S(2)}, u32[]{:S(2)}) async-start(f32[16,1,2048]{2,1,0:T(1,128)} %copy.93), calls=%async_computation.1 | async-start | bytes 262144 | tf_op jit(solution)/shard_map/all_to_all | solution.py:565
  97.8 18.0 %all-to-all-start.2 = ((bf16[16,128,128]{2,1,0:T(8,128)(2,1)}), bf16[16,128,128]{2,1,0:T(8,128)(2,1)S(1)}, u32[]{:S(2)}, u32[]{:S(2)}) async-start(bf16[16,128,128]{2,1,0:T(8,128)(2,1)} %get-tuple-element.20), calls=%async_computation.2 | async-start | bytes 1048576 | tf_op jit(solution)/shard_map/all_to_all | solution.py:565
  101.4 15.0 %collective-permute-start.2 = (f32[16,8,256]{2,1,0:T(8,128)S(1)}, f32[16,8,256]{2,1,0:T(8,128)S(1)}, u32[]{:S(2)}, u32[]{:S(2)}) collective-permute-start(f32[16,8,256]{2,1,0:T(8,128)S(1)} %get-tuple-element.21), channel_id=1, source_target_pairs={{0,1},{1,2},{2,3},{3,4},{4,5},{5,6},{6,7},{7,8},{8,9},{9,10},{10,1... | collective-permute-start | bytes 393224 | tf_op jit(solution)/shard_map/ppermute | solution.py:676
  103.6 12.8 %collective-permute-start.3 = (f32[16,8,256]{2,1,0:T(8,128)S(1)}, f32[16,8,256]{2,1,0:T(8,128)S(1)}, u32[]{:S(2)}, u32[]{:S(2)}) collective-permute-start(f32[16,8,256]{2,1,0:T(8,128)S(1)} %get-tuple-element.22), channel_id=1, source_target_pairs={{1,0},{2,1},{3,2},{4,3},{5,4},{6,5},{7,6},{8,7},{9,8},{10,9},{11,1... | collective-permute-start | bytes 393224 | tf_op jit(solution)/shard_map/ppermute | solution.py:677
  116.0 19.3 %copy-start = (f32[16,192,256]{2,1,0:T(8,128)S(1)}, f32[16,192,256]{2,1,0:T(8,128)}, u32[]{:S(2)}) copy-start(f32[16,192,256]{2,1,0:T(8,128)} %get-tuple-element.24.refs_1_) | copy-start | bytes 9437188

commit v3 on v2

--- a/solution.py
+++ b/solution.py
@@ -33,6 +33,12 @@
 def exact(a, b):
     return lax.dot_general(
         a, b, (((1,), (0,)), ((), ())), precision=lax.Precision.HIGHEST, preferred_element_type=F32
+    )
+
+
+def exact_t(a, b):
+    return lax.dot_general(
+        a, b, (((1,), (1,)), ((), ())), precision=lax.Precision.HIGHEST, preferred_element_type=F32
     )
 
 
@@ -122,9 +128,7 @@
     pool = np.zeros((CG, HALF), np.float32)
     for c in range(HALF):
         pool[c // 4, c] = 1
-    spread = np.zeros((blocks, CG, blocks, HALF), np.float32)
-    for a in range(blocks):
-        spread[a, :, a, :] = pool
+    none = np.zeros((CG, HALF), np.float32)
     return dict(
         sel_x=sel_x.reshape(blocks * 64, width),
         sel_s=sel_s.reshape(blocks * 128, width),
@@ -136,8 +140,7 @@
         eut=np.concatenate(list(np.swapaxes(eu, 1, 2)), 0),
         ef=ef,
         eft=ef.T,
-        pool=pool,
-        spread=spread.reshape(blocks * CG, blocks * HALF),
+        pool_both=np.concatenate([pool, none, none, pool], 0),
     )
 
 
@@ -184,52 +187,55 @@
     patches = jnp.concatenate(windows, axis=1).astype(BF)
     first_value, first_slope = gelu_both(nn(w1_ref[...], patches))
     yield
-    lane_h = lax.broadcasted_iota(jnp.int32, first_value.shape, 1) % CG
-    first_value = first_value.astype(BF).astype(F32)
-    hidden_by_col = (
-        moved(first_value, 4, lane_h, lambda x: x >= 4).astype(BF),
-        first_value.astype(BF),
-        moved(first_value, -4, lane_h, lambda x: x < CG - 4).astype(BF),
-    )
-    columns = jnp.concatenate(
-        [
-            hidden_by_col[col_tap][:, window * cells : (window + 1) * cells]
-            for window in range(3)
-            for col_tap in range(3)
-        ],
-        axis=0,
-    )
-    second_value, second_slope = gelu_both(nn(second_t_ref[...], columns))
+    hidden = first_value.astype(BF)
+    stacked = jnp.concatenate(
+        [hidden[:, window * cells : (window + 1) * cells] for window in range(3)], axis=0
+    )
+    taps = nn(second_t_ref[...], stacked)
+    lane_c = lax.broadcasted_iota(jnp.int32, (128, cells), 1) % CG
+    second_pre = (
+        taps[128:256]
+        + moved(taps[0:128], 4, lane_c, lambda x: x >= 4)
+        + moved(taps[256:384], -4, lane_c, lambda x: x < CG - 4)
+    )
+    second_value, second_slope = gelu_both(second_pre)
     yield
     feature = second_value.astype(BF)
     patches_s[place] = patches
-    columns_s[place] = columns
+    columns_s[place] = stacked
     first_slope_s[place] = first_slope
     second_slope_s[place] = second_slope
     feature_s[place] = feature
-    wide_s[place] = nn(feature, spread_ref[...]).astype(BF)
-
-
-def coarse_backward(blocks, d_project, project_ref, second_ref, store, place, grad_ref, fg_ref):
+    pairs = [feature[:, at * 128 : (at + 1) * 128] for at in range(blocks // 2)]
+    pairs = jnp.concatenate(pairs, axis=0) if blocks > 2 else pairs[0]
+    for parity in range(2):
+        wide = nn(pairs, spread_ref[parity * 128 : (parity + 1) * 128, :]).astype(BF)
+        for at in range(blocks // 2):
+            b = 2 * at + parity
+            wide_s[place, :, b * HALF : (b + 1) * HALF] = wide[at * 128 : (at + 1) * 128]
+
+
+def coarse_backward(blocks, d_project, project_ref, second_ref, store, place, dil_ref, pg_ref, fg_ref):
     patches_s, columns_s, first_slope_s, second_slope_s, feature_s, _ = store
     cells = blocks * CG
-    grad_ref[PROJECT_AT : PROJECT_AT + 128, :] += nn(feature_s[place], d_project)
-    d_feature = nt(project_ref[...], d_project).astype(BF).astype(F32)
-    d_second = (d_feature * second_slope_s[place]).astype(BF)
-    yield
-    grad_ref[0:1152, :] += nt(columns_s[place], d_second)
-    back = nn(second_ref[...], d_second)
+    pg_ref[...] += nt(feature_s[place], d_project)
+    d_feature = nn(project_ref[...], d_project).astype(BF).astype(F32)
+    d_second = (d_feature * second_slope_s[place]).astype(BF).astype(F32)
     yield
     lane_c = lax.broadcasted_iota(jnp.int32, (128, cells), 1) % CG
-    parts = []
-    for window in range(3):
-        at = window * 384
-        parts.append(
-            back[at + 128 : at + 256]
-            + moved(back[at : at + 128], -4, lane_c, lambda x: x < CG - 4)
-            + moved(back[at + 256 : at + 384], 4, lane_c, lambda x: x >= 4)
-        )
-    d_first = (jnp.concatenate(parts, axis=1) * first_slope_s[place]).astype(BF)
+    shifted = jnp.concatenate(
+        [
+            moved(d_second, -4, lane_c, lambda x: x < CG - 4),
+            d_second,
+            moved(d_second, 4, lane_c, lambda x: x >= 4),
+        ],
+        axis=0,
+    ).astype(BF)
+    dil_ref[...] += nt(columns_s[place], shifted)
+    back = nn(second_ref[...], shifted)
+    yield
+    d_first_hidden = jnp.concatenate([back[0:128], back[128:256], back[256:384]], axis=1)
+    d_first = (d_first_hidden * first_slope_s[place]).astype(BF)
     fg_ref[...] += nt(patches_s[place], d_first)
 
 
@@ -263,7 +269,6 @@
     eut_ref,
     ef_ref,
     eft_ref,
-    pool_ref,
     spread_ref,
     first_t_ref,
     second_t_ref,
@@ -278,7 +283,8 @@
     to_first_ref,
     own_ref,
     sent_ref,
-    grad_ref,
+    dil_ref,
+    pg_ref,
     w_ref,
     u_ref,
     ut_ref,
@@ -302,7 +308,7 @@
 
     def backward(place):
         return coarse_backward(
-            blocks, d_project_ref[...], project_ref, second_ref, store, place, grad_ref, fg_ref
+            blocks, d_project_ref[...], project_ref, second_ref, store, place, dil_ref, pg_ref, fg_ref
         )
 
     @pl.when(step == 0)
@@ -318,7 +324,8 @@
         gu_ref[...] = jnp.zeros_like(gu_ref)
         gd_ref[...] = jnp.zeros_like(gd_ref)
         fg_ref[...] = jnp.zeros_like(fg_ref)
-        grad_ref[...] = jnp.zeros_like(grad_ref)
+        dil_ref[...] = jnp.zeros_like(dil_ref)
+        pg_ref[...] = jnp.zeros_like(pg_ref)
         d_project_ref[...] = jnp.zeros_like(d_project_ref)
         for buffer in store:
             buffer[2] = jnp.zeros(buffer.shape[1:], buffer.dtype)
@@ -360,19 +367,28 @@
         value, slope = gelu_both(third)
         return x_taps, s_taps, value.astype(BF), (d_hidden * slope).astype(BF)
 
-    def leave(held):
-        x_taps, s_taps, hidden, d_third = held
+    def leave(b, held):
+        hidden = held[2]
         taps = nn(ut_ref[...], hidden)
         c0 = taps[0:64] + moved(taps[192:256], 1, lane64, not_first)
         c1 = taps[64:128] + moved(taps[128:192], -1, lane64, not_last)
-        gu_ref[...] += nt(s_taps, hidden)
-        both = nt(jnp.concatenate([x_taps, pool_ref[...]], axis=0), d_third)
-        gd_ref[...] += both[0:128]
-        per_row = both[128:192]
-        cells_sum = (per_row[:, 0:128] + per_row[:, 128:256]) + (
-            per_row[:, 256:384] + per_row[:, 384:512]
+        return [c0 * flux_scale, c1 * flux_scale]
+
+    def collect(even, odd):
+        s_taps = jnp.concatenate([even[1], odd[1]], axis=1)
+        hidden = jnp.concatenate([even[2], odd[2]], axis=1)
+        gu_ref[...] += nt(hidden, s_taps)
+        x_taps = jnp.concatenate(
+            [
+                jnp.concatenate([even[0], odd[0]], axis=1),
+                jnp.concatenate([spread_ref[0:128, :], spread_ref[128:256, :]], axis=1),
+            ],
+            axis=0,
         )
-        return [c0 * flux_scale, c1 * flux_scale], cells_sum
+        both = nt(jnp.concatenate([even[3], odd[3]], axis=1), x_taps)
+        gd_ref[...] += both[:, 0:128]
+        per_row = both[:, 128:256]
+        return (per_row[0:128] + per_row[128:256]) + (per_row[256:384] + per_row[384:512])
 
     combined = []
     pooled = []
@@ -389,16 +405,15 @@
             held[turn - 1] = middle(entered.pop(turn - 1))
         if turn >= 3:
             advance(ahead)
-        if turn - 2 >= 0:
-            pair, cells_sum = leave(held.pop(turn - 2))
-            combined += pair
-            pooled.append(cells_sum)
+        b = turn - 2
+        if b >= 0:
+            combined += leave(b, held[b])
+            if b % 2 == 1:
+                pooled.append(collect(held[b - 1], held[b]))
 
     out = jnp.concatenate(combined, axis=0)
-    out_high = out.astype(BF)
-    out_low = (out - out_high.astype(F32)).astype(BF)
     finish(ahead)
-    placed = nn(sel_o_ref[...], out_high) + nn(sel_o_ref[...], out_low)
+    placed = nn(sel_o_ref[...], out.astype(BF))
     main = pred_ref.shape[1]
     pred_ref[0] = placed[0:main]
     before_flux = placed[main + 8 : main + 16]
@@ -412,7 +427,7 @@
     chunk = GRAD_ROWS // peers
     sent_ref[step, chunk : chunk + 16, :] = flux_high
     sent_ref[step, chunk + 16 : chunk + 32, :] = (flux - flux_high.astype(F32)).astype(BF)
-    d_project_ref[...] = jnp.concatenate(pooled, axis=0).astype(BF)
+    d_project_ref[...] = jnp.concatenate(pooled, axis=1).astype(BF)
 
     @pl.when(step == pl.num_programs(0) - 1)
     def _():
@@ -421,13 +436,19 @@
         down = jnp.zeros((48, 128), F32)
         for r in range(4):
             lanes = slice(r * 128, (r + 1) * 128)
-            up = up + exact(eut_ref[r * 96 : (r + 1) * 96, :], gu_ref[:, lanes])
-            down = down + exact(ext_ref[r * 48 : (r + 1) * 48, :], gd_ref[:, lanes])
-        grad_ref[UP_AT : UP_AT + 96, :] = up
-        grad_ref[DOWN_AT : DOWN_AT + 48, :] = down
-        grad_ref[FIRST_AT : FIRST_AT + 32, :] = exact(eft_ref[...], fg_ref[...])
+            up = up + exact_t(eut_ref[r * 96 : (r + 1) * 96, :], gu_ref[lanes, :])
+            down = down + exact_t(ext_ref[r * 48 : (r + 1) * 48, :], gd_ref[lanes, :])
+        first = exact(eft_ref[...], fg_ref[...])
+        pieces = [
+            dil_ref[i * 128 : (i + 1) * 128, j * 128 : (j + 1) * 128]
+            for i in range(3)
+            for j in range(3)
+        ]
+        pieces += [pg_ref[...], up, down, first]
+        pieces.append(jnp.zeros((GRAD_ROWS - FIRST_AT - 32, 128), F32))
+        grads = jnp.concatenate(pieces, axis=0).astype(BF)
         for t in range(peers):
-            sent_ref[t, 0:chunk, :] = grad_ref[t * chunk : (t + 1) * chunk, :].astype(BF)
+            sent_ref[t, 0:chunk, :] = grads[t * chunk : (t + 1) * chunk, :]
 
 
 def run_slots(peers, ids, tile, coarse, fine, cot, before, after, later, fixed, weights):
@@ -466,17 +487,18 @@
         in_specs=in_specs,
         out_specs=[per_slot(a) for a in out_shape[:4]] + [whole(out_shape[4])],
         scratch_shapes=[
-            pltpu.VMEM((GRAD_ROWS, 128), F32),
+            pltpu.VMEM((384, 384), F32),
+            pltpu.VMEM((128, 128), F32),
             pltpu.VMEM((512, 256), BF),
             pltpu.VMEM((512, 256), BF),
             pltpu.VMEM((256, 512), BF),
             pltpu.VMEM((128, 80), BF),
-            pltpu.VMEM((256, 512), F32),
-            pltpu.VMEM((128, 512), F32),
+            pltpu.VMEM((512, 256), F32),
+            pltpu.VMEM((512, 128), F32),
             pltpu.VMEM((80, 128), F32),
-            pltpu.VMEM((cells, 128), BF),
+            pltpu.VMEM((128, cells), BF),
             pltpu.VMEM((3, 80, 3 * cells), BF),
-            pltpu.VMEM((3, 1152, cells), BF),
+            pltpu.VMEM((3, 384, cells), BF),
             pltpu.VMEM((3, 128, 3 * cells), F32),
             pltpu.VMEM((3, 128, cells), F32),
             pltpu.VMEM((3, 128, cells), BF),
@@ -642,15 +664,14 @@
         jnp.asarray(made["eut"], F32),
         jnp.asarray(made["ef"], BF),
         jnp.asarray(made["eft"], F32),
-        jnp.asarray(made["pool"], BF),
-        jnp.asarray(made["spread"], BF),
+        jnp.asarray(made["pool_both"], BF),
     ]
-    second = dilated_weight.reshape(1152, 128)
+    second = dilated_weight
     up_flat = up_weight.reshape(96, 128)
     weights = [
         jnp.pad(first_weight.reshape(27, 128), ((0, 5), (0, 0))).T,
-        second.T,
-        second,
+        jnp.transpose(second, (1, 3, 0, 2)).reshape(384, 384),
+        jnp.transpose(second, (0, 2, 1, 3)).reshape(384, 384),
         project_weight,
         project_weight.T,
         down_weight.reshape(48, 128).T,

time: 139 us -> 138 us (level)
  Pallas kernels: 62 us -> 59.5 us
    pallas_call x1, Pallas kernels: 59.9 us -> 57.4 us  [run_slots(): pl.pallas_call(body, grid_spec=grid_spec, out_shape=out_shape, compiler_p...]
  transfers between devices with their start and end apart: 7 -> 7, of which waited for: 3 -> 3; matrix products, arithmetic and copies ran while one was open for 5% -> 6% of each run, Pallas kernels for 0% -> 0%
where the time goes in v3:
time: 138 us; the launch traced here: 137 us
  Pallas kernels  59.5 us (43%)
  starting transfers between devices  23.6 us (17%)
  waiting for transfers between devices  19.5 us (14%)
  blocking collectives  18.7 us (14%)
  local copies, waits for them, and re-layouts  8.79 us (6%)
  other arithmetic  5.84 us (4%)
  between operations  1.39 us (1%)
    pallas_call x1, Pallas kernels, run_slots(): pl.pallas_call(body, grid_spec=grid_spec, out_shape=out_shape, compiler_p...  57.4 us
    all_to_all x3, waiting for transfers between devices, exchanged(): lax.all_to_all(value, 'tile', split_axis=0, concat_axis=0, tiled=True)  19.5 us
    all_to_all x1, blocking collectives, exchanged(): lax.all_to_all(value, 'tile', split_axis=0, concat_axis=0, tiled=True)  18.7 us
    all_to_all x3, starting transfers between devices, exchanged(): lax.all_to_all(value, 'tile', split_axis=0, concat_axis=0, tiled=True)  15.8 us
    ppermute x1, starting transfers between devices, local(): from_before = lax.ppermute(edge_last, 'tile', up)  3.04 us
  transfers between devices with their start and end apart: 7, of which 3 were waited for; matrix products, arithmetic and copies ran while one was open for 6% of the time, Pallas kernels for 0%

profile of v3, /device:TPU:0, one launch (start us, length us, event | category | flops | bytes accessed | tf_op | source)
XLA Modules:
  0.0 137.3 jit_solution(12220976494385928020)
XLA Ops:
  0.6 0.7 convert_bitcast_fusion
  1.4 0.7 convert_element_type.27
  2.4 2.0 %convert_reduce_fusion = f32[16,3,2,256]{3,2,1,0:T(2,128)S(1)} fusion(bf16[16,3,2,2,16,256]{5,4,3,2,1,0:T(8,128)(2,1)} %param.24), kind=kLoop, calls=%fused_computation | loop fusion | flops 1548288 | bytes 1671168 | tf_op jit(solution)/shard_map/reduce_sum | solution.py:609
  4.7 0.3 stack.67
  5.1 0.9 all_to_all.20
  6.0 7.4 %all-to-all-start = ((f32[16,1,5120]{2,1,0:T(1,128)}), f32[16,1,5120]{2,1,0:T(1,128)S(1)}, u32[]{:S(2)}, u32[]{:S(2)}) async-start(f32[16,1,5120]{2,1,0:T(1,128)} %all_to_all.20), calls=%async_computation | async-start | bytes 655360 | tf_op jit(solution)/shard_map/all_to_all | solution.py:587
  13.4 1.3 fusion.30
  14.7 1.3 fusion.29
  16.3 0.1 maximum_maximum_fusion.1
  16.4 1.3 collective-permute-start.1
  17.7 3.0 %collective-permute-start = (bf16[16,16,256]{2,1,0:T(8,128)(2,1)S(1)}, bf16[16,16,256]{2,1,0:T(8,128)(2,1)S(1)}, u32[]{:S(2)}, u32[]{:S(2)}) collective-permute-start(bf16[16,16,256]{2,1,0:T(8,128)(2,1)S(1)} %get-tuple-element.87), channel_id=1, source_target_pairs={{0,1},{1,2},{2,3},{3,4},{4,5},{5,6},{6,7},{7,8},{8,9},{9,10},{10,1... | collective-permute-start | bytes 393224 | tf_op jit(solution)/shard_map/ppermute | solution.py:650
  20.8 0.2 copy.98
  21.1 0.3 copy.99
  21.4 0.9 copy_bitcast_fusion.1
  22.4 2.2 %all-to-all-done = f32[16,1,5120]{2,1,0:T(1,128)S(1)} async-done(((f32[16,1,5120]{2,1,0:T(1,128)}), f32[16,1,5120]{2,1,0:T(1,128)S(1)}, u32[]{:S(2)}, u32[]{:S(2)}) %all-to-all-start) | async-done | bytes 327712 | tf_op jit(solution)/shard_map/all_to_all | solution.py:587
  24.6 0.5 select_reduce_fusion.1
  25.2 0.8 copy.96
  25.9 4.8 %all-to-all-start.1 = ((f32[16,1,2048]{2,1,0:T(1,128)}), f32[16,1,2048]{2,1,0:T(1,128)S(1)}, u32[]{:S(2)}, u32[]{:S(2)}) async-start(f32[16,1,2048]{2,1,0:T(1,128)} %copy.96), calls=%async_computation.1 | async-start | bytes 262144 | tf_op jit(solution)/shard_map/all_to_all | solution.py:587
  30.8 0.7 broadcast_select_fusion.refs_10_
  32.1 0.1 reshape.120.refs_2_.refs_3_
  32.3 6.4 %all-to-all-done.1 = f32[16,1,2048]{2,1,0:T(1,128)S(1)} async-done(((f32[16,1,2048]{2,1,0:T(1,128)}), f32[16,1,2048]{2,1,0:T(1,128)S(1)}, u32[]{:S(2)}, u32[]{:S(2)}) %all-to-all-start.1) | async-done | bytes 131104 | tf_op jit(solution)/shard_map/all_to_all | solution.py:587
  38.7 0.3 reduce
  39.2 57.4 %shard_map.244 = (f32[16,192,256]{2,1,0:T(8,128)}, f32[16,8,256]{2,1,0:T(8,128)S(1)}, f32[16,8,256]{2,1,0:T(8,128)S(1)}, f32[16,8,256]{2,1,0:T(8,128)S(1)}, bf16[16,128,128]{2,1,0:T(8,128)(2,1)}) custom-call(s32[16]{0:T(128)S(1)} %copy-done.2, s32[1]{0:T(128)} %bitcast.refs_1_, f32[16,3,1024]{2,1,0:T(4,128)S(1)} %reshape.120.refs_2_.refs_3_, ...), custom_call_target="tpu_custom_call" | custom-call | flops 32000000000 | bytes 16000000 | tf_op jit(solution)/shard_map/pallas_call | solution.py:512
  96.6 3.6 %all-to-all-start.2 = ((bf16[16,128,128]{2,1,0:T(8,128)(2,1)}), bf16[16,128,128]{2,1,0:T(8,128)(2,1)S(1)}, u32[]{:S(2)}, u32[]{:S(2)}) async-start(bf16[16,128,128]{2,1,0:T(8,128)(2,1)} %get-tuple-element.20), calls=%async_computation.2 | async-start | bytes 1048576 | tf_op jit(solution)/shard_map/all_to_all | solution.py:587
  100.2 2.2 %collective-permute-start.2 = (f32[16,8,256]{2,1,0:T(8,128)S(1)}, f32[16,8,256]{2,1,0:T(8,128)S(1)}, u32[]{:S(2)}, u32[]{:S(2)}) collective-permute-start(f32[16,8,256]{2,1,0:T(8,128)S(1)} %get-tuple-element.21), channel_id=1, source_target_pairs={{0,1},{1,2},{2,3},{3,4},{4,5},{5,6},{6,7},{7,8},{8,9},{9,10},{10,1... | collective-permute-start | bytes 393224 | tf_op jit(solution)/shard_map/ppermute | solution.py:697
  102.4 1.3 collective-permute-start.3
  103.7 10.9 %all-to-all-done.2 = bf16[16,128,128]{2,1,0:T(8,128)(2,1)S(1)} async-done(((bf16[16,128,128]{2,1,0:T(8,128)(2,1)}), bf16[16,128,128]{2,1,0:T(8,128)(2,1)S(1)}, u32[]{:S(2)}, u32[]{:S(2)}) %all-to-all-start.2) | async-done | bytes 524320 | tf_op jit(solution)/shard_map/all_to_all | solution.py:587
  114.7 0.3 select_reduce_fusion
  115.3 18.7 %all_to_all.31.refs_0_ = bf16[16,128,128]{2,1,0:T(8,128)(2,1)S(1)} all-to-all(bf16[16,128,128]{2,1,0:T(8,128)(2,1)S(1)} %pad_maximum_fusion), channel_id=1, replica_groups=mesh['groups'=2,'tile'=16] {'tile'}, dimensions={0} | all-to-all | bytes 1048576 | tf_op jit(solution)/shard_map/all_to_all | solution.py:587
  134.0 2.1 %shard_map.245 = (bf16[16,192,256]{2,1,0:T(8,128)(2,1)}, f32[1152,128]{1,0:T(8,128)}, f32[128,128]{1,0:T(8,128)}, f32[96,128]{1,0:T(8,128)S(1)}, f32[48,128]{1,0:T(8,128)}, /*index=5*/f32[32,128]{1,0:T(8,128)S(1)}) custom-call(bf16[16,128,128]{2,1,0:T(8,128)(2,1)S(1)} %all_to_all.31.refs_0_, f32[16,192,256]{2,1,0:T(8,128)S(1)} %copy-done, ...), custom_call_target="tpu_custom_call" | custom-call | tf_op jit(solution)/shard_map/pallas_call | solution.py:573
  136.1 0.6 reshape.130
  136.7 0.6 copy.104
  (92 shorter events, 1.7 us)
Async XLA Ops:
  5.0 15.7 %copy-start.10 = (bf16[3,3,128,128]{3,2,1,0:T(8,128)(2,1)S(1)}, bf16[3,3,128,128]{3,2,1,0:T(8,128)(2,1)}, u32[]{:S(2)}) copy-start(bf16[3,3,128,128]{3,2,1,0:T(8,128)(2,1)} %param.27) | copy-start | bytes 884740
  6.0 18.5 %all-to-all-start = ((f32[16,1,5120]{2,1,0:T(1,128)}), f32[16,1,5120]{2,1,0:T(1,128)S(1)}, u32[]{:S(2)}, u32[]{:S(2)}) async-start(f32[16,1,5120]{2,1,0:T(1,128)} %all_to_all.20), calls=%async_computation | async-start | bytes 655360 | tf_op jit(solution)/shard_map/all_to_all | solution.py:587
  16.4 22.7 %collective-permute-start.1 = (bf16[16,16,256]{2,1,0:T(8,128)(2,1)S(1)}, bf16[16,16,256]{2,1,0:T(8,128)(2,1)S(1)}, u32[]{:S(2)}, u32[]{:S(2)}) collective-permute-start(bf16[16,16,256]{2,1,0:T(8,128)(2,1)S(1)} %get-tuple-element.86), channel_id=1, source_target_pairs={{1,0},{2,1},{3,2},{4,3},{5,4},{6,5},{7,6},{8,7},{9,8},{10,9},{11,1... | collective-permute-start | bytes 393224 | tf_op jit(solution)/shard_map/ppermute | solution.py:651
  17.7 21.4 %collective-permute-start = (bf16[16,16,256]{2,1,0:T(8,128)(2,1)S(1)}, bf16[16,16,256]{2,1,0:T(8,128)(2,1)S(1)}, u32[]{:S(2)}, u32[]{:S(2)}) collective-permute-start(bf16[16,16,256]{2,1,0:T(8,128)(2,1)S(1)} %get-tuple-element.87), channel_id=1, source_target_pairs={{0,1},{1,2},{2,3},{3,4},{4,5},{5,6},{6,7},{7,8},{8,9},{9,10},{10,1... | collective-permute-start | bytes 393224 | tf_op jit(solution)/shard_map/ppermute | solution.py:650
  20.8 10.0 %copy-start.11 = (bf16[512,240]{1,0:T(8,128)(2,1)S(1)}, bf16[512,240]{1,0:T(8,128)(2,1)}, u32[]{:S(2)}) copy-start(bf16[512,240]{1,0:T(8,128)(2,1)} %constant.35.clone) | copy-start | bytes 737284
  20.8 10.0 %copy-start.12 = (bf16[512,240]{1,0:T(8,128)(2,1)S(1)}, bf16[512,240]{1,0:T(8,128)(2,1)}, u32[]{:S(2)}) copy-start(bf16[512,240]{1,0:T(8,128)(2,1)} %constant.34.clone) | copy-start | bytes 737284
  21.3 10.2 %copy-start.15 = (bf16[3,3,3,128]{3,2,1,0:T(4,128)(2,1)S(1)}, bf16[3,3,3,128]{3,2,1,0:T(4,128)(2,1)}, u32[]{:S(2)}) copy-start(bf16[3,3,3,128]{3,2,1,0:T(4,128)(2,1)} %param.26) | copy-start | bytes 20740
  21.3 10.3 %copy-start.14 = (bf16[3,4,4,128]{3,2,1,0:T(4,128)(2,1)S(1)}, bf16[3,4,4,128]{3,2,1,0:T(4,128)(2,1)}, u32[]{:S(2)}) copy-start(bf16[3,4,4,128]{3,2,1,0:T(4,128)(2,1)} %param.29) | copy-start | bytes 36868
  21.4 10.4 %copy-start.13 = (bf16[4,4,6,128]{3,1,2,0:T(4,128)(2,1)S(1)}, bf16[4,4,6,128]{3,1,2,0:T(4,128)(2,1)}, u32[]{:S(2)}) copy-start(bf16[4,4,6,128]{3,1,2,0:T(4,128)(2,1)} %param.30) | copy-start | bytes 73732
  21.4 10.6 %copy-start.1 = (bf16[128,128]{1,0:T(8,128)(2,1)S(1)}, bf16[128,128]{1,0:T(8,128)(2,1)}, u32[]{:S(2)}) copy-start(bf16[128,128]{1,0:T(8,128)(2,1)} %refs_22_.1) | copy-start | bytes 98308
  22.3 16.8 %copy-start.2 = (s32[16]{0:T(128)S(1)}, s32[16]{0:T(128)}, u32[]{:S(2)}) copy-start(s32[16]{0:T(128)} %refs_0_.1) | copy-start | bytes 196
  22.3 16.8 %copy-start.3 = (bf16[224,512]{1,0:T(8,128)(2,1)S(1)}, bf16[224,512]{1,0:T(8,128)(2,1)}, u32[]{:S(2)}) copy-start(bf16[224,512]{1,0:T(8,128)(2,1)} %constant.37.clone.refs_11_) | copy-start | bytes 688132
  22.3 16.8 %copy-start.4 = (bf16[256,256]{1,0:T(8,128)(2,1)S(1)}, bf16[256,256]{1,0:T(8,128)(2,1)}, u32[]{:S(2)}) copy-start(bf16[256,256]{1,0:T(8,128)(2,1)} %constant.44.clone.refs_18_) | copy-start | bytes 393220
  22.3 16.8 %copy-start.5 = (bf16[512,48]{1,0:T(8,128)(2,1)S(1)}, bf16[512,48]{1,0:T(8,128)(2,1)}, u32[]{:S(2)}) copy-start(bf16[512,48]{1,0:T(8,128)(2,1)} %constant.38.clone.refs_12_) | copy-start | bytes 147460
  22.3 16.8 %copy-start.6 = (bf16[256,240]{1,0:T(8,128)(2,1)S(1)}, bf16[256,240]{1,0:T(8,128)(2,1)}, u32[]{:S(2)}) copy-start(bf16[256,240]{1,0:T(8,128)(2,1)} %constant.36.clone.refs_9_) | copy-start | bytes 368644
  22.3 16.8 %copy-start.7 = (f32[192,128]{1,0:T(8,128)S(1)}, f32[192,128]{1,0:T(8,128)}, u32[]{:S(2)}) copy-start(f32[192,128]{1,0:T(8,128)} %constant.40.clone.refs_14_) | copy-start | bytes 294916
  22.3 16.8 %copy-start.8 = (bf16[80,32]{1,0:T(8,128)(2,1)S(1)}, bf16[80,32]{1,0:T(8,128)(2,1)}, u32[]{:S(2)}) copy-start(bf16[80,32]{1,0:T(8,128)(2,1)} %constant.42.clone.refs_16_) | copy-start | bytes 15364
  22.3 16.8 %copy-start.9 = (f32[32,80]{1,0:T(8,128)S(1)}, f32[32,80]{1,0:T(8,128)}, u32[]{:S(2)}) copy-start(f32[32,80]{1,0:T(8,128)} %constant.43.clone.refs_17_) | copy-start | bytes 30724
  25.9 12.8 %all-to-all-start.1 = ((f32[16,1,2048]{2,1,0:T(1,128)}), f32[16,1,2048]{2,1,0:T(1,128)S(1)}, u32[]{:S(2)}, u32[]{:S(2)}) async-start(f32[16,1,2048]{2,1,0:T(1,128)} %copy.96), calls=%async_computation.1 | async-start | bytes 262144 | tf_op jit(solution)/shard_map/all_to_all | solution.py:587
  96.6 18.0 %all-to-all-start.2 = ((bf16[16,128,128]{2,1,0:T(8,128)(2,1)}), bf16[16,128,128]{2,1,0:T(8,128)(2,1)S(1)}, u32[]{:S(2)}, u32[]{:S(2)}) async-start(bf16[16,128,128]{2,1,0:T(8,128)(2,1)} %get-tuple-element.20), calls=%async_computation.2 | async-start | bytes 1048576 | tf_op jit(solution)/shard_map/all_to_all | solution.py:587
  100.2 15.0 %collective-permute-start.2 = (f32[16,8,256]{2,1,0:T(8,128)S(1)}, f32[16,8,256]{2,1,0:T(8,128)S(1)}, u32[]{:S(2)}, u32[]{:S(2)}) collective-permute-start(f32[16,8,256]{2,1,0:T(8,128)S(1)} %get-tuple-element.21), channel_id=1, source_target_pairs={{0,1},{1,2},{2,3},{3,4},{4,5},{5,6},{6,7},{7,8},{8,9},{9,10},{10,1... | collective-permute-start | bytes 393224 | tf_op jit(solution)/shard_map/ppermute | solution.py:697
  102.4 12.8 %collective-permute-start.3 = (f32[16,8,256]{2,1,0:T(8,128)S(1)}, f32[16,8,256]{2,1,0:T(8,128)S(1)}, u32[]{:S(2)}, u32[]{:S(2)}) collective-permute-start(f32[16,8,256]{2,1,0:T(8,128)S(1)} %get-tuple-element.22), channel_id=1, source_target_pairs={{1,0},{2,1},{3,2},{4,3},{5,4},{6,5},{7,6},{8,7},{9,8},{10,9},{11,1... | collective-permute-start | bytes 393224 | tf_op jit(solution)/shard_map/ppermute | solution.py:698
  114.7 19.3 %copy-start = (f32[16,192,256]{2,1,0:T(8,128)S(1)}, f32[16,192,256]{2,1,0:T(8,128)}, u32[]{:S(2)}) copy-start(f32[16,192,256]{2,1,0:T(8,128)} %get-tuple-element.24.refs_1_) | copy-start | bytes 9437188

commit v4 on v3

--- a/solution.py
+++ b/solution.py
@@ -18,6 +18,9 @@
 F32 = jnp.float32
 
 AUX = 48
+SENT_INPUT = 64
+SENT_EARLY = SENT_INPUT + 32
+PER_STEP = 2
 GRAD_ROWS = 1536
 UP_AT, DOWN_AT, FIRST_AT, PROJECT_AT = 1280, 1376, 1424, 1152
 
@@ -107,10 +110,16 @@
                         sel_o[base + 24 + ch * 2 + q, b, q, 32 + at] = 1
                     if o == last:
                         sel_o[base + 16 + ch * 2 + q, b, q, at] = 1
-    sel_s_first = sel_s.copy()
-    for q in range(2):
-        for ch in range(3):
-            sel_s_first[0, q, 32 + ch * 10 + 8] = 0
+    early_x = np.zeros((48, 12 * rows), np.float32)
+    early_s = np.zeros((48, 12 * rows), np.float32)
+    for ch in range(3):
+        for q in range(2):
+            at = ch * 2 + q
+            for o in range(last):
+                early_s[at, held(ch, q, o)] = 1
+            for start, o in ((16, last - 1), (32, 0)):
+                early_x[start + at, held(ch, q, o)] = 1
+                early_s[start + 6 + at, held(ch, q, o)] = 1
     ex = np.zeros((4, 128, 48), np.float32)
     eu = np.zeros((4, 256, 96), np.float32)
     for r in range(4):
@@ -132,7 +141,8 @@
     return dict(
         sel_x=sel_x.reshape(blocks * 64, width),
         sel_s=sel_s.reshape(blocks * 128, width),
-        sel_s_first=sel_s_first.reshape(blocks * 128, width),
+        early_x=early_x,
+        early_s=early_s,
         sel_o=sel_o.reshape(12 * rows + 32, blocks * 128),
         ex=ex.reshape(512, 48),
         eu=eu.reshape(1024, 96),
@@ -161,7 +171,10 @@
 def coarse_forward(blocks, tile, coarse_ref, w1_ref, second_t_ref, spread_ref, store, place):
     patches_s, columns_s, first_slope_s, second_slope_s, feature_s, wide_s = store
     cells = blocks * CG
-    inputs = jnp.concatenate([coarse_ref[0], jnp.zeros((5, coarse_ref.shape[2]), F32)], axis=0)
+    by_segment = coarse_ref[0, 0:SENT_INPUT, :].astype(F32)
+    inputs = jnp.concatenate(
+        [by_segment[at : at + 8] for at in range(0, SENT_INPUT, 8)], axis=1
+    )
     lane_in = lax.broadcasted_iota(jnp.int32, inputs.shape, 1) % CG
     by_col = (
         moved(inputs, 2, lane_in, lambda x: x >= 2),
@@ -254,7 +267,8 @@
     ids_ref,
     tile_ref,
     coarse_first_ref,
-    coarse_ref,
+    coarse_a_ref,
+    coarse_b_ref,
     fine_ref,
     cot_ref,
     before_ref,
@@ -297,9 +311,7 @@
 ):
     step = pl.program_id(0)
     tile = tile_ref[0]
-    now = lax.rem(step, 3)
-    soon = lax.rem(step + 1, 3)
-    done = lax.rem(step + 2, 3)
+    chunk = GRAD_ROWS // peers
 
     def forward(source, place):
         return coarse_forward(
@@ -331,107 +343,113 @@
             buffer[2] = jnp.zeros(buffer.shape[1:], buffer.dtype)
         finish(forward(coarse_first_ref, 0))
 
-    back = backward(done)
-    ahead = forward(coarse_ref, soon)
-    advance(back)
-    later = later_ref[0]
-    later_high = later.astype(BF).astype(F32)
-    later_both = jnp.concatenate([later_high, later - later_high], axis=0).astype(BF)
-    aux = [before_ref[0], after_ref[0], later_both]
-    fine_all = nn(sel_x_ref[...], jnp.concatenate([fine_ref[0]] + aux, axis=0))
-    slope_all = nn(sel_s_ref[...], jnp.concatenate([cot_ref[0]] + aux, axis=0))
-    row = lax.broadcasted_iota(jnp.int32, (64, HALF), 0)
-    flux_scale = jnp.where(row >= 32, SCALE, 1.0)
-    lane32 = lax.broadcasted_iota(jnp.int32, (32, HALF), 1)
-    lane64 = lax.broadcasted_iota(jnp.int32, (64, HALF), 1)
-    not_first = lambda x: x >= 1
-    not_last = lambda x: x < HALF - 1
-
-    def enter(b):
-        x0 = fine_all[b * 64 : b * 64 + 32]
-        x1 = fine_all[b * 64 + 32 : b * 64 + 64]
-        x_taps = jnp.concatenate(
-            [x0, x1, moved(x1, 1, lane32, not_first), moved(x0, -1, lane32, not_last)], axis=0
-        ).astype(BF)
-        s0 = slope_all[b * 128 : b * 128 + 64] * flux_scale
-        s1 = slope_all[b * 128 + 64 : b * 128 + 128] * flux_scale
-        s_taps = jnp.concatenate(
-            [s0, s1, moved(s1, 1, lane64, not_first), moved(s0, -1, lane64, not_last)], axis=0
-        ).astype(BF)
-        wide = store[5][now, :, b * HALF : (b + 1) * HALF]
-        third = nn(w_ref[...], jnp.concatenate([x_taps, wide], axis=0))
-        return x_taps, s_taps, third, nn(u_ref[...], s_taps)
-
-    def middle(entered):
-        x_taps, s_taps, third, d_hidden = entered
-        value, slope = gelu_both(third)
-        return x_taps, s_taps, value.astype(BF), (d_hidden * slope).astype(BF)
-
-    def leave(b, held):
-        hidden = held[2]
-        taps = nn(ut_ref[...], hidden)
-        c0 = taps[0:64] + moved(taps[192:256], 1, lane64, not_first)
-        c1 = taps[64:128] + moved(taps[128:192], -1, lane64, not_last)
-        return [c0 * flux_scale, c1 * flux_scale]
-
-    def collect(even, odd):
-        s_taps = jnp.concatenate([even[1], odd[1]], axis=1)
-        hidden = jnp.concatenate([even[2], odd[2]], axis=1)
-        gu_ref[...] += nt(hidden, s_taps)
-        x_taps = jnp.concatenate(
-            [
-                jnp.concatenate([even[0], odd[0]], axis=1),
-                jnp.concatenate([spread_ref[0:128, :], spread_ref[128:256, :]], axis=1),
-            ],
-            axis=0,
-        )
-        both = nt(jnp.concatenate([even[3], odd[3]], axis=1), x_taps)
-        gd_ref[...] += both[:, 0:128]
-        per_row = both[:, 128:256]
-        return (per_row[0:128] + per_row[128:256]) + (per_row[256:384] + per_row[384:512])
-
-    combined = []
-    pooled = []
-    entered = {}
-    held = {}
-    for turn in range(blocks + 2):
-        if turn < blocks:
-            entered[turn] = enter(turn)
-        if turn == 1:
-            advance(back)
-        if turn == 2:
-            finish(back)
-        if 0 <= turn - 1 < blocks:
-            held[turn - 1] = middle(entered.pop(turn - 1))
-        if turn >= 3:
-            advance(ahead)
-        b = turn - 2
-        if b >= 0:
-            combined += leave(b, held[b])
-            if b % 2 == 1:
-                pooled.append(collect(held[b - 1], held[b]))
-
-    out = jnp.concatenate(combined, axis=0)
-    finish(ahead)
-    placed = nn(sel_o_ref[...], out.astype(BF))
-    main = pred_ref.shape[1]
-    pred_ref[0] = placed[0:main]
-    before_flux = placed[main + 8 : main + 16]
-    own = before_flux * jnp.where(tile >= 1, 1.0, 0.0)
-    flux = placed[main + 24 : main + 32] + own
-    to_last_ref[0] = placed[main : main + 8] + before_flux
-    to_first_ref[0] = placed[main + 16 : main + 24]
-    own_ref[0] = own
-    flux = jnp.concatenate([flux[:, 0:128], flux[:, 128:256]], axis=0)
-    flux_high = flux.astype(BF)
-    chunk = GRAD_ROWS // peers
-    sent_ref[step, chunk : chunk + 16, :] = flux_high
-    sent_ref[step, chunk + 16 : chunk + 32, :] = (flux - flux_high.astype(F32)).astype(BF)
-    d_project_ref[...] = jnp.concatenate(pooled, axis=1).astype(BF)
+    def one_slot(u, slot, now, soon, done):
+        back = backward(done)
+        ahead = forward((coarse_a_ref, coarse_b_ref)[u], soon)
+        advance(back)
+        later = jnp.concatenate([later_ref[u, 0:8, :], later_ref[u, 8:16, :]], axis=1)
+        later_high = later.astype(BF).astype(F32)
+        later_both = jnp.concatenate([later_high, later - later_high], axis=0).astype(BF)
+        aux = [before_ref[u], after_ref[u], later_both]
+        fine_all = nn(sel_x_ref[...], jnp.concatenate([fine_ref[u]] + aux, axis=0))
+        slope_all = nn(sel_s_ref[...], jnp.concatenate([cot_ref[u]] + aux, axis=0))
+        row = lax.broadcasted_iota(jnp.int32, (64, HALF), 0)
+        flux_scale = jnp.where(row >= 32, SCALE, 1.0)
+        outside = (row == 40) | (row == 50) | (row == 60)
+        top_scale = jnp.where(outside & (tile == 0), 0.0, flux_scale)
+        lane32 = lax.broadcasted_iota(jnp.int32, (32, HALF), 1)
+        lane64 = lax.broadcasted_iota(jnp.int32, (64, HALF), 1)
+        not_first = lambda x: x >= 1
+        not_last = lambda x: x < HALF - 1
+
+        def enter(b):
+            x0 = fine_all[b * 64 : b * 64 + 32]
+            x1 = fine_all[b * 64 + 32 : b * 64 + 64]
+            x_taps = jnp.concatenate(
+                [x0, x1, moved(x1, 1, lane32, not_first), moved(x0, -1, lane32, not_last)], axis=0
+            ).astype(BF)
+            scale = top_scale if b == 0 else flux_scale
+            s0 = slope_all[b * 128 : b * 128 + 64] * scale
+            s1 = slope_all[b * 128 + 64 : b * 128 + 128] * scale
+            s_taps = jnp.concatenate(
+                [s0, s1, moved(s1, 1, lane64, not_first), moved(s0, -1, lane64, not_last)], axis=0
+            ).astype(BF)
+            wide = store[5][now, :, b * HALF : (b + 1) * HALF]
+            third = nn(w_ref[...], jnp.concatenate([x_taps, wide], axis=0))
+            return x_taps, s_taps, third, nn(u_ref[...], s_taps)
+
+        def middle(entered):
+            x_taps, s_taps, third, d_hidden = entered
+            value, slope = gelu_both(third)
+            return x_taps, s_taps, value.astype(BF), (d_hidden * slope).astype(BF)
+
+        def leave(b, held):
+            hidden = held[2]
+            taps = nn(ut_ref[...], hidden)
+            c0 = taps[0:64] + moved(taps[192:256], 1, lane64, not_first)
+            c1 = taps[64:128] + moved(taps[128:192], -1, lane64, not_last)
+            return [c0 * flux_scale, c1 * flux_scale]
+
+        def collect(even, odd):
+            s_taps = jnp.concatenate([even[1], odd[1]], axis=1)
+            hidden = jnp.concatenate([even[2], odd[2]], axis=1)
+            gu_ref[...] += nt(hidden, s_taps)
+            x_taps = jnp.concatenate(
+                [
+                    jnp.concatenate([even[0], odd[0]], axis=1),
+                    jnp.concatenate([spread_ref[0:128, :], spread_ref[128:256, :]], axis=1),
+                ],
+                axis=0,
+            )
+            both = nt(jnp.concatenate([even[3], odd[3]], axis=1), x_taps)
+            gd_ref[...] += both[:, 0:128]
+            per_row = both[:, 128:256]
+            return (per_row[0:128] + per_row[128:256]) + (per_row[256:384] + per_row[384:512])
+
+        combined = []
+        pooled = []
+        entered = {}
+        held = {}
+        for turn in range(blocks + 2):
+            if turn < blocks:
+                entered[turn] = enter(turn)
+            if turn == 1:
+                advance(back)
+            if turn == 2:
+                finish(back)
+            if 0 <= turn - 1 < blocks:
+                held[turn - 1] = middle(entered.pop(turn - 1))
+            if turn >= 3:
+                advance(ahead)
+            b = turn - 2
+            if b >= 0:
+                combined += leave(b, held[b])
+                if b % 2 == 1:
+                    pooled.append(collect(held[b - 1], held[b]))
+
+        out = jnp.concatenate(combined, axis=0)
+        finish(ahead)
+        placed = nn(sel_o_ref[...], out.astype(BF))
+        main = pred_ref.shape[1]
+        pred_ref[u] = placed[0:main]
+        before_flux = placed[main + 8 : main + 16]
+        own = before_flux * jnp.where(tile >= 1, 1.0, 0.0)
+        flux = placed[main + 24 : main + 32] + own
+        to_last_ref[u] = placed[main : main + 8] + before_flux
+        to_first_ref[u] = placed[main + 16 : main + 24]
+        own_ref[u] = own
+        flux = jnp.concatenate([flux[:, 0:128], flux[:, 128:256]], axis=0)
+        sent_ref[slot, chunk : chunk + 16, :] = flux.astype(BF)
+        d_project_ref[...] = jnp.concatenate(pooled, axis=1).astype(BF)
+
+    for u in range(PER_STEP):
+        slot = step * PER_STEP + u
+        now = lax.rem(slot, 3)
+        one_slot(u, slot, now, lax.rem(slot + 1, 3), lax.rem(slot + 2, 3))
 
     @pl.when(step == pl.num_programs(0) - 1)
     def _():
-        finish(backward(now))
+        finish(backward((pl.num_programs(0) * PER_STEP - 1) % 3))
         up = jnp.zeros((96, 128), F32)
         down = jnp.zeros((48, 128), F32)
         for r in range(4):
@@ -457,16 +475,22 @@
     cells = blocks * CG
     chunk = GRAD_ROWS // peers
 
+    def coarse_of(ahead):
+        return pl.BlockSpec(
+            one, lambda n, ids, tile: (ids[jnp.minimum(n * PER_STEP + ahead, slots - 1)], 0, 0)
+        )
+
     def whole(array):
         return pl.BlockSpec(array.shape, lambda n, ids, tile: (0,) * array.ndim)
 
     def per_slot(array):
-        return pl.BlockSpec((1,) + array.shape[1:], lambda n, ids, tile: (n, 0, 0))
+        return pl.BlockSpec((PER_STEP,) + array.shape[1:], lambda n, ids, tile: (n, 0, 0))
 
     one = (1,) + coarse.shape[1:]
     in_specs = [
         pl.BlockSpec(one, lambda n, ids, tile: (ids[0], 0, 0)),
-        pl.BlockSpec(one, lambda n, ids, tile: (ids[jnp.minimum(n + 1, slots - 1)], 0, 0)),
+        coarse_of(1),
+        coarse_of(2),
         per_slot(fine),
         per_slot(cot),
         per_slot(before),
@@ -479,11 +503,11 @@
         edge,
         edge,
         edge,
-        jax.ShapeDtypeStruct((peers, chunk + 32, 128), BF),
+        jax.ShapeDtypeStruct((peers, chunk + 16, 128), BF),
     ]
     grid_spec = pltpu.PrefetchScalarGridSpec(
         num_scalar_prefetch=2,
-        grid=(slots,),
+        grid=(slots // PER_STEP,),
         in_specs=in_specs,
         out_specs=[per_slot(a) for a in out_shape[:4]] + [whole(out_shape[4])],
         scratch_shapes=[
@@ -517,7 +541,75 @@
         cost_estimate=pl.CostEstimate(
             flops=slots * blocks * 500_000_000, bytes_accessed=16_000_000, transcendentals=0
         ),
-    )(ids, tile, coarse, coarse, fine, cot, before, after, later, *fixed, *weights)
+    )(ids, tile, coarse, coarse, coarse, fine, cot, before, after, later, *fixed, *weights)
+
+
+EARLY_SLOTS = 4
+
+
+def early_kernel(
+    blocks, peers, solution_ref, geometry_ref, fine_ref, cot_ref, x_ref, s_ref, sent_ref, last_ref, first_ref
+):
+    step = pl.program_id(0)
+
+    @pl.when(step == 0)
+    def _():
+        inputs = jnp.concatenate(
+            [
+                solution_ref[0].astype(F32),
+                geometry_ref[...].astype(F32),
+                jnp.zeros((5, CG * CG), F32),
+            ],
+            axis=0,
+        )
+        edge = jnp.zeros((8, 6 * CG), F32)
+        inputs = jnp.concatenate([edge, inputs, edge, jnp.zeros((8, 2 * CG), F32)], axis=1)
+        for t in range(peers):
+            for segment in range(0, SENT_INPUT // 8, 2):
+                at = t * blocks * CG + segment * 128
+                sent_ref[t, segment * 8 : segment * 8 + 16, :] = jnp.concatenate(
+                    [inputs[:, at : at + 128], inputs[:, at + 128 : at + 256]], axis=0
+                ).astype(BF)
+
+    for u in range(EARLY_SLOTS):
+        slot = step * EARLY_SLOTS + u
+        picked = nn(x_ref[...], fine_ref[u]) + nn(s_ref[...], cot_ref[u])
+        totals = jnp.concatenate(
+            [picked[0:8, 0:128], picked[0:8, 128:256]], axis=0
+        )
+        high = totals.astype(BF)
+        sent_ref[slot, SENT_INPUT : SENT_INPUT + 16, :] = high
+        sent_ref[slot, SENT_INPUT + 16 : SENT_INPUT + 32, :] = (
+            totals - high.astype(F32)
+        ).astype(BF)
+        last_ref[u] = picked[16:32].astype(BF)
+        first_ref[u] = picked[32:48].astype(BF)
+
+
+def run_early(peers, solution, geometry, fine, cot, pick_x, pick_s):
+    slots, main, width = fine.shape
+
+    def whole(array):
+        return pl.BlockSpec(array.shape, lambda n: (0,) * array.ndim)
+
+    def per_slots(array):
+        return pl.BlockSpec((EARLY_SLOTS,) + array.shape[1:], lambda n: (n, 0, 0))
+
+    edge = jax.ShapeDtypeStruct((slots, 16, width), BF)
+    sent = jax.ShapeDtypeStruct((peers, SENT_EARLY, 128), BF)
+
+    def body(*refs):
+        early_kernel(main // 48, peers, *refs)
+
+    return pl.pallas_call(
+        body,
+        grid=(slots // EARLY_SLOTS,),
+        in_specs=[whole(solution), whole(geometry), per_slots(fine), per_slots(cot)]
+        + [whole(pick_x), whole(pick_s)],
+        out_specs=[whole(sent), per_slots(edge), per_slots(edge)],
+        out_shape=[sent, edge, edge],
+        compiler_params=pltpu.CompilerParams(vmem_limit_bytes=32 * 1024 * 1024),
+    )(solution, geometry, fine, cot, pick_x, pick_s)
 
 
 FINAL_SLOTS = 4
@@ -543,7 +635,6 @@
     for s in range(out_ref.shape[0]):
         slot = step * out_ref.shape[0] + s
         ahead = back_ref[slot, chunk : chunk + 16, :].astype(F32)
-        ahead = ahead + back_ref[slot, chunk + 16 : chunk + 32, :].astype(F32)
         base = jnp.concatenate([ahead[0:8], ahead[8:16]], axis=1) + own_ref[s]
         for k in range(3):
             for p in range(2):
@@ -561,7 +652,7 @@
 
 def run_final(back, pred, own, first, last):
     slots, main, width = pred.shape
-    chunk = back.shape[1] - 32
+    chunk = back.shape[1] - 16
     held = FINAL_SLOTS if main % 192 == 0 else 2 * FINAL_SLOTS
 
     def per_slots(array):
@@ -602,61 +693,35 @@
     peers = lax.axis_size("tile")
     position = lax.axis_index("tile")
     slots, rows = fine_fields.shape[0], fine_fields.shape[4]
-    blocks = rows // 4
     up = [(i, i + 1) for i in range(peers - 1)]
     down = [(i + 1, i) for i in range(peers - 1)]
 
-    totals = jnp.sum(cotangent.astype(F32), axis=(2, 4)).reshape(slots, 6, HALF)
-    totals = jnp.pad(totals, ((0, 0), (0, 2), (0, 0)))
-    mine = coarse_solution.shape[0]
-    inputs = jnp.concatenate([coarse_solution.astype(F32), geometry.astype(F32)[:, None]], axis=1)
-    padded = jnp.pad(inputs, ((0, 0), (0, 0), (6 * CG, 6 * CG)))
-    span = (blocks + 12) * CG
-    windows = jnp.stack(
-        [padded[:, :, t * blocks * CG : t * blocks * CG + span] for t in range(peers)], 0
-    )
-    sent = jnp.concatenate(
-        [
-            windows.reshape(peers, mine * 3 * span),
-            totals.reshape(peers, (slots // peers) * 8 * HALF),
-        ],
-        axis=1,
-    )
-    got = exchanged(sent)
-    coarse = got[:, : mine * 3 * span].reshape(peers * mine, 3, span)
-    sums = got[:, mine * 3 * span :]
+    made = constants(rows)
+    fine = fine_fields.reshape(slots, 12 * rows, HALF)
+    cot = cotangent.reshape(slots, 12 * rows, HALF)
+
+    sent, edge_last, edge_first = run_early(
+        peers,
+        coarse_solution,
+        geometry,
+        fine,
+        cot,
+        jnp.asarray(made["early_x"], BF),
+        jnp.asarray(made["early_s"], BF),
+    )
+    coarse = exchanged(sent)
+    from_before = lax.ppermute(edge_last, "tile", up)
+    from_after = lax.ppermute(edge_first, "tile", down)
+    sums = coarse[:, SENT_INPUT:].astype(F32)
+    sums = sums[:, :16] + sums[:, 16:]
     order = lax.broadcasted_iota(jnp.int32, (peers, peers), 0)
     other = lax.broadcasted_iota(jnp.int32, (peers, peers), 1)
-    behind = jnp.sum(jnp.where((other > order)[:, :, None], sums[None], 0.0), axis=1)
-    later = exchanged(behind).reshape(slots, 8, HALF)
-
-    blank = jnp.zeros((slots, 4, HALF), BF)
-    edge_last = jnp.concatenate(
-        [
-            fine_fields[:, :, 1, :, -1].reshape(slots, 6, HALF),
-            cotangent[:, :, 1, :, -1].reshape(slots, 6, HALF),
-            blank,
-        ],
-        axis=1,
-    )
-    edge_first = jnp.concatenate(
-        [
-            fine_fields[:, :, 0, :, 0].reshape(slots, 6, HALF),
-            cotangent[:, :, 0, :, 0].reshape(slots, 6, HALF),
-            blank,
-        ],
-        axis=1,
-    )
-    from_before = lax.ppermute(edge_last, "tile", up)
-    from_after = lax.ppermute(edge_first, "tile", down)
-
-    made = constants(rows)
-    sel_s = jnp.where(
-        position == 0, jnp.asarray(made["sel_s_first"], BF), jnp.asarray(made["sel_s"], BF)
-    )
+    behind = jnp.sum(jnp.where((other > order)[:, :, None, None], sums[None], 0.0), axis=1)
+    later = exchanged(behind)
+
     fixed = [
         jnp.asarray(made["sel_x"], BF),
-        sel_s,
+        jnp.asarray(made["sel_s"], BF),
         jnp.asarray(made["sel_o"], BF),
         jnp.asarray(made["ex"], BF),
         jnp.asarray(made["eu"], BF),
@@ -683,8 +748,8 @@
         sample_ids,
         position.reshape(1).astype(jnp.int32),
         coarse,
-        fine_fields.reshape(slots, 12 * rows, HALF),
-        cotangent.reshape(slots, 12 * rows, HALF),
+        fine,
+        cot,
         from_before,
         from_after,
         later,
@@ -697,16 +762,14 @@
     to_first = lax.ppermute(first_edge, "tile", up)
     to_last = lax.ppermute(last_edge, "tile", down)
     reduced = jnp.sum(got[:, :chunk], axis=0).astype(BF)
-    sums = got[:, chunk : chunk + 16] + got[:, chunk + 16 :]
+    sums = got[:, chunk:]
     ahead = jnp.sum(jnp.where((other < order)[:, :, None, None], sums[None], 0.0), axis=1)
-    high = lax.reduce_precision(ahead, 8, 7)
     reduced, to_first, to_last = lax.optimization_barrier((reduced, to_first, to_last))
     back = exchanged(
         jnp.concatenate(
             [
                 jnp.broadcast_to(reduced, (peers, chunk, 128)),
-                high.astype(BF),
-                (ahead - high).astype(BF),
+                ahead.astype(BF),
             ],
             axis=1,
         )

time: 138 us -> 135 us (0.978)
  other arithmetic: 5.84 us -> 1.52 us
  waiting for transfers between devices: 19.5 us -> 23.8 us
  starting transfers between devices: 23.6 us -> 21.7 us
    unnamed x60 -> x47, local copies, waits for them, and re-layouts: 1.34 us -> 6.57 us
    all_to_all x3, waiting for transfers between devices: 19.5 us -> 23.8 us  [exchanged(): lax.all_to_all(value, 'tile', split_axis=0, concat_axis=0, tiled=True)]
    slice x4 -> x1, local copies, waits for them, and re-layouts: 2.61 us -> 0.01 us  [local(): sums = got[:, chunk:]]
    pallas_call x1, Pallas kernels: 57.4 us -> 54.9 us  [run_slots(): pl.pallas_call(body, grid_spec=grid_spec, out_shape=out_shape, compiler_p...]
    pallas_call x0 -> x1, Pallas kernels: none -> 1.82 us  [run_early(): pl.pallas_call(body, grid=(slots // EARLY_SLOTS,), in_specs=[whole(soluti...]
    all_to_all x2 -> x0, local copies, waits for them, and re-layouts: 1.74 us -> none  [exchanged(): lax.all_to_all(value, 'tile', split_axis=0, concat_axis=0, tiled=True)]
    reduce_sum x2 -> x1, other arithmetic: 2.51 us -> 1 us  [local(): jnp.sum(jnp.where((other > order)[:, :, None, None], sums[None], 0.0), ax...]
  transfers between devices with their start and end apart: 7 -> 7, of which waited for: 3 -> 3; matrix products, arithmetic and copies ran while one was open for 6% -> 2% of each run, Pallas kernels for 0% -> 0%
where the time goes in v4:
time: 135 us; the launch traced here: 134 us
  Pallas kernels  58.8 us (44%)
  waiting for transfers between devices  23.8 us (18%)
  starting transfers between devices  21.7 us (16%)
  blocking collectives  17.7 us (13%)
  local copies, waits for them, and re-layouts  9.08 us (7%)
  other arithmetic  1.52 us (1%)
    pallas_call x1, Pallas kernels, run_slots(): pl.pallas_call(body, grid_spec=grid_spec, out_shape=out_shape, compiler_p...  54.9 us
    all_to_all x3, waiting for transfers between devices, exchanged(): lax.all_to_all(value, 'tile', split_axis=0, concat_axis=0, tiled=True)  23.8 us
    all_to_all x1, blocking collectives, exchanged(): lax.all_to_all(value, 'tile', split_axis=0, concat_axis=0, tiled=True)  17.7 us
    all_to_all x3, starting transfers between devices, exchanged(): lax.all_to_all(value, 'tile', split_axis=0, concat_axis=0, tiled=True)  14.5 us
    unnamed x47, local copies, waits for them, and re-layouts  6.57 us
  transfers between devices with their start and end apart: 7, of which 3 were waited for; matrix products, arithmetic and copies ran while one was open for 2% of the time, Pallas kernels for 0%

profile of v4, /device:TPU:0, one launch (start us, length us, event | category | flops | bytes accessed | tf_op | source)
XLA Modules:
  0.0 133.7 jit_solution(9895901237755405143)
XLA Ops:
  0.6 1.4 %copy-done.1 = bf16[16,3,2,2,16,256]{5,4,3,2,1,0:T(8,128)(2,1)S(1)} copy-done((bf16[16,3,2,2,16,256]{5,4,3,2,1,0:T(8,128)(2,1)S(1)}, bf16[16,3,2,2,16,256]{5,4,3,2,1,0:T(8,128)(2,1)}, u32[]{:S(2)}) %copy-start.1) | copy-done | bytes 1572888
  2.0 1.4 %copy-done.2 = bf16[16,3,2,2,16,256]{5,4,3,2,1,0:T(8,128)(2,1)S(1)} copy-done((bf16[16,3,2,2,16,256]{5,4,3,2,1,0:T(8,128)(2,1)S(1)}, bf16[16,3,2,2,16,256]{5,4,3,2,1,0:T(8,128)(2,1)}, u32[]{:S(2)}) %copy-start.2) | copy-done | bytes 1572888
  3.5 0.7 copy-done.4
  4.2 0.7 copy-done.5
  4.9 0.7 copy-done.6
  5.6 0.7 copy-done.7
  6.4 1.8 %shard_map.253 = (bf16[16,96,128]{2,1,0:T(8,128)(2,1)}, bf16[16,16,256]{2,1,0:T(8,128)(2,1)S(1)}, bf16[16,16,256]{2,1,0:T(8,128)(2,1)S(1)}) custom-call(bf16[1,2,4096]{2,1,0:T(2,128)(2,1)S(1)} %copy-done.6, s32[1,4096]{1,0:T(1,128)S(1)} %copy-done.7, bf16[16,192,256]{2,1,0:T(8,128)(2,1)S(1)} %bitcast.24, bf16[16,192,256]{2,1,0:T(8,128)(2,1)S(1)} %bitcast.26, ...), custom_call_target="tpu_custom_call" | custom-call | tf_op jit(solution)/shard_map/pallas_call | solution.py:604
  8.2 7.4 %all-to-all-start = ((bf16[16,96,128]{2,1,0:T(8,128)(2,1)}), bf16[16,96,128]{2,1,0:T(8,128)(2,1)S(1)}, u32[]{:S(2)}, u32[]{:S(2)}) async-start(bf16[16,96,128]{2,1,0:T(8,128)(2,1)} %get-tuple-element.23), calls=%async_computation | async-start | bytes 786432 | tf_op jit(solution)/shard_map/all_to_all | solution.py:678
  15.6 2.4 %collective-permute-start = (bf16[16,16,256]{2,1,0:T(8,128)(2,1)S(1)}, bf16[16,16,256]{2,1,0:T(8,128)(2,1)S(1)}, u32[]{:S(2)}, u32[]{:S(2)}) collective-permute-start(bf16[16,16,256]{2,1,0:T(8,128)(2,1)S(1)} %get-tuple-element.24), channel_id=1, source_target_pairs={{0,1},{1,2},{2,3},{3,4},{4,5},{5,6},{6,7},{7,8},{8,9},{9,10},{10,1... | collective-permute-start | bytes 393224 | tf_op jit(solution)/shard_map/ppermute | solution.py:713
  18.1 1.3 collective-permute-start.1
  19.5 0.2 copy.45
  19.8 0.3 copy.46
  20.0 7.7 %all-to-all-done.refs_2_.refs_3_.refs_4_ = bf16[16,96,128]{2,1,0:T(8,128)(2,1)S(1)} async-done(((bf16[16,96,128]{2,1,0:T(8,128)(2,1)}), bf16[16,96,128]{2,1,0:T(8,128)(2,1)S(1)}, u32[]{:S(2)}, u32[]{:S(2)}) %all-to-all-start) | async-done | bytes 393248 | tf_op jit(solution)/shard_map/all_to_all | solution.py:678
  27.8 1.0 select_reduce_fusion.1
  28.8 3.5 %all-to-all-start.1 = ((f32[16,16,128]{2,1,0:T(8,128)}), f32[16,16,128]{2,1,0:T(8,128)S(1)}, u32[]{:S(2)}, u32[]{:S(2)}) async-start(f32[16,16,128]{2,1,0:T(8,128)} %select_reduce_fusion.1), calls=%async_computation.1 | async-start | bytes 262144 | tf_op jit(solution)/shard_map/all_to_all | solution.py:678
  32.4 0.9 copy_bitcast_fusion
  33.3 0.1 copy.44
  33.4 0.1 copy.48
  33.6 0.1 copy.50
  33.7 0.1 copy.47
  33.9 6.4 %all-to-all-done.1.refs_9_ = f32[16,16,128]{2,1,0:T(8,128)S(1)} async-done(((f32[16,16,128]{2,1,0:T(8,128)}), f32[16,16,128]{2,1,0:T(8,128)S(1)}, u32[]{:S(2)}, u32[]{:S(2)}) %all-to-all-start.1) | async-done | bytes 131104 | tf_op jit(solution)/shard_map/all_to_all | solution.py:678
  40.4 54.9 %shard_map.254 = (f32[16,192,256]{2,1,0:T(8,128)}, f32[16,8,256]{2,1,0:T(8,128)S(1)}, f32[16,8,256]{2,1,0:T(8,128)S(1)}, f32[16,8,256]{2,1,0:T(8,128)S(1)}, bf16[16,112,128]{2,1,0:T(8,128)(2,1)}) custom-call(s32[16]{0:T(128)S(1)} %copy-done.8, s32[1]{0:T(128)} %bitcast.refs_1_, bf16[16,96,128]{2,1,0:T(8,128)(2,1)} %copy-done.18, ...), custom_call_target="tpu_custom_call" | custom-call | flops 32000000000 | bytes 16000000 | tf_op jit(solution)/shard_map/pallas_call | solution.py:536
  95.3 3.6 %all-to-all-start.2 = ((bf16[16,112,128]{2,1,0:T(8,128)(2,1)}), bf16[16,112,128]{2,1,0:T(8,128)(2,1)S(1)}, u32[]{:S(2)}, u32[]{:S(2)}) async-start(bf16[16,112,128]{2,1,0:T(8,128)(2,1)} %get-tuple-element.26), calls=%async_computation.2 | async-start | bytes 917504 | tf_op jit(solution)/shard_map/all_to_all | solution.py:678
  98.9 2.2 %collective-permute-start.2 = (f32[16,8,256]{2,1,0:T(8,128)S(1)}, f32[16,8,256]{2,1,0:T(8,128)S(1)}, u32[]{:S(2)}, u32[]{:S(2)}) collective-permute-start(f32[16,8,256]{2,1,0:T(8,128)S(1)} %get-tuple-element.27), channel_id=1, source_target_pairs={{0,1},{1,2},{2,3},{3,4},{4,5},{5,6},{6,7},{7,8},{8,9},{9,10},{10,1... | collective-permute-start | bytes 393224 | tf_op jit(solution)/shard_map/ppermute | solution.py:762
  101.1 1.3 collective-permute-start.3
  102.4 9.7 %all-to-all-done.2 = bf16[16,112,128]{2,1,0:T(8,128)(2,1)S(1)} async-done(((bf16[16,112,128]{2,1,0:T(8,128)(2,1)}), bf16[16,112,128]{2,1,0:T(8,128)(2,1)S(1)}, u32[]{:S(2)}, u32[]{:S(2)}) %all-to-all-start.2) | async-done | bytes 458784 | tf_op jit(solution)/shard_map/all_to_all | solution.py:678
  112.1 0.1 convert_element_type.15
  112.2 0.3 select_reduce_fusion
  112.7 17.7 %all_to_all.20.refs_0_ = bf16[16,112,128]{2,1,0:T(8,128)(2,1)S(1)} all-to-all(bf16[16,112,128]{2,1,0:T(8,128)(2,1)S(1)} %pad_maximum_fusion), channel_id=1, replica_groups=mesh['groups'=2,'tile'=16] {'tile'}, dimensions={0} | all-to-all | bytes 917504 | tf_op jit(solution)/shard_map/all_to_all | solution.py:678
  130.4 2.1 %shard_map.255 = (bf16[16,192,256]{2,1,0:T(8,128)(2,1)}, f32[1152,128]{1,0:T(8,128)}, f32[128,128]{1,0:T(8,128)}, f32[96,128]{1,0:T(8,128)S(1)}, f32[48,128]{1,0:T(8,128)}, /*index=5*/f32[32,128]{1,0:T(8,128)S(1)}) custom-call(bf16[16,112,128]{2,1,0:T(8,128)(2,1)S(1)} %all_to_all.20.refs_0_, f32[16,192,256]{2,1,0:T(8,128)S(1)} %copy-done, ...), custom_call_target="tpu_custom_call" | custom-call | tf_op jit(solution)/shard_map/pallas_call | solution.py:664
  132.5 0.6 reshape.76
  133.1 0.6 copy.51
  (55 shorter events, 0.4 us)
Async XLA Ops:
  0.6 1.4 %copy-start.1 = (bf16[16,3,2,2,16,256]{5,4,3,2,1,0:T(8,128)(2,1)S(1)}, bf16[16,3,2,2,16,256]{5,4,3,2,1,0:T(8,128)(2,1)}, u32[]{:S(2)}) copy-start(bf16[16,3,2,2,16,256]{5,4,3,2,1,0:T(8,128)(2,1)} %param.24) | copy-start | bytes 4718596
  2.0 1.4 %copy-start.2 = (bf16[16,3,2,2,16,256]{5,4,3,2,1,0:T(8,128)(2,1)S(1)}, bf16[16,3,2,2,16,256]{5,4,3,2,1,0:T(8,128)(2,1)}, u32[]{:S(2)}) copy-start(bf16[16,3,2,2,16,256]{5,4,3,2,1,0:T(8,128)(2,1)} %param.25) | copy-start | bytes 4718596
  3.5 0.7 copy-start.4
  4.2 0.7 copy-start.5
  4.9 0.7 copy-start.6
  5.6 0.7 copy-start.7
  6.4 13.0 %copy-start.17 = (bf16[3,3,128,128]{3,2,1,0:T(8,128)(2,1)S(1)}, bf16[3,3,128,128]{3,2,1,0:T(8,128)(2,1)}, u32[]{:S(2)}) copy-start(bf16[3,3,128,128]{3,2,1,0:T(8,128)(2,1)} %param.28) | copy-start | bytes 884740
  8.2 19.6 %all-to-all-start = ((bf16[16,96,128]{2,1,0:T(8,128)(2,1)}), bf16[16,96,128]{2,1,0:T(8,128)(2,1)S(1)}, u32[]{:S(2)}, u32[]{:S(2)}) async-start(bf16[16,96,128]{2,1,0:T(8,128)(2,1)} %get-tuple-element.23), calls=%async_computation | async-start | bytes 786432 | tf_op jit(solution)/shard_map/all_to_all | solution.py:678
  15.6 17.7 %copy-start.21 = (bf16[3,3,3,128]{3,2,1,0:T(4,128)(2,1)S(1)}, bf16[3,3,3,128]{3,2,1,0:T(4,128)(2,1)}, u32[]{:S(2)}) copy-start(bf16[3,3,3,128]{3,2,1,0:T(4,128)(2,1)} %param.27) | copy-start | bytes 20740
  15.6 17.8 %copy-start.20 = (bf16[3,4,4,128]{3,2,1,0:T(4,128)(2,1)S(1)}, bf16[3,4,4,128]{3,2,1,0:T(4,128)(2,1)}, u32[]{:S(2)}) copy-start(bf16[3,4,4,128]{3,2,1,0:T(4,128)(2,1)} %param.30) | copy-start | bytes 36868
  15.6 17.9 %copy-start.19 = (bf16[4,4,6,128]{3,1,2,0:T(4,128)(2,1)S(1)}, bf16[4,4,6,128]{3,1,2,0:T(4,128)(2,1)}, u32[]{:S(2)}) copy-start(bf16[4,4,6,128]{3,1,2,0:T(4,128)(2,1)} %param.31) | copy-start | bytes 73732
  15.6 18.3 %collective-permute-start = (bf16[16,16,256]{2,1,0:T(8,128)(2,1)S(1)}, bf16[16,16,256]{2,1,0:T(8,128)(2,1)S(1)}, u32[]{:S(2)}, u32[]{:S(2)}) collective-permute-start(bf16[16,16,256]{2,1,0:T(8,128)(2,1)S(1)} %get-tuple-element.24), channel_id=1, source_target_pairs={{0,1},{1,2},{2,3},{3,4},{4,5},{5,6},{6,7},{7,8},{8,9},{9,10},{10,1... | collective-permute-start | bytes 393224 | tf_op jit(solution)/shard_map/ppermute | solution.py:713
  18.1 15.8 %collective-permute-start.1 = (bf16[16,16,256]{2,1,0:T(8,128)(2,1)S(1)}, bf16[16,16,256]{2,1,0:T(8,128)(2,1)S(1)}, u32[]{:S(2)}, u32[]{:S(2)}) collective-permute-start(bf16[16,16,256]{2,1,0:T(8,128)(2,1)S(1)} %get-tuple-element.25), channel_id=1, source_target_pairs={{1,0},{2,1},{3,2},{4,3},{5,4},{6,5},{7,6},{8,7},{9,8},{10,9},{11,1... | collective-permute-start | bytes 393224 | tf_op jit(solution)/shard_map/ppermute | solution.py:714
  19.4 14.3 %copy-start.3 = (bf16[128,128]{1,0:T(8,128)(2,1)S(1)}, bf16[128,128]{1,0:T(8,128)(2,1)}, u32[]{:S(2)}) copy-start(bf16[128,128]{1,0:T(8,128)(2,1)} %refs_23_.1) | copy-start | bytes 98308
  19.4 20.9 %copy-start.8 = (s32[16]{0:T(128)S(1)}, s32[16]{0:T(128)}, u32[]{:S(2)}) copy-start(s32[16]{0:T(128)} %refs_0_.3) | copy-start | bytes 196
  19.4 20.9 %copy-start.9 = (bf16[512,240]{1,0:T(8,128)(2,1)S(1)}, bf16[512,240]{1,0:T(8,128)(2,1)}, u32[]{:S(2)}) copy-start(bf16[512,240]{1,0:T(8,128)(2,1)} %constant.36.clone.refs_11_) | copy-start | bytes 737284
  19.4 20.9 %copy-start.10 = (bf16[224,512]{1,0:T(8,128)(2,1)S(1)}, bf16[224,512]{1,0:T(8,128)(2,1)}, u32[]{:S(2)}) copy-start(bf16[224,512]{1,0:T(8,128)(2,1)} %constant.37.clone.refs_12_) | copy-start | bytes 688132
  19.4 20.9 %copy-start.11 = (bf16[256,256]{1,0:T(8,128)(2,1)S(1)}, bf16[256,256]{1,0:T(8,128)(2,1)}, u32[]{:S(2)}) copy-start(bf16[256,256]{1,0:T(8,128)(2,1)} %constant.44.clone.refs_19_) | copy-start | bytes 393220
  19.4 20.9 %copy-start.12 = (bf16[512,48]{1,0:T(8,128)(2,1)S(1)}, bf16[512,48]{1,0:T(8,128)(2,1)}, u32[]{:S(2)}) copy-start(bf16[512,48]{1,0:T(8,128)(2,1)} %constant.38.clone.refs_13_) | copy-start | bytes 147460
  19.5 20.9 %copy-start.13 = (bf16[256,240]{1,0:T(8,128)(2,1)S(1)}, bf16[256,240]{1,0:T(8,128)(2,1)}, u32[]{:S(2)}) copy-start(bf16[256,240]{1,0:T(8,128)(2,1)} %constant.35.clone.refs_10_) | copy-start | bytes 368644
  19.5 20.9 %copy-start.14 = (f32[192,128]{1,0:T(8,128)S(1)}, f32[192,128]{1,0:T(8,128)}, u32[]{:S(2)}) copy-start(f32[192,128]{1,0:T(8,128)} %constant.40.clone.refs_15_) | copy-start | bytes 294916
  19.5 20.9 %copy-start.15 = (bf16[80,32]{1,0:T(8,128)(2,1)S(1)}, bf16[80,32]{1,0:T(8,128)(2,1)}, u32[]{:S(2)}) copy-start(bf16[80,32]{1,0:T(8,128)(2,1)} %constant.42.clone.refs_17_) | copy-start | bytes 15364
  19.5 20.9 %copy-start.16 = (f32[32,80]{1,0:T(8,128)S(1)}, f32[32,80]{1,0:T(8,128)}, u32[]{:S(2)}) copy-start(f32[32,80]{1,0:T(8,128)} %constant.43.clone.refs_18_) | copy-start | bytes 30724
  27.8 12.5 %copy-start.18 = (bf16[16,96,128]{2,1,0:T(8,128)(2,1)}, bf16[16,96,128]{2,1,0:T(8,128)(2,1)S(1)}, u32[]{:S(2)}) copy-start(bf16[16,96,128]{2,1,0:T(8,128)(2,1)S(1)} %all-to-all-done.refs_2_.refs_3_.refs_4_) | copy-start | bytes 1179652
  28.8 11.5 %all-to-all-start.1 = ((f32[16,16,128]{2,1,0:T(8,128)}), f32[16,16,128]{2,1,0:T(8,128)S(1)}, u32[]{:S(2)}, u32[]{:S(2)}) async-start(f32[16,16,128]{2,1,0:T(8,128)} %select_reduce_fusion.1), calls=%async_computation.1 | async-start | bytes 262144 | tf_op jit(solution)/shard_map/all_to_all | solution.py:678
  95.3 16.8 %all-to-all-start.2 = ((bf16[16,112,128]{2,1,0:T(8,128)(2,1)}), bf16[16,112,128]{2,1,0:T(8,128)(2,1)S(1)}, u32[]{:S(2)}, u32[]{:S(2)}) async-start(bf16[16,112,128]{2,1,0:T(8,128)(2,1)} %get-tuple-element.26), calls=%async_computation.2 | async-start | bytes 917504 | tf_op jit(solution)/shard_map/all_to_all | solution.py:678
  98.9 13.3 %collective-permute-start.2 = (f32[16,8,256]{2,1,0:T(8,128)S(1)}, f32[16,8,256]{2,1,0:T(8,128)S(1)}, u32[]{:S(2)}, u32[]{:S(2)}) collective-permute-start(f32[16,8,256]{2,1,0:T(8,128)S(1)} %get-tuple-element.27), channel_id=1, source_target_pairs={{0,1},{1,2},{2,3},{3,4},{4,5},{5,6},{6,7},{7,8},{8,9},{9,10},{10,1... | collective-permute-start | bytes 393224 | tf_op jit(solution)/shard_map/ppermute | solution.py:762
  101.1 11.1 %collective-permute-start.3 = (f32[16,8,256]{2,1,0:T(8,128)S(1)}, f32[16,8,256]{2,1,0:T(8,128)S(1)}, u32[]{:S(2)}, u32[]{:S(2)}) collective-permute-start(f32[16,8,256]{2,1,0:T(8,128)S(1)} %get-tuple-element.28), channel_id=1, source_target_pairs={{1,0},{2,1},{3,2},{4,3},{5,4},{6,5},{7,6},{8,7},{9,8},{10,9},{11,1... | collective-permute-start | bytes 393224 | tf_op jit(solution)/shard_map/ppermute | solution.py:763
  112.1 18.3 %copy-start = (f32[16,192,256]{2,1,0:T(8,128)S(1)}, f32[16,192,256]{2,1,0:T(8,128)}, u32[]{:S(2)}) copy-start(f32[16,192,256]{2,1,0:T(8,128)} %get-tuple-element.30.refs_1_) | copy-start | bytes 9437188

commit v5 on v4

--- a/solution.py
+++ b/solution.py
@@ -17,10 +17,10 @@
 BF = jnp.bfloat16
 F32 = jnp.float32
 
-AUX = 48
-SENT_INPUT = 64
+AUX = 64
+SENT_INPUT = 32
 SENT_EARLY = SENT_INPUT + 32
-PER_STEP = 2
+PER_STEP = 4
 GRAD_ROWS = 1536
 UP_AT, DOWN_AT, FIRST_AT, PROJECT_AT = 1280, 1376, 1424, 1152
 
@@ -33,16 +33,9 @@
     return lax.dot_general(a, b, (((1,), (1,)), ((), ())), preferred_element_type=F32)
 
 
-def exact(a, b):
-    return lax.dot_general(
-        a, b, (((1,), (0,)), ((), ())), precision=lax.Precision.HIGHEST, preferred_element_type=F32
-    )
-
-
-def exact_t(a, b):
-    return lax.dot_general(
-        a, b, (((1,), (1,)), ((), ())), precision=lax.Precision.HIGHEST, preferred_element_type=F32
-    )
+def halves(value):
+    high = value.astype(BF)
+    return high, (value - high.astype(F32)).astype(BF)
 
 
 def row_at(tap, r):
@@ -146,8 +139,8 @@
         sel_o=sel_o.reshape(12 * rows + 32, blocks * 128),
         ex=ex.reshape(512, 48),
         eu=eu.reshape(1024, 96),
-        ext=np.concatenate(list(np.swapaxes(ex, 1, 2)), 0),
-        eut=np.concatenate(list(np.swapaxes(eu, 1, 2)), 0),
+        ext=np.concatenate(list(np.swapaxes(ex, 1, 2)), 1),
+        eut=np.concatenate(list(np.swapaxes(eu, 1, 2)), 1),
         ef=ef,
         eft=ef.T,
         pool_both=np.concatenate([pool, none, none, pool], 0),
@@ -173,8 +166,9 @@
     cells = blocks * CG
     by_segment = coarse_ref[0, 0:SENT_INPUT, :].astype(F32)
     inputs = jnp.concatenate(
-        [by_segment[at : at + 8] for at in range(0, SENT_INPUT, 8)], axis=1
-    )
+        [by_segment[at : at + 4] for at in range(0, SENT_INPUT, 4)], axis=1
+    )
+    inputs = jnp.concatenate([inputs, jnp.zeros_like(inputs)], axis=0)
     lane_in = lax.broadcasted_iota(jnp.int32, inputs.shape, 1) % CG
     by_col = (
         moved(inputs, 2, lane_in, lambda x: x >= 2),
@@ -267,8 +261,7 @@
     ids_ref,
     tile_ref,
     coarse_first_ref,
-    coarse_a_ref,
-    coarse_b_ref,
+    coarse_refs,
     fine_ref,
     cot_ref,
     before_ref,
@@ -345,12 +338,12 @@
 
     def one_slot(u, slot, now, soon, done):
         back = backward(done)
-        ahead = forward((coarse_a_ref, coarse_b_ref)[u], soon)
+        ahead = forward(coarse_refs[u], soon)
         advance(back)
         later = jnp.concatenate([later_ref[u, 0:8, :], later_ref[u, 8:16, :]], axis=1)
         later_high = later.astype(BF).astype(F32)
         later_both = jnp.concatenate([later_high, later - later_high], axis=0).astype(BF)
-        aux = [before_ref[u], after_ref[u], later_both]
+        aux = [before_ref[u], after_ref[u], later_both, jnp.zeros((16, HALF), BF)]
         fine_all = nn(sel_x_ref[...], jnp.concatenate([fine_ref[u]] + aux, axis=0))
         slope_all = nn(sel_s_ref[...], jnp.concatenate([cot_ref[u]] + aux, axis=0))
         row = lax.broadcasted_iota(jnp.int32, (64, HALF), 0)
@@ -450,13 +443,13 @@
     @pl.when(step == pl.num_programs(0) - 1)
     def _():
         finish(backward((pl.num_programs(0) * PER_STEP - 1) % 3))
-        up = jnp.zeros((96, 128), F32)
-        down = jnp.zeros((48, 128), F32)
-        for r in range(4):
-            lanes = slice(r * 128, (r + 1) * 128)
-            up = up + exact_t(eut_ref[r * 96 : (r + 1) * 96, :], gu_ref[lanes, :])
-            down = down + exact_t(ext_ref[r * 48 : (r + 1) * 48, :], gd_ref[lanes, :])
-        first = exact(eft_ref[...], fg_ref[...])
+        rows = [slice(r * 128, (r + 1) * 128) for r in range(4)]
+        taps = halves(jnp.concatenate([gu_ref[at, :] for at in rows], axis=1))
+        up = nt(eut_ref[...], taps[0]) + nt(eut_ref[...], taps[1])
+        taps = halves(jnp.concatenate([gd_ref[at, :] for at in rows], axis=1))
+        down = nt(ext_ref[...], taps[0]) + nt(ext_ref[...], taps[1])
+        taps = halves(fg_ref[...])
+        first = nn(eft_ref[...], taps[0]) + nn(eft_ref[...], taps[1])
         pieces = [
             dil_ref[i * 128 : (i + 1) * 128, j * 128 : (j + 1) * 128]
             for i in range(3)
@@ -489,8 +482,7 @@
     one = (1,) + coarse.shape[1:]
     in_specs = [
         pl.BlockSpec(one, lambda n, ids, tile: (ids[0], 0, 0)),
-        coarse_of(1),
-        coarse_of(2),
+        *[coarse_of(ahead + 1) for ahead in range(PER_STEP)],
         per_slot(fine),
         per_slot(cot),
         per_slot(before),
@@ -531,7 +523,7 @@
     )
 
     def body(*refs):
-        slot_kernel(blocks, peers, *refs)
+        slot_kernel(blocks, peers, *refs[:3], refs[3 : 3 + PER_STEP], *refs[3 + PER_STEP :])
 
     return pl.pallas_call(
         body,
@@ -541,7 +533,7 @@
         cost_estimate=pl.CostEstimate(
             flops=slots * blocks * 500_000_000, bytes_accessed=16_000_000, transcendentals=0
         ),
-    )(ids, tile, coarse, coarse, coarse, fine, cot, before, after, later, *fixed, *weights)
+    )(ids, tile, *[coarse] * (PER_STEP + 1), fine, cot, before, after, later, *fixed, *weights)
 
 
 EARLY_SLOTS = 4
@@ -565,11 +557,14 @@
         edge = jnp.zeros((8, 6 * CG), F32)
         inputs = jnp.concatenate([edge, inputs, edge, jnp.zeros((8, 2 * CG), F32)], axis=1)
         for t in range(peers):
-            for segment in range(0, SENT_INPUT // 8, 2):
-                at = t * blocks * CG + segment * 128
-                sent_ref[t, segment * 8 : segment * 8 + 16, :] = jnp.concatenate(
-                    [inputs[:, at : at + 128], inputs[:, at + 128 : at + 256]], axis=0
-                ).astype(BF)
+            at = t * blocks * CG
+            sent_ref[t, 0:SENT_INPUT, :] = jnp.concatenate(
+                [
+                    inputs[0:4, at + segment * 128 : at + segment * 128 + 128]
+                    for segment in range(SENT_INPUT // 4)
+                ],
+                axis=0,
+            ).astype(BF)
 
     for u in range(EARLY_SLOTS):
         slot = step * EARLY_SLOTS + u
@@ -608,7 +603,7 @@
         + [whole(pick_x), whole(pick_s)],
         out_specs=[whole(sent), per_slots(edge), per_slots(edge)],
         out_shape=[sent, edge, edge],
-        compiler_params=pltpu.CompilerParams(vmem_limit_bytes=32 * 1024 * 1024),
+        compiler_params=pltpu.CompilerParams(vmem_limit_bytes=60 * 1024 * 1024),
     )(solution, geometry, fine, cot, pick_x, pick_s)
 
 
@@ -725,10 +720,10 @@
         jnp.asarray(made["sel_o"], BF),
         jnp.asarray(made["ex"], BF),
         jnp.asarray(made["eu"], BF),
-        jnp.asarray(made["ext"], F32),
-        jnp.asarray(made["eut"], F32),
+        jnp.asarray(made["ext"], BF),
+        jnp.asarray(made["eut"], BF),
         jnp.asarray(made["ef"], BF),
-        jnp.asarray(made["eft"], F32),
+        jnp.asarray(made["eft"], BF),
         jnp.asarray(made["pool_both"], BF),
     ]
     second = dilated_weight

time: 135 us -> 128 us (0.948)
  local copies, waits for them, and re-layouts: 9.08 us -> 3.34 us
  waiting for transfers between devices: 23.8 us -> 21.7 us
    unnamed x47 -> x35, local copies, waits for them, and re-layouts: 6.57 us -> 0.85 us
    pallas_call x1, Pallas kernels: 1.82 us -> 4.22 us  [run_early(): pl.pallas_call(body, grid=(slots // EARLY_SLOTS,), in_specs=[whole(soluti...]
    all_to_all x3, waiting for transfers between devices: 23.8 us -> 21.7 us  [exchanged(): lax.all_to_all(value, 'tile', split_axis=0, concat_axis=0, tiled=True)]
where the time goes in v5:
time: 128 us; the launch traced here: 127 us
  Pallas kernels  60 us (47%)
  starting transfers between devices  21.7 us (17%)
  waiting for transfers between devices  21.7 us (17%)
  blocking collectives  17.7 us (14%)
  local copies, waits for them, and re-layouts  3.34 us (3%)
  other arithmetic  1.52 us (1%)
    pallas_call x1, Pallas kernels, run_slots(): pl.pallas_call(body, grid_spec=grid_spec, out_shape=out_shape, compiler_p...  53.7 us
    all_to_all x3, waiting for transfers between devices, exchanged(): lax.all_to_all(value, 'tile', split_axis=0, concat_axis=0, tiled=True)  21.7 us
    all_to_all x1, blocking collectives, exchanged(): lax.all_to_all(value, 'tile', split_axis=0, concat_axis=0, tiled=True)  17.7 us
    all_to_all x3, starting transfers between devices, exchanged(): lax.all_to_all(value, 'tile', split_axis=0, concat_axis=0, tiled=True)  14.5 us
    pallas_call x1, Pallas kernels, run_early(): pl.pallas_call(body, grid=(slots // EARLY_SLOTS,), in_specs=[whole(soluti...  4.22 us
  transfers between devices with their start and end apart: 7, of which 3 were waited for; matrix products, arithmetic and copies ran while one was open for 2% of the time, Pallas kernels for 0%

profile of v5, /device:TPU:0, one launch (start us, length us, event | category | flops | bytes accessed | tf_op | source)
XLA Modules:
  0.0 127.0 jit_solution(4721896891362002287)
XLA Ops:
  0.6 4.2 %shard_map.253 = (bf16[16,64,128]{2,1,0:T(8,128)(2,1)}, bf16[16,16,256]{2,1,0:T(8,128)(2,1)}, bf16[16,16,256]{2,1,0:T(8,128)(2,1)}) custom-call(bf16[1,2,4096]{2,1,0:T(2,128)(2,1)} %refs_0_.2, s32[1,4096]{1,0:T(1,128)} %refs_1_.1, bf16[16,192,256]{2,1,0:T(8,128)(2,1)} %bitcast.27, bf16[16,192,256]{2,1,0:T(8,128)(2,1)} %bitcast.29, ...), custom_call_target="tpu_custom_call" | custom-call | tf_op jit(solution)/shard_map/pallas_call | solution.py:599
  4.9 7.4 %all-to-all-start = ((bf16[16,64,128]{2,1,0:T(8,128)(2,1)}), bf16[16,64,128]{2,1,0:T(8,128)(2,1)S(1)}, u32[]{:S(2)}, u32[]{:S(2)}) async-start(bf16[16,64,128]{2,1,0:T(8,128)(2,1)} %get-tuple-element.23), calls=%async_computation | async-start | bytes 524288 | tf_op jit(solution)/shard_map/all_to_all | solution.py:673
  12.3 2.4 %collective-permute-start = (bf16[16,16,256]{2,1,0:T(8,128)(2,1)}, bf16[16,16,256]{2,1,0:T(8,128)(2,1)S(1)}, u32[]{:S(2)}, u32[]{:S(2)}) collective-permute-start(bf16[16,16,256]{2,1,0:T(8,128)(2,1)} %get-tuple-element.24), channel_id=1, source_target_pairs={{0,1},{1,2},{2,3},{3,4},{4,5},{5,6},{6,7},{7,8},{8,9},{9,10},{10,1... | collective-permute-start | bytes 393224 | tf_op jit(solution)/shard_map/ppermute | solution.py:708
  14.8 1.3 %collective-permute-start.1 = (bf16[16,16,256]{2,1,0:T(8,128)(2,1)}, bf16[16,16,256]{2,1,0:T(8,128)(2,1)S(1)}, u32[]{:S(2)}, u32[]{:S(2)}) collective-permute-start(bf16[16,16,256]{2,1,0:T(8,128)(2,1)} %get-tuple-element.25), channel_id=1, source_target_pairs={{1,0},{2,1},{3,2},{4,3},{5,4},{6,5},{7,6},{8,7},{9,8},{10,9},{11,1... | collective-permute-start | bytes 393224 | tf_op jit(solution)/shard_map/ppermute | solution.py:709
  16.1 0.0 copy-start.3
  16.1 0.0 copy-start.4
  16.1 0.0 copy-start.5
  16.1 0.0 copy-start.7
  16.2 0.0 copy-start.8
  16.2 0.2 copy.45
  16.5 0.3 copy.46
  16.7 5.6 %all-to-all-done.refs_2_.refs_3_.refs_4_.refs_5_.refs_6_ = bf16[16,64,128]{2,1,0:T(8,128)(2,1)S(1)} async-done(((bf16[16,64,128]{2,1,0:T(8,128)(2,1)}), bf16[16,64,128]{2,1,0:T(8,128)(2,1)S(1)}, u32[]{:S(2)}, u32[]{:S(2)}) %all-to-all-start) | async-done | bytes 262176 | tf_op jit(solution)/shard_map/all_to_all | solution.py:673
  22.4 1.0 select_reduce_fusion.1
  23.4 3.5 %all-to-all-start.1 = ((f32[16,16,128]{2,1,0:T(8,128)}), f32[16,16,128]{2,1,0:T(8,128)S(1)}, u32[]{:S(2)}, u32[]{:S(2)}) async-start(f32[16,16,128]{2,1,0:T(8,128)} %select_reduce_fusion.1), calls=%async_computation.1 | async-start | bytes 262144 | tf_op jit(solution)/shard_map/all_to_all | solution.py:673
  26.9 0.9 copy_bitcast_fusion
  27.8 0.1 copy.44
  27.9 0.1 copy.48
  28.1 0.1 copy.50
  28.2 0.1 copy.47
  28.4 6.4 %all-to-all-done.1.refs_11_ = f32[16,16,128]{2,1,0:T(8,128)S(1)} async-done(((f32[16,16,128]{2,1,0:T(8,128)}), f32[16,16,128]{2,1,0:T(8,128)S(1)}, u32[]{:S(2)}, u32[]{:S(2)}) %all-to-all-start.1) | async-done | bytes 131104 | tf_op jit(solution)/shard_map/all_to_all | solution.py:673
  34.9 53.7 %shard_map.254 = (f32[16,192,256]{2,1,0:T(8,128)}, f32[16,8,256]{2,1,0:T(8,128)S(1)}, f32[16,8,256]{2,1,0:T(8,128)S(1)}, f32[16,8,256]{2,1,0:T(8,128)S(1)}, bf16[16,112,128]{2,1,0:T(8,128)(2,1)}) custom-call(s32[16]{0:T(128)S(1)} %copy-done.2, s32[1]{0:T(128)} %bitcast.refs_1_, bf16[16,64,128]{2,1,0:T(8,128)(2,1)} %copy-done.12, ...), custom_call_target="tpu_custom_call" | custom-call | flops 32000000000 | bytes 16000000 | tf_op jit(solution)/shard_map/pallas_call | solution.py:528
  88.6 3.6 %all-to-all-start.2 = ((bf16[16,112,128]{2,1,0:T(8,128)(2,1)}), bf16[16,112,128]{2,1,0:T(8,128)(2,1)S(1)}, u32[]{:S(2)}, u32[]{:S(2)}) async-start(bf16[16,112,128]{2,1,0:T(8,128)(2,1)} %get-tuple-element.26), calls=%async_computation.2 | async-start | bytes 917504 | tf_op jit(solution)/shard_map/all_to_all | solution.py:673
  92.2 2.2 %collective-permute-start.2 = (f32[16,8,256]{2,1,0:T(8,128)S(1)}, f32[16,8,256]{2,1,0:T(8,128)S(1)}, u32[]{:S(2)}, u32[]{:S(2)}) collective-permute-start(f32[16,8,256]{2,1,0:T(8,128)S(1)} %get-tuple-element.27), channel_id=1, source_target_pairs={{0,1},{1,2},{2,3},{3,4},{4,5},{5,6},{6,7},{7,8},{8,9},{9,10},{10,1... | collective-permute-start | bytes 393224 | tf_op jit(solution)/shard_map/ppermute | solution.py:757
  94.4 1.3 %collective-permute-start.3 = (f32[16,8,256]{2,1,0:T(8,128)S(1)}, f32[16,8,256]{2,1,0:T(8,128)S(1)}, u32[]{:S(2)}, u32[]{:S(2)}) collective-permute-start(f32[16,8,256]{2,1,0:T(8,128)S(1)} %get-tuple-element.28), channel_id=1, source_target_pairs={{1,0},{2,1},{3,2},{4,3},{5,4},{6,5},{7,6},{8,7},{9,8},{10,9},{11,1... | collective-permute-start | bytes 393224 | tf_op jit(solution)/shard_map/ppermute | solution.py:758
  95.7 9.7 %all-to-all-done.2 = bf16[16,112,128]{2,1,0:T(8,128)(2,1)S(1)} async-done(((bf16[16,112,128]{2,1,0:T(8,128)(2,1)}), bf16[16,112,128]{2,1,0:T(8,128)(2,1)S(1)}, u32[]{:S(2)}, u32[]{:S(2)}) %all-to-all-start.2) | async-done | bytes 458784 | tf_op jit(solution)/shard_map/all_to_all | solution.py:673
  105.4 0.1 convert_element_type.15
  105.5 0.3 select_reduce_fusion
  105.9 0.1 broadcast_in_dim.41
  106.0 17.7 %all_to_all.20.refs_0_ = bf16[16,112,128]{2,1,0:T(8,128)(2,1)S(1)} all-to-all(bf16[16,112,128]{2,1,0:T(8,128)(2,1)S(1)} %pad_maximum_fusion), channel_id=1, replica_groups=mesh['groups'=2,'tile'=16] {'tile'}, dimensions={0} | all-to-all | bytes 917504 | tf_op jit(solution)/shard_map/all_to_all | solution.py:673
  123.7 2.1 %shard_map.255 = (bf16[16,192,256]{2,1,0:T(8,128)(2,1)}, f32[1152,128]{1,0:T(8,128)}, f32[128,128]{1,0:T(8,128)}, f32[96,128]{1,0:T(8,128)S(1)}, f32[48,128]{1,0:T(8,128)}, /*index=5*/f32[32,128]{1,0:T(8,128)S(1)}) custom-call(bf16[16,112,128]{2,1,0:T(8,128)(2,1)S(1)} %all_to_all.20.refs_0_, f32[16,192,256]{2,1,0:T(8,128)S(1)} %copy-done, ...), custom_call_target="tpu_custom_call" | custom-call | tf_op jit(solution)/shard_map/pallas_call | solution.py:659
  125.8 0.6 reshape.76
  126.4 0.6 copy.51
  (43 shorter events, 0.3 us)
Async XLA Ops:
  0.6 15.4 %copy-start.11 = (bf16[3,3,128,128]{3,2,1,0:T(8,128)(2,1)S(1)}, bf16[3,3,128,128]{3,2,1,0:T(8,128)(2,1)}, u32[]{:S(2)}) copy-start(bf16[3,3,128,128]{3,2,1,0:T(8,128)(2,1)} %param.28) | copy-start | bytes 884740
  4.9 17.5 %all-to-all-start = ((bf16[16,64,128]{2,1,0:T(8,128)(2,1)}), bf16[16,64,128]{2,1,0:T(8,128)(2,1)S(1)}, u32[]{:S(2)}, u32[]{:S(2)}) async-start(bf16[16,64,128]{2,1,0:T(8,128)(2,1)} %get-tuple-element.23), calls=%async_computation | async-start | bytes 524288 | tf_op jit(solution)/shard_map/all_to_all | solution.py:673
  12.3 15.5 %copy-start.15 = (bf16[3,3,3,128]{3,2,1,0:T(4,128)(2,1)S(1)}, bf16[3,3,3,128]{3,2,1,0:T(4,128)(2,1)}, u32[]{:S(2)}) copy-start(bf16[3,3,3,128]{3,2,1,0:T(4,128)(2,1)} %param.27) | copy-start | bytes 20740
  12.3 15.7 %copy-start.14 = (bf16[3,4,4,128]{3,2,1,0:T(4,128)(2,1)S(1)}, bf16[3,4,4,128]{3,2,1,0:T(4,128)(2,1)}, u32[]{:S(2)}) copy-start(bf16[3,4,4,128]{3,2,1,0:T(4,128)(2,1)} %param.30) | copy-start | bytes 36868
  12.3 15.8 %copy-start.13 = (bf16[4,4,6,128]{3,1,2,0:T(4,128)(2,1)S(1)}, bf16[4,4,6,128]{3,1,2,0:T(4,128)(2,1)}, u32[]{:S(2)}) copy-start(bf16[4,4,6,128]{3,1,2,0:T(4,128)(2,1)} %param.31) | copy-start | bytes 73732
  12.3 16.1 %collective-permute-start = (bf16[16,16,256]{2,1,0:T(8,128)(2,1)}, bf16[16,16,256]{2,1,0:T(8,128)(2,1)S(1)}, u32[]{:S(2)}, u32[]{:S(2)}) collective-permute-start(bf16[16,16,256]{2,1,0:T(8,128)(2,1)} %get-tuple-element.24), channel_id=1, source_target_pairs={{0,1},{1,2},{2,3},{3,4},{4,5},{5,6},{6,7},{7,8},{8,9},{9,10},{10,1... | collective-permute-start | bytes 393224 | tf_op jit(solution)/shard_map/ppermute | solution.py:708
  14.8 13.6 %collective-permute-start.1 = (bf16[16,16,256]{2,1,0:T(8,128)(2,1)}, bf16[16,16,256]{2,1,0:T(8,128)(2,1)S(1)}, u32[]{:S(2)}, u32[]{:S(2)}) collective-permute-start(bf16[16,16,256]{2,1,0:T(8,128)(2,1)} %get-tuple-element.25), channel_id=1, source_target_pairs={{1,0},{2,1},{3,2},{4,3},{5,4},{6,5},{7,6},{8,7},{9,8},{10,9},{11,1... | collective-permute-start | bytes 393224 | tf_op jit(solution)/shard_map/ppermute | solution.py:709
  16.1 12.2 %copy-start.1 = (bf16[128,128]{1,0:T(8,128)(2,1)S(1)}, bf16[128,128]{1,0:T(8,128)(2,1)}, u32[]{:S(2)}) copy-start(bf16[128,128]{1,0:T(8,128)(2,1)} %refs_25_.1) | copy-start | bytes 98308
  16.1 18.7 %copy-start.2 = (s32[16]{0:T(128)S(1)}, s32[16]{0:T(128)}, u32[]{:S(2)}) copy-start(s32[16]{0:T(128)} %refs_0_.3) | copy-start | bytes 196
  16.1 18.7 %copy-start.3 = (bf16[224,512]{1,0:T(8,128)(2,1)S(1)}, bf16[224,512]{1,0:T(8,128)(2,1)}, u32[]{:S(2)}) copy-start(bf16[224,512]{1,0:T(8,128)(2,1)} %constant.37.clone.refs_14_) | copy-start | bytes 688132
  16.1 18.7 %copy-start.4 = (bf16[96,1024]{1,0:T(8,128)(2,1)S(1)}, bf16[96,1024]{1,0:T(8,128)(2,1)}, u32[]{:S(2)}) copy-start(bf16[96,1024]{1,0:T(8,128)(2,1)} %constant.41.clone.refs_18_) | copy-start | bytes 589828
  16.1 18.7 %copy-start.5 = (bf16[256,256]{1,0:T(8,128)(2,1)S(1)}, bf16[256,256]{1,0:T(8,128)(2,1)}, u32[]{:S(2)}) copy-start(bf16[256,256]{1,0:T(8,128)(2,1)} %constant.44.clone.refs_21_) | copy-start | bytes 393220
  16.1 18.7 %copy-start.6 = (bf16[512,48]{1,0:T(8,128)(2,1)S(1)}, bf16[512,48]{1,0:T(8,128)(2,1)}, u32[]{:S(2)}) copy-start(bf16[512,48]{1,0:T(8,128)(2,1)} %constant.38.clone.refs_15_) | copy-start | bytes 147460
  16.1 18.7 %copy-start.7 = (bf16[256,256]{1,0:T(8,128)(2,1)S(1)}, bf16[256,256]{1,0:T(8,128)(2,1)}, u32[]{:S(2)}) copy-start(bf16[256,256]{1,0:T(8,128)(2,1)} %constant.35.clone.refs_12_) | copy-start | bytes 393220
  16.2 18.7 %copy-start.8 = (bf16[48,512]{1,0:T(8,128)(2,1)S(1)}, bf16[48,512]{1,0:T(8,128)(2,1)}, u32[]{:S(2)}) copy-start(bf16[48,512]{1,0:T(8,128)(2,1)} %constant.40.clone.refs_17_) | copy-start | bytes 147460
  16.2 18.7 %copy-start.9 = (bf16[80,32]{1,0:T(8,128)(2,1)S(1)}, bf16[80,32]{1,0:T(8,128)(2,1)}, u32[]{:S(2)}) copy-start(bf16[80,32]{1,0:T(8,128)(2,1)} %constant.42.clone.refs_19_) | copy-start | bytes 15364
  16.2 18.7 %copy-start.10 = (bf16[32,80]{1,0:T(8,128)(2,1)S(1)}, bf16[32,80]{1,0:T(8,128)(2,1)}, u32[]{:S(2)}) copy-start(bf16[32,80]{1,0:T(8,128)(2,1)} %constant.43.clone.refs_20_) | copy-start | bytes 15364
  22.3 12.5 %copy-start.12 = (bf16[16,64,128]{2,1,0:T(8,128)(2,1)}, bf16[16,64,128]{2,1,0:T(8,128)(2,1)S(1)}, u32[]{:S(2)}) copy-start(bf16[16,64,128]{2,1,0:T(8,128)(2,1)S(1)} %all-to-all-done.refs_2_.refs_3_.refs_4_.refs_5_.refs_6_) | copy-start | bytes 786436
  23.4 11.4 %all-to-all-start.1 = ((f32[16,16,128]{2,1,0:T(8,128)}), f32[16,16,128]{2,1,0:T(8,128)S(1)}, u32[]{:S(2)}, u32[]{:S(2)}) async-start(f32[16,16,128]{2,1,0:T(8,128)} %select_reduce_fusion.1), calls=%async_computation.1 | async-start | bytes 262144 | tf_op jit(solution)/shard_map/all_to_all | solution.py:673
  88.6 16.8 %all-to-all-start.2 = ((bf16[16,112,128]{2,1,0:T(8,128)(2,1)}), bf16[16,112,128]{2,1,0:T(8,128)(2,1)S(1)}, u32[]{:S(2)}, u32[]{:S(2)}) async-start(bf16[16,112,128]{2,1,0:T(8,128)(2,1)} %get-tuple-element.26), calls=%async_computation.2 | async-start | bytes 917504 | tf_op jit(solution)/shard_map/all_to_all | solution.py:673
  92.2 13.3 %collective-permute-start.2 = (f32[16,8,256]{2,1,0:T(8,128)S(1)}, f32[16,8,256]{2,1,0:T(8,128)S(1)}, u32[]{:S(2)}, u32[]{:S(2)}) collective-permute-start(f32[16,8,256]{2,1,0:T(8,128)S(1)} %get-tuple-element.27), channel_id=1, source_target_pairs={{0,1},{1,2},{2,3},{3,4},{4,5},{5,6},{6,7},{7,8},{8,9},{9,10},{10,1... | collective-permute-start | bytes 393224 | tf_op jit(solution)/shard_map/ppermute | solution.py:757
  94.4 11.1 %collective-permute-start.3 = (f32[16,8,256]{2,1,0:T(8,128)S(1)}, f32[16,8,256]{2,1,0:T(8,128)S(1)}, u32[]{:S(2)}, u32[]{:S(2)}) collective-permute-start(f32[16,8,256]{2,1,0:T(8,128)S(1)} %get-tuple-element.28), channel_id=1, source_target_pairs={{1,0},{2,1},{3,2},{4,3},{5,4},{6,5},{7,6},{8,7},{9,8},{10,9},{11,1... | collective-permute-start | bytes 393224 | tf_op jit(solution)/shard_map/ppermute | solution.py:758
  105.4 18.3 %copy-start = (f32[16,192,256]{2,1,0:T(8,128)S(1)}, f32[16,192,256]{2,1,0:T(8,128)}, u32[]{:S(2)}) copy-start(f32[16,192,256]{2,1,0:T(8,128)} %get-tuple-element.30.refs_1_) | copy-start | bytes 9437188

commit v6 on v5

--- a/solution.py
+++ b/solution.py
@@ -127,6 +127,9 @@
     for ch in range(3):
         for tap in range(9):
             ef[tap * 8 + ch, ch * 9 + tap] = 1
+    ef_all = np.zeros((3, 256, 32), np.float32)
+    for window in range(3):
+        ef_all[window, window * 80 : (window + 1) * 80] = ef
     pool = np.zeros((CG, HALF), np.float32)
     for c in range(HALF):
         pool[c // 4, c] = 1
@@ -141,7 +144,7 @@
         eu=eu.reshape(1024, 96),
         ext=np.concatenate(list(np.swapaxes(ex, 1, 2)), 1),
         eut=np.concatenate(list(np.swapaxes(eu, 1, 2)), 1),
-        ef=ef,
+        ef=ef_all.reshape(768, 32),
         eft=ef.T,
         pool_both=np.concatenate([pool, none, none, pool], 0),
     )
@@ -185,19 +188,17 @@
                 start = (4 * window + 2 * row_tap) * CG
                 pieces.append(by_col[col_tap][:, start : start + cells])
         pieces.append(jnp.zeros((8, cells), F32))
-        stacked = jnp.concatenate(pieces, axis=0)
+        piece = jnp.concatenate(pieces, axis=0)
         if window == 0:
-            stacked = stacked * above
+            piece = piece * above
         if window == 2:
-            stacked = stacked * below
-        windows.append(stacked)
-    patches = jnp.concatenate(windows, axis=1).astype(BF)
-    first_value, first_slope = gelu_both(nn(w1_ref[...], patches))
+            piece = piece * below
+        windows.append(piece.astype(BF))
+    first_value, first_slope = gelu_both(
+        nn(w1_ref[...], jnp.concatenate(windows + [jnp.zeros((16, cells), BF)], axis=0))
+    )
     yield
-    hidden = first_value.astype(BF)
-    stacked = jnp.concatenate(
-        [hidden[:, window * cells : (window + 1) * cells] for window in range(3)], axis=0
-    )
+    stacked = first_value.astype(BF)
     taps = nn(second_t_ref[...], stacked)
     lane_c = lax.broadcasted_iota(jnp.int32, (128, cells), 1) % CG
     second_pre = (
@@ -208,7 +209,7 @@
     second_value, second_slope = gelu_both(second_pre)
     yield
     feature = second_value.astype(BF)
-    patches_s[place] = patches
+    patches_s[place] = jnp.concatenate(windows, axis=1)
     columns_s[place] = stacked
     first_slope_s[place] = first_slope
     second_slope_s[place] = second_slope
@@ -241,8 +242,8 @@
     dil_ref[...] += nt(columns_s[place], shifted)
     back = nn(second_ref[...], shifted)
     yield
-    d_first_hidden = jnp.concatenate([back[0:128], back[128:256], back[256:384]], axis=1)
-    d_first = (d_first_hidden * first_slope_s[place]).astype(BF)
+    d_first = (back * first_slope_s[place]).astype(BF)
+    d_first = jnp.concatenate([d_first[0:128], d_first[128:256], d_first[256:384]], axis=1)
     fg_ref[...] += nt(patches_s[place], d_first)
 
 
@@ -325,7 +326,10 @@
             taps = eu_ref[r * 256 : (r + 1) * 256, :]
             u_ref[rows, :] = nt(up_t_ref[...], taps).astype(BF)
             ut_ref[:, rows] = nn(taps, up_ref[...]).astype(BF)
-        w1_ref[...] = nt(first_t_ref[...], ef_ref[...]).astype(BF)
+        for window in range(3):
+            w1_ref[window * 128 : (window + 1) * 128, :] = nt(
+                first_t_ref[...], ef_ref[window * 256 : (window + 1) * 256, :]
+            ).astype(BF)
         gu_ref[...] = jnp.zeros_like(gu_ref)
         gd_ref[...] = jnp.zeros_like(gd_ref)
         fg_ref[...] = jnp.zeros_like(fg_ref)
@@ -369,12 +373,12 @@
             ).astype(BF)
             wide = store[5][now, :, b * HALF : (b + 1) * HALF]
             third = nn(w_ref[...], jnp.concatenate([x_taps, wide], axis=0))
-            return x_taps, s_taps, third, nn(u_ref[...], s_taps)
-
-        def middle(entered):
-            x_taps, s_taps, third, d_hidden = entered
-            value, slope = gelu_both(third)
-            return x_taps, s_taps, value.astype(BF), (d_hidden * slope).astype(BF)
+            return [x_taps, s_taps, third]
+
+        def middle(entered, part):
+            rows = slice(part * 128, (part + 1) * 128)
+            value, slope = gelu_both(entered[2][rows])
+            return value.astype(BF), (entered[3][rows] * slope).astype(BF)
 
         def leave(b, held):
             hidden = held[2]
@@ -404,21 +408,36 @@
         entered = {}
         held = {}
         for turn in range(blocks + 2):
+            working = 0 <= turn - 1 < blocks
+            parts = []
+
+            def work():
+                if working:
+                    parts.append(middle(entered[turn - 1], len(parts)))
+
             if turn < blocks:
                 entered[turn] = enter(turn)
+            work()
+            if turn < blocks:
+                entered[turn].append(nn(u_ref[...], entered[turn][1]))
+            work()
+            b = turn - 2
+            if b >= 0:
+                combined += leave(b, held[b])
+            work()
+            if b >= 0 and b % 2 == 1:
+                pooled.append(collect(held[b - 1], held[b]))
             if turn == 1:
                 advance(back)
             if turn == 2:
                 finish(back)
-            if 0 <= turn - 1 < blocks:
-                held[turn - 1] = middle(entered.pop(turn - 1))
             if turn >= 3:
                 advance(ahead)
-            b = turn - 2
-            if b >= 0:
-                combined += leave(b, held[b])
-                if b % 2 == 1:
-                    pooled.append(collect(held[b - 1], held[b]))
+            work()
+            if working:
+                held[turn - 1] = entered[turn - 1][:2] + [
+                    jnp.concatenate([part[at] for part in parts], axis=0) for at in range(2)
+                ]
 
         out = jnp.concatenate(combined, axis=0)
         finish(ahead)
@@ -508,14 +527,14 @@
             pltpu.VMEM((512, 256), BF),
             pltpu.VMEM((512, 256), BF),
             pltpu.VMEM((256, 512), BF),
-            pltpu.VMEM((128, 80), BF),
+            pltpu.VMEM((384, 256), BF),
             pltpu.VMEM((512, 256), F32),
             pltpu.VMEM((512, 128), F32),
             pltpu.VMEM((80, 128), F32),
             pltpu.VMEM((128, cells), BF),
             pltpu.VMEM((3, 80, 3 * cells), BF),
             pltpu.VMEM((3, 384, cells), BF),
-            pltpu.VMEM((3, 128, 3 * cells), F32),
+            pltpu.VMEM((3, 384, cells), F32),
             pltpu.VMEM((3, 128, cells), F32),
             pltpu.VMEM((3, 128, cells), BF),
             pltpu.VMEM((3, 128, blocks * HALF), BF),
@@ -609,6 +628,7 @@
 
 FINAL_SLOTS = 4
 PARTS = ((0, 1152), (PROJECT_AT, 128), (UP_AT, 96), (DOWN_AT, 48), (FIRST_AT, 32))
+SHAPES = ((1152, 128), (128, 128), (4, 4, 6, 128), (3, 4, 4, 128), (3, 3, 3, 128))
 
 
 def final_kernel(chunk, rows, back_ref, pred_ref, own_ref, first_ref, last_ref, out_ref, *grads):
@@ -617,14 +637,22 @@
     @pl.when(step == 0)
     def _():
         for (start, size), grad in zip(PARTS, grads):
+            pieces = []
             at = start
             while at < start + size:
                 t = at // chunk
                 stop = min((t + 1) * chunk, start + size)
-                grad[at - start : stop - start, :] = back_ref[
-                    t, at - t * chunk : stop - t * chunk, :
-                ].astype(F32)
+                pieces.append(back_ref[t, at - t * chunk : stop - t * chunk, :].astype(F32))
                 at = stop
+            whole = jnp.concatenate(pieces, axis=0) if len(pieces) > 1 else pieces[0]
+            if len(grad.shape) == 2:
+                grad[...] = whole
+            else:
+                group = grad.shape[2]
+                for i in range(grad.shape[0]):
+                    for j in range(grad.shape[1]):
+                        at = (i * grad.shape[1] + j) * group
+                        grad[i, j] = whole[at : at + group]
 
     row = lax.broadcasted_iota(jnp.int32, (rows, HALF), 0)
     for s in range(out_ref.shape[0]):
@@ -662,9 +690,9 @@
         in_specs=[pl.BlockSpec(back.shape, lambda n: (0, 0, 0))]
         + [per_slots(a) for a in (pred, own, first, last)],
         out_specs=[per_slots(pred)]
-        + [pl.BlockSpec((size, 128), lambda n: (0, 0)) for _, size in PARTS],
+        + [pl.BlockSpec(shape, lambda n, dims=len(shape): (0,) * dims) for shape in SHAPES],
         out_shape=[jax.ShapeDtypeStruct(pred.shape, BF)]
-        + [jax.ShapeDtypeStruct((size, 128), F32) for _, size in PARTS],
+        + [jax.ShapeDtypeStruct(shape, F32) for shape in SHAPES],
         compiler_params=pltpu.CompilerParams(vmem_limit_bytes=32 * 1024 * 1024),
     )(back, pred, own, first, last)
 
@@ -774,11 +802,11 @@
     )
     return (
         prediction.reshape(fine_fields.shape),
-        first[0:27].reshape(first_weight.shape),
+        first,
         dilated.reshape(dilated_weight.shape),
         project,
-        down_grad.reshape(down_weight.shape),
-        up_grad.reshape(up_weight.shape),
+        down_grad,
+        up_grad,
     )
 
 

time: 128 us -> 125 us (0.977)
  Pallas kernels: 60 us -> 58.4 us
    pallas_call x1, Pallas kernels: 53.7 us -> 52.1 us  [run_slots(): pl.pallas_call(body, grid_spec=grid_spec, out_shape=out_shape, compiler_p...]
where the time goes in v6:
time: 125 us
  Pallas kernels  58.4 us (47%)
  starting transfers between devices  21.7 us (17%)
  waiting for transfers between devices  21.7 us (17%)
  blocking collectives  17.7 us (14%)
  local copies, waits for them, and re-layouts  2.71 us (2%)
  other arithmetic  1.52 us (1%)
    pallas_call x1, Pallas kernels, run_slots(): pl.pallas_call(body, grid_spec=grid_spec, out_shape=out_shape, compiler_p...  52.1 us
    all_to_all x3, waiting for transfers between devices, exchanged(): lax.all_to_all(value, 'tile', split_axis=0, concat_axis=0, tiled=True)  21.7 us
    all_to_all x1, blocking collectives, exchanged(): lax.all_to_all(value, 'tile', split_axis=0, concat_axis=0, tiled=True)  17.7 us
    all_to_all x3, starting transfers between devices, exchanged(): lax.all_to_all(value, 'tile', split_axis=0, concat_axis=0, tiled=True)  14.5 us
    pallas_call x1, Pallas kernels, run_early(): pl.pallas_call(body, grid=(slots // EARLY_SLOTS,), in_specs=[whole(soluti...  4.23 us
  transfers between devices with their start and end apart: 7, of which 3 were waited for; matrix products, arithmetic and copies ran while one was open for 2% of the time, Pallas kernels for 0%

profile of v6, /device:TPU:0, one launch (start us, length us, event | category | flops | bytes accessed | tf_op | source)
XLA Modules:
  0.0 124.8 jit_solution(13245426488214112537)
XLA Ops:
  0.6 4.2 %shard_map.253 = (bf16[16,64,128]{2,1,0:T(8,128)(2,1)}, bf16[16,16,256]{2,1,0:T(8,128)(2,1)}, bf16[16,16,256]{2,1,0:T(8,128)(2,1)}) custom-call(bf16[1,2,4096]{2,1,0:T(2,128)(2,1)} %refs_0_.2, s32[1,4096]{1,0:T(1,128)} %refs_1_.1, bf16[16,192,256]{2,1,0:T(8,128)(2,1)} %bitcast.24, bf16[16,192,256]{2,1,0:T(8,128)(2,1)} %bitcast.26, ...), custom_call_target="tpu_custom_call" | custom-call | tf_op jit(solution)/shard_map/pallas_call | solution.py:618
  4.9 7.4 %all-to-all-start = ((bf16[16,64,128]{2,1,0:T(8,128)(2,1)}), bf16[16,64,128]{2,1,0:T(8,128)(2,1)S(1)}, u32[]{:S(2)}, u32[]{:S(2)}) async-start(bf16[16,64,128]{2,1,0:T(8,128)(2,1)} %get-tuple-element.23), calls=%async_computation | async-start | bytes 524288 | tf_op jit(solution)/shard_map/all_to_all | solution.py:701
  12.3 2.4 %collective-permute-start = (bf16[16,16,256]{2,1,0:T(8,128)(2,1)}, bf16[16,16,256]{2,1,0:T(8,128)(2,1)S(1)}, u32[]{:S(2)}, u32[]{:S(2)}) collective-permute-start(bf16[16,16,256]{2,1,0:T(8,128)(2,1)} %get-tuple-element.24), channel_id=1, source_target_pairs={{0,1},{1,2},{2,3},{3,4},{4,5},{5,6},{6,7},{7,8},{8,9},{9,10},{10,1... | collective-permute-start | bytes 393224 | tf_op jit(solution)/shard_map/ppermute | solution.py:736
  14.8 1.3 %collective-permute-start.1 = (bf16[16,16,256]{2,1,0:T(8,128)(2,1)}, bf16[16,16,256]{2,1,0:T(8,128)(2,1)S(1)}, u32[]{:S(2)}, u32[]{:S(2)}) collective-permute-start(bf16[16,16,256]{2,1,0:T(8,128)(2,1)} %get-tuple-element.25), channel_id=1, source_target_pairs={{1,0},{2,1},{3,2},{4,3},{5,4},{6,5},{7,6},{8,7},{9,8},{10,9},{11,1... | collective-permute-start | bytes 393224 | tf_op jit(solution)/shard_map/ppermute | solution.py:737
  16.1 0.0 copy-start.3
  16.1 0.0 copy-start.4
  16.1 0.0 copy-start.6
  16.2 0.0 copy-start.7
  16.2 0.0 copy-start.8
  16.2 0.0 copy-start.9
  16.2 0.2 copy.45
  16.4 0.3 copy.46
  16.7 5.6 %all-to-all-done.refs_2_.refs_3_.refs_4_.refs_5_.refs_6_ = bf16[16,64,128]{2,1,0:T(8,128)(2,1)S(1)} async-done(((bf16[16,64,128]{2,1,0:T(8,128)(2,1)}), bf16[16,64,128]{2,1,0:T(8,128)(2,1)S(1)}, u32[]{:S(2)}, u32[]{:S(2)}) %all-to-all-start) | async-done | bytes 262176 | tf_op jit(solution)/shard_map/all_to_all | solution.py:701
  22.4 1.0 select_reduce_fusion.1
  23.4 3.5 %all-to-all-start.1 = ((f32[16,16,128]{2,1,0:T(8,128)}), f32[16,16,128]{2,1,0:T(8,128)S(1)}, u32[]{:S(2)}, u32[]{:S(2)}) async-start(f32[16,16,128]{2,1,0:T(8,128)} %select_reduce_fusion.1), calls=%async_computation.1 | async-start | bytes 262144 | tf_op jit(solution)/shard_map/all_to_all | solution.py:701
  26.9 0.9 copy_bitcast_fusion
  27.8 0.1 copy.44
  27.9 0.1 copy.48
  28.1 0.1 copy.50
  28.2 0.1 copy.47
  28.4 6.4 %all-to-all-done.1.refs_11_ = f32[16,16,128]{2,1,0:T(8,128)S(1)} async-done(((f32[16,16,128]{2,1,0:T(8,128)}), f32[16,16,128]{2,1,0:T(8,128)S(1)}, u32[]{:S(2)}, u32[]{:S(2)}) %all-to-all-start.1) | async-done | bytes 131104 | tf_op jit(solution)/shard_map/all_to_all | solution.py:701
  34.9 52.1 %shard_map.254 = (f32[16,192,256]{2,1,0:T(8,128)}, f32[16,8,256]{2,1,0:T(8,128)S(1)}, f32[16,8,256]{2,1,0:T(8,128)S(1)}, f32[16,8,256]{2,1,0:T(8,128)S(1)}, bf16[16,112,128]{2,1,0:T(8,128)(2,1)}) custom-call(s32[16]{0:T(128)S(1)} %copy-done.2, s32[1]{0:T(128)} %bitcast.refs_1_, bf16[16,64,128]{2,1,0:T(8,128)(2,1)} %copy-done.11, ...), custom_call_target="tpu_custom_call" | custom-call | flops 32000000000 | bytes 16000000 | tf_op jit(solution)/shard_map/pallas_call | solution.py:547
  87.0 3.6 %all-to-all-start.2 = ((bf16[16,112,128]{2,1,0:T(8,128)(2,1)}), bf16[16,112,128]{2,1,0:T(8,128)(2,1)S(1)}, u32[]{:S(2)}, u32[]{:S(2)}) async-start(bf16[16,112,128]{2,1,0:T(8,128)(2,1)} %get-tuple-element.26), calls=%async_computation.2 | async-start | bytes 917504 | tf_op jit(solution)/shard_map/all_to_all | solution.py:701
  90.6 2.2 %collective-permute-start.2 = (f32[16,8,256]{2,1,0:T(8,128)S(1)}, f32[16,8,256]{2,1,0:T(8,128)S(1)}, u32[]{:S(2)}, u32[]{:S(2)}) collective-permute-start(f32[16,8,256]{2,1,0:T(8,128)S(1)} %get-tuple-element.27), channel_id=1, source_target_pairs={{0,1},{1,2},{2,3},{3,4},{4,5},{5,6},{6,7},{7,8},{8,9},{9,10},{10,1... | collective-permute-start | bytes 393224 | tf_op jit(solution)/shard_map/ppermute | solution.py:785
  92.8 1.3 %collective-permute-start.3 = (f32[16,8,256]{2,1,0:T(8,128)S(1)}, f32[16,8,256]{2,1,0:T(8,128)S(1)}, u32[]{:S(2)}, u32[]{:S(2)}) collective-permute-start(f32[16,8,256]{2,1,0:T(8,128)S(1)} %get-tuple-element.28), channel_id=1, source_target_pairs={{1,0},{2,1},{3,2},{4,3},{5,4},{6,5},{7,6},{8,7},{9,8},{10,9},{11,1... | collective-permute-start | bytes 393224 | tf_op jit(solution)/shard_map/ppermute | solution.py:786
  94.1 9.7 %all-to-all-done.2 = bf16[16,112,128]{2,1,0:T(8,128)(2,1)S(1)} async-done(((bf16[16,112,128]{2,1,0:T(8,128)(2,1)}), bf16[16,112,128]{2,1,0:T(8,128)(2,1)S(1)}, u32[]{:S(2)}, u32[]{:S(2)}) %all-to-all-start.2) | async-done | bytes 458784 | tf_op jit(solution)/shard_map/all_to_all | solution.py:701
  103.8 0.1 convert_element_type.15
  103.9 0.3 select_reduce_fusion
  104.3 0.1 broadcast_in_dim.41
  104.4 17.7 %all_to_all.20.refs_0_ = bf16[16,112,128]{2,1,0:T(8,128)(2,1)S(1)} all-to-all(bf16[16,112,128]{2,1,0:T(8,128)(2,1)S(1)} %pad_maximum_fusion), channel_id=1, replica_groups=mesh['groups'=2,'tile'=16] {'tile'}, dimensions={0} | all-to-all | bytes 917504 | tf_op jit(solution)/shard_map/all_to_all | solution.py:701
  122.1 2.1 %shard_map.255 = (bf16[16,192,256]{2,1,0:T(8,128)(2,1)}, f32[1152,128]{1,0:T(8,128)}, f32[128,128]{1,0:T(8,128)}, f32[4,4,6,128]{3,2,1,0:T(8,128)S(1)}, f32[3,4,...) custom-call(bf16[16,112,128]{2,1,0:T(8,128)(2,1)S(1)} %all_to_all.20.refs_0_, f32[16,192,256]{2,1,0:T(8,128)S(1)} %copy-done, ...), custom_call_target="tpu_custom_call" | custom-call | tf_op jit(solution)/shard_map/pallas_call | solution.py:687
  124.2 0.6 copy.51
  (39 shorter events, 0.3 us)
Async XLA Ops:
  0.6 15.4 %copy-start.10 = (bf16[3,3,128,128]{3,2,1,0:T(8,128)(2,1)S(1)}, bf16[3,3,128,128]{3,2,1,0:T(8,128)(2,1)}, u32[]{:S(2)}) copy-start(bf16[3,3,128,128]{3,2,1,0:T(8,128)(2,1)} %param.28) | copy-start | bytes 884740
  4.9 17.5 %all-to-all-start = ((bf16[16,64,128]{2,1,0:T(8,128)(2,1)}), bf16[16,64,128]{2,1,0:T(8,128)(2,1)S(1)}, u32[]{:S(2)}, u32[]{:S(2)}) async-start(bf16[16,64,128]{2,1,0:T(8,128)(2,1)} %get-tuple-element.23), calls=%async_computation | async-start | bytes 524288 | tf_op jit(solution)/shard_map/all_to_all | solution.py:701
  12.3 15.5 %copy-start.14 = (bf16[3,3,3,128]{3,2,1,0:T(4,128)(2,1)S(1)}, bf16[3,3,3,128]{3,2,1,0:T(4,128)(2,1)}, u32[]{:S(2)}) copy-start(bf16[3,3,3,128]{3,2,1,0:T(4,128)(2,1)} %param.27) | copy-start | bytes 20740
  12.3 15.7 %copy-start.13 = (bf16[3,4,4,128]{3,2,1,0:T(4,128)(2,1)S(1)}, bf16[3,4,4,128]{3,2,1,0:T(4,128)(2,1)}, u32[]{:S(2)}) copy-start(bf16[3,4,4,128]{3,2,1,0:T(4,128)(2,1)} %param.30) | copy-start | bytes 36868
  12.3 15.8 %copy-start.12 = (bf16[4,4,6,128]{3,1,2,0:T(4,128)(2,1)S(1)}, bf16[4,4,6,128]{3,1,2,0:T(4,128)(2,1)}, u32[]{:S(2)}) copy-start(bf16[4,4,6,128]{3,1,2,0:T(4,128)(2,1)} %param.31) | copy-start | bytes 73732
  12.3 16.1 %collective-permute-start = (bf16[16,16,256]{2,1,0:T(8,128)(2,1)}, bf16[16,16,256]{2,1,0:T(8,128)(2,1)S(1)}, u32[]{:S(2)}, u32[]{:S(2)}) collective-permute-start(bf16[16,16,256]{2,1,0:T(8,128)(2,1)} %get-tuple-element.24), channel_id=1, source_target_pairs={{0,1},{1,2},{2,3},{3,4},{4,5},{5,6},{6,7},{7,8},{8,9},{9,10},{10,1... | collective-permute-start | bytes 393224 | tf_op jit(solution)/shard_map/ppermute | solution.py:736
  14.8 13.6 %collective-permute-start.1 = (bf16[16,16,256]{2,1,0:T(8,128)(2,1)}, bf16[16,16,256]{2,1,0:T(8,128)(2,1)S(1)}, u32[]{:S(2)}, u32[]{:S(2)}) collective-permute-start(bf16[16,16,256]{2,1,0:T(8,128)(2,1)} %get-tuple-element.25), channel_id=1, source_target_pairs={{1,0},{2,1},{3,2},{4,3},{5,4},{6,5},{7,6},{8,7},{9,8},{10,9},{11,1... | collective-permute-start | bytes 393224 | tf_op jit(solution)/shard_map/ppermute | solution.py:737
  16.1 12.2 %copy-start.1 = (bf16[128,128]{1,0:T(8,128)(2,1)S(1)}, bf16[128,128]{1,0:T(8,128)(2,1)}, u32[]{:S(2)}) copy-start(bf16[128,128]{1,0:T(8,128)(2,1)} %refs_25_.1) | copy-start | bytes 98308
  16.1 18.7 %copy-start.2 = (s32[16]{0:T(128)S(1)}, s32[16]{0:T(128)}, u32[]{:S(2)}) copy-start(s32[16]{0:T(128)} %refs_0_.3) | copy-start | bytes 196
  16.1 18.7 %copy-start.3 = (bf16[768,32]{1,0:T(8,128)(2,1)S(1)}, bf16[768,32]{1,0:T(8,128)(2,1)}, u32[]{:S(2)}) copy-start(bf16[768,32]{1,0:T(8,128)(2,1)} %constant.42.clone.refs_19_) | copy-start | bytes 147460
  16.1 18.7 %copy-start.4 = (bf16[96,1024]{1,0:T(8,128)(2,1)S(1)}, bf16[96,1024]{1,0:T(8,128)(2,1)}, u32[]{:S(2)}) copy-start(bf16[96,1024]{1,0:T(8,128)(2,1)} %constant.41.clone.refs_18_) | copy-start | bytes 589828
  16.1 18.7 %copy-start.5 = (bf16[256,256]{1,0:T(8,128)(2,1)S(1)}, bf16[256,256]{1,0:T(8,128)(2,1)}, u32[]{:S(2)}) copy-start(bf16[256,256]{1,0:T(8,128)(2,1)} %constant.44.clone.refs_21_) | copy-start | bytes 393220
  16.1 18.7 %copy-start.6 = (bf16[512,48]{1,0:T(8,128)(2,1)S(1)}, bf16[512,48]{1,0:T(8,128)(2,1)}, u32[]{:S(2)}) copy-start(bf16[512,48]{1,0:T(8,128)(2,1)} %constant.38.clone.refs_15_) | copy-start | bytes 147460
  16.2 18.7 %copy-start.7 = (bf16[256,256]{1,0:T(8,128)(2,1)S(1)}, bf16[256,256]{1,0:T(8,128)(2,1)}, u32[]{:S(2)}) copy-start(bf16[256,256]{1,0:T(8,128)(2,1)} %constant.35.clone.refs_12_) | copy-start | bytes 393220
  16.2 18.7 %copy-start.8 = (bf16[48,512]{1,0:T(8,128)(2,1)S(1)}, bf16[48,512]{1,0:T(8,128)(2,1)}, u32[]{:S(2)}) copy-start(bf16[48,512]{1,0:T(8,128)(2,1)} %constant.40.clone.refs_17_) | copy-start | bytes 147460
  16.2 18.7 %copy-start.9 = (bf16[32,80]{1,0:T(8,128)(2,1)S(1)}, bf16[32,80]{1,0:T(8,128)(2,1)}, u32[]{:S(2)}) copy-start(bf16[32,80]{1,0:T(8,128)(2,1)} %constant.43.clone.refs_20_) | copy-start | bytes 15364
  22.3 12.5 %copy-start.11 = (bf16[16,64,128]{2,1,0:T(8,128)(2,1)}, bf16[16,64,128]{2,1,0:T(8,128)(2,1)S(1)}, u32[]{:S(2)}) copy-start(bf16[16,64,128]{2,1,0:T(8,128)(2,1)S(1)} %all-to-all-done.refs_2_.refs_3_.refs_4_.refs_5_.refs_6_) | copy-start | bytes 786436
  23.4 11.4 %all-to-all-start.1 = ((f32[16,16,128]{2,1,0:T(8,128)}), f32[16,16,128]{2,1,0:T(8,128)S(1)}, u32[]{:S(2)}, u32[]{:S(2)}) async-start(f32[16,16,128]{2,1,0:T(8,128)} %select_reduce_fusion.1), calls=%async_computation.1 | async-start | bytes 262144 | tf_op jit(solution)/shard_map/all_to_all | solution.py:701
  87.0 16.8 %all-to-all-start.2 = ((bf16[16,112,128]{2,1,0:T(8,128)(2,1)}), bf16[16,112,128]{2,1,0:T(8,128)(2,1)S(1)}, u32[]{:S(2)}, u32[]{:S(2)}) async-start(bf16[16,112,128]{2,1,0:T(8,128)(2,1)} %get-tuple-element.26), calls=%async_computation.2 | async-start | bytes 917504 | tf_op jit(solution)/shard_map/all_to_all | solution.py:701
  90.6 13.3 %collective-permute-start.2 = (f32[16,8,256]{2,1,0:T(8,128)S(1)}, f32[16,8,256]{2,1,0:T(8,128)S(1)}, u32[]{:S(2)}, u32[]{:S(2)}) collective-permute-start(f32[16,8,256]{2,1,0:T(8,128)S(1)} %get-tuple-element.27), channel_id=1, source_target_pairs={{0,1},{1,2},{2,3},{3,4},{4,5},{5,6},{6,7},{7,8},{8,9},{9,10},{10,1... | collective-permute-start | bytes 393224 | tf_op jit(solution)/shard_map/ppermute | solution.py:785
  92.8 11.1 %collective-permute-start.3 = (f32[16,8,256]{2,1,0:T(8,128)S(1)}, f32[16,8,256]{2,1,0:T(8,128)S(1)}, u32[]{:S(2)}, u32[]{:S(2)}) collective-permute-start(f32[16,8,256]{2,1,0:T(8,128)S(1)} %get-tuple-element.28), channel_id=1, source_target_pairs={{1,0},{2,1},{3,2},{4,3},{5,4},{6,5},{7,6},{8,7},{9,8},{10,9},{11,1... | collective-permute-start | bytes 393224 | tf_op jit(solution)/shard_map/ppermute | solution.py:786
  103.8 18.3 %copy-start = (f32[16,192,256]{2,1,0:T(8,128)S(1)}, f32[16,192,256]{2,1,0:T(8,128)}, u32[]{:S(2)}) copy-start(f32[16,192,256]{2,1,0:T(8,128)} %get-tuple-element.30.refs_1_) | copy-start | bytes 9437188

commit v7 on v6

--- a/solution.py
+++ b/solution.py
@@ -143,10 +143,13 @@
         ex=ex.reshape(512, 48),
         eu=eu.reshape(1024, 96),
         ext=np.concatenate(list(np.swapaxes(ex, 1, 2)), 1),
-        eut=np.concatenate(list(np.swapaxes(eu, 1, 2)), 1),
+        eut=np.concatenate(list(np.swapaxes(eu, 1, 2)), 1)
+        .reshape(4, 4, 6, 1024)
+        .swapaxes(1, 2)
+        .reshape(96, 1024),
         ef=ef_all.reshape(768, 32),
         eft=ef.T,
-        pool_both=np.concatenate([pool, none, none, pool], 0),
+        pool_both=np.concatenate([pool, none, none, pool, pool, pool], 0),
     )
 
 
@@ -164,7 +167,7 @@
     return jnp.where(keep(lane), pltpu.roll(value, shift % width, 1), 0.0)
 
 
-def coarse_forward(blocks, tile, coarse_ref, w1_ref, second_t_ref, spread_ref, store, place):
+def coarse_forward(blocks, tile, coarse_ref, w1_ref, second_t_ref, project_t_ref, store, place):
     patches_s, columns_s, first_slope_s, second_slope_s, feature_s, wide_s = store
     cells = blocks * CG
     by_segment = coarse_ref[0, 0:SENT_INPUT, :].astype(F32)
@@ -214,13 +217,16 @@
     first_slope_s[place] = first_slope
     second_slope_s[place] = second_slope
     feature_s[place] = feature
-    pairs = [feature[:, at * 128 : (at + 1) * 128] for at in range(blocks // 2)]
-    pairs = jnp.concatenate(pairs, axis=0) if blocks > 2 else pairs[0]
-    for parity in range(2):
-        wide = nn(pairs, spread_ref[parity * 128 : (parity + 1) * 128, :]).astype(BF)
-        for at in range(blocks // 2):
-            b = 2 * at + parity
-            wide_s[place, :, b * HALF : (b + 1) * HALF] = wide[at * 128 : (at + 1) * 128]
+    projected = nn(project_t_ref[...], feature)
+    left = lax.broadcasted_iota(jnp.int32, (128, 128), 1) < CG
+    for at in range(blocks // 2):
+        pair = projected[:, at * 128 : (at + 1) * 128]
+        high = pair.astype(BF).astype(F32)
+        low = pair - high
+        even = jnp.where(left, high, pltpu.roll(low, CG, 1))
+        odd = jnp.where(left, pltpu.roll(high, CG, 1), low)
+        wide_s[place, at * 256 : at * 256 + 128, :] = even.astype(BF)
+        wide_s[place, at * 256 + 128 : at * 256 + 256, :] = odd.astype(BF)
 
 
 def coarse_backward(blocks, d_project, project_ref, second_ref, store, place, dil_ref, pg_ref, fg_ref):
@@ -309,7 +315,7 @@
 
     def forward(source, place):
         return coarse_forward(
-            blocks, tile, source, w1_ref, second_t_ref, spread_ref, store, place
+            blocks, tile, source, w1_ref, second_t_ref, project_t_ref, store, place
         )
 
     def backward(place):
@@ -321,8 +327,7 @@
     def _():
         for r in range(4):
             rows = slice(r * 128, (r + 1) * 128)
-            w_ref[rows, 0:128] = nt(down_t_ref[...], ex_ref[rows, :]).astype(BF)
-            w_ref[rows, 128:256] = project_t_ref[...]
+            w_ref[rows, :] = nt(down_t_ref[...], ex_ref[rows, :]).astype(BF)
             taps = eu_ref[r * 256 : (r + 1) * 256, :]
             u_ref[rows, :] = nt(up_t_ref[...], taps).astype(BF)
             ut_ref[:, rows] = nn(taps, up_ref[...]).astype(BF)
@@ -371,8 +376,11 @@
             s_taps = jnp.concatenate(
                 [s0, s1, moved(s1, 1, lane64, not_first), moved(s0, -1, lane64, not_last)], axis=0
             ).astype(BF)
-            wide = store[5][now, :, b * HALF : (b + 1) * HALF]
-            third = nn(w_ref[...], jnp.concatenate([x_taps, wide], axis=0))
+            coarse_part = store[5][now, b * 128 : (b + 1) * 128, :]
+            left = jnp.concatenate(
+                [w_ref[...], jnp.concatenate([coarse_part] * 4, axis=0)], axis=1
+            )
+            third = nn(left, jnp.concatenate([x_taps, spread_ref[256:384, :]], axis=0))
             return [x_taps, s_taps, third]
 
         def middle(entered, part):
@@ -524,7 +532,7 @@
         scratch_shapes=[
             pltpu.VMEM((384, 384), F32),
             pltpu.VMEM((128, 128), F32),
-            pltpu.VMEM((512, 256), BF),
+            pltpu.VMEM((512, 128), BF),
             pltpu.VMEM((512, 256), BF),
             pltpu.VMEM((256, 512), BF),
             pltpu.VMEM((384, 256), BF),
@@ -537,7 +545,7 @@
             pltpu.VMEM((3, 384, cells), F32),
             pltpu.VMEM((3, 128, cells), F32),
             pltpu.VMEM((3, 128, cells), BF),
-            pltpu.VMEM((3, 128, blocks * HALF), BF),
+            pltpu.VMEM((3, blocks * 128, 128), BF),
         ],
     )
 
@@ -628,7 +636,7 @@
 
 FINAL_SLOTS = 4
 PARTS = ((0, 1152), (PROJECT_AT, 128), (UP_AT, 96), (DOWN_AT, 48), (FIRST_AT, 32))
-SHAPES = ((1152, 128), (128, 128), (4, 4, 6, 128), (3, 4, 4, 128), (3, 3, 3, 128))
+SHAPES = ((1152, 128), (128, 128), (4, 6, 4, 128), (3, 4, 4, 128), (3, 3, 3, 128))
 
 
 def final_kernel(chunk, rows, back_ref, pred_ref, own_ref, first_ref, last_ref, out_ref, *grads):
@@ -806,7 +814,7 @@
         dilated.reshape(dilated_weight.shape),
         project,
         down_grad,
-        up_grad,
+        jnp.swapaxes(up_grad, 1, 2),
     )
 
 

time: 125 us -> 125 us (level)
  no operation moved by 1% of the time
where the time goes in v7:
time: 125 us; the launch traced here: 124 us
  Pallas kernels  58.7 us (47%)
  starting transfers between devices  21.7 us (17%)
  waiting for transfers between devices  21.7 us (17%)
  blocking collectives  17.7 us (14%)
  local copies, waits for them, and re-layouts  2.07 us (2%)
  other arithmetic  1.52 us (1%)
    pallas_call x1, Pallas kernels, run_slots(): pl.pallas_call(body, grid_spec=grid_spec, out_shape=out_shape, compiler_p...  52.4 us
    all_to_all x3, waiting for transfers between devices, exchanged(): lax.all_to_all(value, 'tile', split_axis=0, concat_axis=0, tiled=True)  21.7 us
    all_to_all x1, blocking collectives, exchanged(): lax.all_to_all(value, 'tile', split_axis=0, concat_axis=0, tiled=True)  17.7 us
    all_to_all x3, starting transfers between devices, exchanged(): lax.all_to_all(value, 'tile', split_axis=0, concat_axis=0, tiled=True)  14.5 us
    pallas_call x1, Pallas kernels, run_early(): pl.pallas_call(body, grid=(slots // EARLY_SLOTS,), in_specs=[whole(soluti...  4.23 us
  transfers between devices with their start and end apart: 7, of which 3 were waited for; matrix products, arithmetic and copies ran while one was open for 2% of the time, Pallas kernels for 0%

profile of v7, /device:TPU:0, one launch (start us, length us, event | category | flops | bytes accessed | tf_op | source)
XLA Modules:
  0.0 124.4 jit_solution(653765341273642480)
XLA Ops:
  0.6 4.2 %shard_map.253 = (bf16[16,64,128]{2,1,0:T(8,128)(2,1)}, bf16[16,16,256]{2,1,0:T(8,128)(2,1)}, bf16[16,16,256]{2,1,0:T(8,128)(2,1)}) custom-call(bf16[1,2,4096]{2,1,0:T(2,128)(2,1)} %refs_0_.2, s32[1,4096]{1,0:T(1,128)} %refs_1_.1, bf16[16,192,256]{2,1,0:T(8,128)(2,1)} %bitcast.25, bf16[16,192,256]{2,1,0:T(8,128)(2,1)} %bitcast.27, ...), custom_call_target="tpu_custom_call" | custom-call | tf_op jit(solution)/shard_map/pallas_call | solution.py:626
  4.9 7.4 %all-to-all-start = ((bf16[16,64,128]{2,1,0:T(8,128)(2,1)}), bf16[16,64,128]{2,1,0:T(8,128)(2,1)S(1)}, u32[]{:S(2)}, u32[]{:S(2)}) async-start(bf16[16,64,128]{2,1,0:T(8,128)(2,1)} %get-tuple-element.23), calls=%async_computation | async-start | bytes 524288 | tf_op jit(solution)/shard_map/all_to_all | solution.py:709
  12.3 2.4 %collective-permute-start = (bf16[16,16,256]{2,1,0:T(8,128)(2,1)}, bf16[16,16,256]{2,1,0:T(8,128)(2,1)S(1)}, u32[]{:S(2)}, u32[]{:S(2)}) collective-permute-start(bf16[16,16,256]{2,1,0:T(8,128)(2,1)} %get-tuple-element.24), channel_id=1, source_target_pairs={{0,1},{1,2},{2,3},{3,4},{4,5},{5,6},{6,7},{7,8},{8,9},{9,10},{10,1... | collective-permute-start | bytes 393224 | tf_op jit(solution)/shard_map/ppermute | solution.py:744
  14.8 1.3 %collective-permute-start.1 = (bf16[16,16,256]{2,1,0:T(8,128)(2,1)}, bf16[16,16,256]{2,1,0:T(8,128)(2,1)S(1)}, u32[]{:S(2)}, u32[]{:S(2)}) collective-permute-start(bf16[16,16,256]{2,1,0:T(8,128)(2,1)} %get-tuple-element.25), channel_id=1, source_target_pairs={{1,0},{2,1},{3,2},{4,3},{5,4},{6,5},{7,6},{8,7},{9,8},{10,9},{11,1... | collective-permute-start | bytes 393224 | tf_op jit(solution)/shard_map/ppermute | solution.py:745
  16.1 0.0 copy-start.3
  16.1 0.0 copy-start.4
  16.1 0.0 copy-start.5
  16.1 0.0 copy-start.6
  16.2 0.0 copy-start.7
  16.2 0.0 copy-start.8
  16.2 0.0 copy-start.9
  16.2 0.2 copy.43
  16.4 0.3 copy.44
  16.7 5.6 %all-to-all-done.refs_2_.refs_3_.refs_4_.refs_5_.refs_6_ = bf16[16,64,128]{2,1,0:T(8,128)(2,1)S(1)} async-done(((bf16[16,64,128]{2,1,0:T(8,128)(2,1)}), bf16[16,64,128]{2,1,0:T(8,128)(2,1)S(1)}, u32[]{:S(2)}, u32[]{:S(2)}) %all-to-all-start) | async-done | bytes 262176 | tf_op jit(solution)/shard_map/all_to_all | solution.py:709
  22.4 1.0 select_reduce_fusion.1
  23.4 3.5 %all-to-all-start.1 = ((f32[16,16,128]{2,1,0:T(8,128)}), f32[16,16,128]{2,1,0:T(8,128)S(1)}, u32[]{:S(2)}, u32[]{:S(2)}) async-start(f32[16,16,128]{2,1,0:T(8,128)} %select_reduce_fusion.1), calls=%async_computation.1 | async-start | bytes 262144 | tf_op jit(solution)/shard_map/all_to_all | solution.py:709
  26.9 0.9 copy_bitcast_fusion
  27.8 0.1 copy.42
  27.9 0.1 copy.46
  28.1 0.1 copy.48
  28.2 0.1 copy.45
  28.4 6.4 %all-to-all-done.1.refs_11_ = f32[16,16,128]{2,1,0:T(8,128)S(1)} async-done(((f32[16,16,128]{2,1,0:T(8,128)}), f32[16,16,128]{2,1,0:T(8,128)S(1)}, u32[]{:S(2)}, u32[]{:S(2)}) %all-to-all-start.1) | async-done | bytes 131104 | tf_op jit(solution)/shard_map/all_to_all | solution.py:709
  34.9 52.4 %shard_map.254 = (f32[16,192,256]{2,1,0:T(8,128)}, f32[16,8,256]{2,1,0:T(8,128)S(1)}, f32[16,8,256]{2,1,0:T(8,128)S(1)}, f32[16,8,256]{2,1,0:T(8,128)S(1)}, bf16[16,112,128]{2,1,0:T(8,128)(2,1)}) custom-call(s32[16]{0:T(128)S(1)} %copy-done.2, s32[1]{0:T(128)} %bitcast.refs_1_, bf16[16,64,128]{2,1,0:T(8,128)(2,1)} %copy-done.11, ...), custom_call_target="tpu_custom_call" | custom-call | flops 32000000000 | bytes 16000000 | tf_op jit(solution)/shard_map/pallas_call | solution.py:555
  87.2 3.6 %all-to-all-start.2 = ((bf16[16,112,128]{2,1,0:T(8,128)(2,1)}), bf16[16,112,128]{2,1,0:T(8,128)(2,1)S(1)}, u32[]{:S(2)}, u32[]{:S(2)}) async-start(bf16[16,112,128]{2,1,0:T(8,128)(2,1)} %get-tuple-element.26), calls=%async_computation.2 | async-start | bytes 917504 | tf_op jit(solution)/shard_map/all_to_all | solution.py:709
  90.8 2.2 %collective-permute-start.2 = (f32[16,8,256]{2,1,0:T(8,128)S(1)}, f32[16,8,256]{2,1,0:T(8,128)S(1)}, u32[]{:S(2)}, u32[]{:S(2)}) collective-permute-start(f32[16,8,256]{2,1,0:T(8,128)S(1)} %get-tuple-element.27), channel_id=1, source_target_pairs={{0,1},{1,2},{2,3},{3,4},{4,5},{5,6},{6,7},{7,8},{8,9},{9,10},{10,1... | collective-permute-start | bytes 393224 | tf_op jit(solution)/shard_map/ppermute | solution.py:793
  93.0 1.3 %collective-permute-start.3 = (f32[16,8,256]{2,1,0:T(8,128)S(1)}, f32[16,8,256]{2,1,0:T(8,128)S(1)}, u32[]{:S(2)}, u32[]{:S(2)}) collective-permute-start(f32[16,8,256]{2,1,0:T(8,128)S(1)} %get-tuple-element.28), channel_id=1, source_target_pairs={{1,0},{2,1},{3,2},{4,3},{5,4},{6,5},{7,6},{8,7},{9,8},{10,9},{11,1... | collective-permute-start | bytes 393224 | tf_op jit(solution)/shard_map/ppermute | solution.py:794
  94.3 9.7 %all-to-all-done.2 = bf16[16,112,128]{2,1,0:T(8,128)(2,1)S(1)} async-done(((bf16[16,112,128]{2,1,0:T(8,128)(2,1)}), bf16[16,112,128]{2,1,0:T(8,128)(2,1)S(1)}, u32[]{:S(2)}, u32[]{:S(2)}) %all-to-all-start.2) | async-done | bytes 458784 | tf_op jit(solution)/shard_map/all_to_all | solution.py:709
  104.0 0.1 convert_element_type.15
  104.2 0.3 select_reduce_fusion
  104.5 0.1 broadcast_in_dim.41
  104.6 17.7 %all_to_all.20.refs_0_ = bf16[16,112,128]{2,1,0:T(8,128)(2,1)S(1)} all-to-all(bf16[16,112,128]{2,1,0:T(8,128)(2,1)S(1)} %pad_maximum_fusion), channel_id=1, replica_groups=mesh['groups'=2,'tile'=16] {'tile'}, dimensions={0} | all-to-all | bytes 917504 | tf_op jit(solution)/shard_map/all_to_all | solution.py:709
  122.3 2.1 %shard_map.255 = (bf16[16,192,256]{2,1,0:T(8,128)(2,1)}, f32[1152,128]{1,0:T(8,128)}, f32[128,128]{1,0:T(8,128)}, f32[4,6,4,128]{3,2,1,0:T(4,128)}, f32[3,4,4,128]{3,2,1,0:T(4,128)}, /*index=5*/f32[3,3,3,128]{3,2,1,0:T(4,128)}) custom-call(bf16[16,112,128]{2,1,0:T(8,128)(2,1)S(1)} %all_to_all.20.refs_0_, f32[16,192,256]{2,1,0:T(8,128)S(1)} %copy-done, ...), custom_call_target="tpu_custom_call" | custom-call | tf_op jit(solution)/shard_map/pallas_call | solution.py:695
  (38 shorter events, 0.3 us)
Async XLA Ops:
  0.6 15.4 %copy-start.10 = (bf16[3,3,128,128]{3,2,1,0:T(8,128)(2,1)S(1)}, bf16[3,3,128,128]{3,2,1,0:T(8,128)(2,1)}, u32[]{:S(2)}) copy-start(bf16[3,3,128,128]{3,2,1,0:T(8,128)(2,1)} %param.28) | copy-start | bytes 884740
  4.9 17.5 %all-to-all-start = ((bf16[16,64,128]{2,1,0:T(8,128)(2,1)}), bf16[16,64,128]{2,1,0:T(8,128)(2,1)S(1)}, u32[]{:S(2)}, u32[]{:S(2)}) async-start(bf16[16,64,128]{2,1,0:T(8,128)(2,1)} %get-tuple-element.23), calls=%async_computation | async-start | bytes 524288 | tf_op jit(solution)/shard_map/all_to_all | solution.py:709
  12.3 15.5 %copy-start.14 = (bf16[3,3,3,128]{3,2,1,0:T(4,128)(2,1)S(1)}, bf16[3,3,3,128]{3,2,1,0:T(4,128)(2,1)}, u32[]{:S(2)}) copy-start(bf16[3,3,3,128]{3,2,1,0:T(4,128)(2,1)} %param.27) | copy-start | bytes 20740
  12.3 15.7 %copy-start.13 = (bf16[3,4,4,128]{3,2,1,0:T(4,128)(2,1)S(1)}, bf16[3,4,4,128]{3,2,1,0:T(4,128)(2,1)}, u32[]{:S(2)}) copy-start(bf16[3,4,4,128]{3,2,1,0:T(4,128)(2,1)} %param.30) | copy-start | bytes 36868
  12.3 15.8 %copy-start.12 = (bf16[4,4,6,128]{3,1,2,0:T(4,128)(2,1)S(1)}, bf16[4,4,6,128]{3,1,2,0:T(4,128)(2,1)}, u32[]{:S(2)}) copy-start(bf16[4,4,6,128]{3,1,2,0:T(4,128)(2,1)} %param.31) | copy-start | bytes 73732
  12.3 16.1 %collective-permute-start = (bf16[16,16,256]{2,1,0:T(8,128)(2,1)}, bf16[16,16,256]{2,1,0:T(8,128)(2,1)S(1)}, u32[]{:S(2)}, u32[]{:S(2)}) collective-permute-start(bf16[16,16,256]{2,1,0:T(8,128)(2,1)} %get-tuple-element.24), channel_id=1, source_target_pairs={{0,1},{1,2},{2,3},{3,4},{4,5},{5,6},{6,7},{7,8},{8,9},{9,10},{10,1... | collective-permute-start | bytes 393224 | tf_op jit(solution)/shard_map/ppermute | solution.py:744
  14.8 13.6 %collective-permute-start.1 = (bf16[16,16,256]{2,1,0:T(8,128)(2,1)}, bf16[16,16,256]{2,1,0:T(8,128)(2,1)S(1)}, u32[]{:S(2)}, u32[]{:S(2)}) collective-permute-start(bf16[16,16,256]{2,1,0:T(8,128)(2,1)} %get-tuple-element.25), channel_id=1, source_target_pairs={{1,0},{2,1},{3,2},{4,3},{5,4},{6,5},{7,6},{8,7},{9,8},{10,9},{11,1... | collective-permute-start | bytes 393224 | tf_op jit(solution)/shard_map/ppermute | solution.py:745
  16.1 12.2 %copy-start.1 = (bf16[128,128]{1,0:T(8,128)(2,1)S(1)}, bf16[128,128]{1,0:T(8,128)(2,1)}, u32[]{:S(2)}) copy-start(bf16[128,128]{1,0:T(8,128)(2,1)} %refs_25_.1) | copy-start | bytes 98308
  16.1 18.7 %copy-start.2 = (s32[16]{0:T(128)S(1)}, s32[16]{0:T(128)}, u32[]{:S(2)}) copy-start(s32[16]{0:T(128)} %refs_0_.3) | copy-start | bytes 196
  16.1 18.7 %copy-start.3 = (bf16[384,256]{1,0:T(8,128)(2,1)S(1)}, bf16[384,256]{1,0:T(8,128)(2,1)}, u32[]{:S(2)}) copy-start(bf16[384,256]{1,0:T(8,128)(2,1)} %constant.44.clone.refs_21_) | copy-start | bytes 589828
  16.1 18.7 %copy-start.4 = (bf16[768,32]{1,0:T(8,128)(2,1)S(1)}, bf16[768,32]{1,0:T(8,128)(2,1)}, u32[]{:S(2)}) copy-start(bf16[768,32]{1,0:T(8,128)(2,1)} %constant.42.clone.refs_19_) | copy-start | bytes 147460
  16.1 18.7 %copy-start.5 = (bf16[96,1024]{1,0:T(8,128)(2,1)S(1)}, bf16[96,1024]{1,0:T(8,128)(2,1)}, u32[]{:S(2)}) copy-start(bf16[96,1024]{1,0:T(8,128)(2,1)} %constant.41.clone.refs_18_) | copy-start | bytes 589828
  16.1 18.7 %copy-start.6 = (bf16[512,48]{1,0:T(8,128)(2,1)S(1)}, bf16[512,48]{1,0:T(8,128)(2,1)}, u32[]{:S(2)}) copy-start(bf16[512,48]{1,0:T(8,128)(2,1)} %constant.38.clone.refs_15_) | copy-start | bytes 147460
  16.2 18.7 %copy-start.7 = (bf16[256,256]{1,0:T(8,128)(2,1)S(1)}, bf16[256,256]{1,0:T(8,128)(2,1)}, u32[]{:S(2)}) copy-start(bf16[256,256]{1,0:T(8,128)(2,1)} %constant.35.clone.refs_12_) | copy-start | bytes 393220
  16.2 18.7 %copy-start.8 = (bf16[48,512]{1,0:T(8,128)(2,1)S(1)}, bf16[48,512]{1,0:T(8,128)(2,1)}, u32[]{:S(2)}) copy-start(bf16[48,512]{1,0:T(8,128)(2,1)} %constant.40.clone.refs_17_) | copy-start | bytes 147460
  16.2 18.7 %copy-start.9 = (bf16[32,80]{1,0:T(8,128)(2,1)S(1)}, bf16[32,80]{1,0:T(8,128)(2,1)}, u32[]{:S(2)}) copy-start(bf16[32,80]{1,0:T(8,128)(2,1)} %constant.43.clone.refs_20_) | copy-start | bytes 15364
  22.3 12.5 %copy-start.11 = (bf16[16,64,128]{2,1,0:T(8,128)(2,1)}, bf16[16,64,128]{2,1,0:T(8,128)(2,1)S(1)}, u32[]{:S(2)}) copy-start(bf16[16,64,128]{2,1,0:T(8,128)(2,1)S(1)} %all-to-all-done.refs_2_.refs_3_.refs_4_.refs_5_.refs_6_) | copy-start | bytes 786436
  23.4 11.4 %all-to-all-start.1 = ((f32[16,16,128]{2,1,0:T(8,128)}), f32[16,16,128]{2,1,0:T(8,128)S(1)}, u32[]{:S(2)}, u32[]{:S(2)}) async-start(f32[16,16,128]{2,1,0:T(8,128)} %select_reduce_fusion.1), calls=%async_computation.1 | async-start | bytes 262144 | tf_op jit(solution)/shard_map/all_to_all | solution.py:709
  87.2 16.8 %all-to-all-start.2 = ((bf16[16,112,128]{2,1,0:T(8,128)(2,1)}), bf16[16,112,128]{2,1,0:T(8,128)(2,1)S(1)}, u32[]{:S(2)}, u32[]{:S(2)}) async-start(bf16[16,112,128]{2,1,0:T(8,128)(2,1)} %get-tuple-element.26), calls=%async_computation.2 | async-start | bytes 917504 | tf_op jit(solution)/shard_map/all_to_all | solution.py:709
  90.8 13.3 %collective-permute-start.2 = (f32[16,8,256]{2,1,0:T(8,128)S(1)}, f32[16,8,256]{2,1,0:T(8,128)S(1)}, u32[]{:S(2)}, u32[]{:S(2)}) collective-permute-start(f32[16,8,256]{2,1,0:T(8,128)S(1)} %get-tuple-element.27), channel_id=1, source_target_pairs={{0,1},{1,2},{2,3},{3,4},{4,5},{5,6},{6,7},{7,8},{8,9},{9,10},{10,1... | collective-permute-start | bytes 393224 | tf_op jit(solution)/shard_map/ppermute | solution.py:793
  93.0 11.1 %collective-permute-start.3 = (f32[16,8,256]{2,1,0:T(8,128)S(1)}, f32[16,8,256]{2,1,0:T(8,128)S(1)}, u32[]{:S(2)}, u32[]{:S(2)}) collective-permute-start(f32[16,8,256]{2,1,0:T(8,128)S(1)} %get-tuple-element.28), channel_id=1, source_target_pairs={{1,0},{2,1},{3,2},{4,3},{5,4},{6,5},{7,6},{8,7},{9,8},{10,9},{11,1... | collective-permute-start | bytes 393224 | tf_op jit(solution)/shard_map/ppermute | solution.py:794
  104.1 18.3 %copy-start = (f32[16,192,256]{2,1,0:T(8,128)S(1)}, f32[16,192,256]{2,1,0:T(8,128)}, u32[]{:S(2)}) copy-start(f32[16,192,256]{2,1,0:T(8,128)} %get-tuple-element.30.refs_1_) | copy-start | bytes 9437188

commit v8 on v7

--- a/solution.py
+++ b/solution.py
@@ -349,7 +349,8 @@
         back = backward(done)
         ahead = forward(coarse_refs[u], soon)
         advance(back)
-        later = jnp.concatenate([later_ref[u, 0:8, :], later_ref[u, 8:16, :]], axis=1)
+        later = later_ref[u].astype(F32)
+        later = jnp.concatenate([later[0:8], later[8:16]], axis=1)
         later_high = later.astype(BF).astype(F32)
         later_both = jnp.concatenate([later_high, later - later_high], axis=0).astype(BF)
         aux = [before_ref[u], after_ref[u], later_both, jnp.zeros((16, HALF), BF)]
@@ -563,7 +564,7 @@
     )(ids, tile, *[coarse] * (PER_STEP + 1), fine, cot, before, after, later, *fixed, *weights)
 
 
-EARLY_SLOTS = 4
+EARLY_SLOTS = 8
 
 
 def early_kernel(
@@ -634,7 +635,7 @@
     )(solution, geometry, fine, cot, pick_x, pick_s)
 
 
-FINAL_SLOTS = 4
+FINAL_SLOTS = 8
 PARTS = ((0, 1152), (PROJECT_AT, 128), (UP_AT, 96), (DOWN_AT, 48), (FIRST_AT, 32))
 SHAPES = ((1152, 128), (128, 128), (4, 6, 4, 128), (3, 4, 4, 128), (3, 3, 3, 128))
 

time: 125 us -> 124 us (level)
  Pallas kernels: 58.7 us -> 57.2 us
where the time goes in v8:
time: 124 us; the launch traced here: 123 us
  Pallas kernels  57.2 us (46%)
  starting transfers between devices  21.7 us (18%)
  waiting for transfers between devices  21.7 us (18%)
  blocking collectives  17.7 us (14%)
  local copies, waits for them, and re-layouts  2.07 us (2%)
  other arithmetic  1.52 us (1%)
    pallas_call x1, Pallas kernels, run_slots(): pl.pallas_call(body, grid_spec=grid_spec, out_shape=out_shape, compiler_p...  52.5 us
    all_to_all x3, waiting for transfers between devices, exchanged(): lax.all_to_all(value, 'tile', split_axis=0, concat_axis=0, tiled=True)  21.7 us
    all_to_all x1, blocking collectives, exchanged(): lax.all_to_all(value, 'tile', split_axis=0, concat_axis=0, tiled=True)  17.7 us
    all_to_all x3, starting transfers between devices, exchanged(): lax.all_to_all(value, 'tile', split_axis=0, concat_axis=0, tiled=True)  14.5 us
    pallas_call x1, Pallas kernels, run_early(): pl.pallas_call(body, grid=(slots // EARLY_SLOTS,), in_specs=[whole(soluti...  3.11 us
  transfers between devices with their start and end apart: 7, of which 3 were waited for; matrix products, arithmetic and copies ran while one was open for 2% of the time, Pallas kernels for 0%

profile of v8, /device:TPU:0, one launch (start us, length us, event | category | flops | bytes accessed | tf_op | source)
XLA Modules:
  0.0 123.0 jit_solution(776622566588284467)
XLA Ops:
  0.6 3.1 %shard_map.253 = (bf16[16,64,128]{2,1,0:T(8,128)(2,1)}, bf16[16,16,256]{2,1,0:T(8,128)(2,1)}, bf16[16,16,256]{2,1,0:T(8,128)(2,1)}) custom-call(bf16[1,2,4096]{2,1,0:T(2,128)(2,1)} %refs_0_.2, s32[1,4096]{1,0:T(1,128)} %refs_1_.1, bf16[16,192,256]{2,1,0:T(8,128)(2,1)} %bitcast.25, bf16[16,192,256]{2,1,0:T(8,128)(2,1)} %bitcast.27, ...), custom_call_target="tpu_custom_call" | custom-call | tf_op jit(solution)/shard_map/pallas_call | solution.py:627
  3.8 7.4 %all-to-all-start = ((bf16[16,64,128]{2,1,0:T(8,128)(2,1)}), bf16[16,64,128]{2,1,0:T(8,128)(2,1)S(1)}, u32[]{:S(2)}, u32[]{:S(2)}) async-start(bf16[16,64,128]{2,1,0:T(8,128)(2,1)} %get-tuple-element.23), calls=%async_computation | async-start | bytes 524288 | tf_op jit(solution)/shard_map/all_to_all | solution.py:710
  11.2 2.4 %collective-permute-start = (bf16[16,16,256]{2,1,0:T(8,128)(2,1)}, bf16[16,16,256]{2,1,0:T(8,128)(2,1)S(1)}, u32[]{:S(2)}, u32[]{:S(2)}) collective-permute-start(bf16[16,16,256]{2,1,0:T(8,128)(2,1)} %get-tuple-element.24), channel_id=1, source_target_pairs={{0,1},{1,2},{2,3},{3,4},{4,5},{5,6},{6,7},{7,8},{8,9},{9,10},{10,1... | collective-permute-start | bytes 393224 | tf_op jit(solution)/shard_map/ppermute | solution.py:745
  13.6 1.3 %collective-permute-start.1 = (bf16[16,16,256]{2,1,0:T(8,128)(2,1)}, bf16[16,16,256]{2,1,0:T(8,128)(2,1)S(1)}, u32[]{:S(2)}, u32[]{:S(2)}) collective-permute-start(bf16[16,16,256]{2,1,0:T(8,128)(2,1)} %get-tuple-element.25), channel_id=1, source_target_pairs={{1,0},{2,1},{3,2},{4,3},{5,4},{6,5},{7,6},{8,7},{9,8},{10,9},{11,1... | collective-permute-start | bytes 393224 | tf_op jit(solution)/shard_map/ppermute | solution.py:746
  15.0 0.0 copy-start.3
  15.0 0.0 copy-start.4
  15.0 0.0 copy-start.5
  15.0 0.0 copy-start.6
  15.0 0.0 copy-start.7
  15.0 0.0 copy-start.8
  15.0 0.0 copy-start.9
  15.1 0.2 copy.43
  15.3 0.3 copy.44
  15.6 5.6 %all-to-all-done.refs_2_.refs_3_.refs_4_.refs_5_.refs_6_ = bf16[16,64,128]{2,1,0:T(8,128)(2,1)S(1)} async-done(((bf16[16,64,128]{2,1,0:T(8,128)(2,1)}), bf16[16,64,128]{2,1,0:T(8,128)(2,1)S(1)}, u32[]{:S(2)}, u32[]{:S(2)}) %all-to-all-start) | async-done | bytes 262176 | tf_op jit(solution)/shard_map/all_to_all | solution.py:710
  21.3 1.0 select_reduce_fusion.1
  22.3 3.5 %all-to-all-start.1 = ((f32[16,16,128]{2,1,0:T(8,128)}), f32[16,16,128]{2,1,0:T(8,128)S(1)}, u32[]{:S(2)}, u32[]{:S(2)}) async-start(f32[16,16,128]{2,1,0:T(8,128)} %select_reduce_fusion.1), calls=%async_computation.1 | async-start | bytes 262144 | tf_op jit(solution)/shard_map/all_to_all | solution.py:710
  25.8 0.9 copy_bitcast_fusion
  26.7 0.1 copy.42
  26.8 0.1 copy.46
  27.0 0.1 copy.48
  27.1 0.1 copy.45
  27.3 6.4 %all-to-all-done.1.refs_11_ = f32[16,16,128]{2,1,0:T(8,128)S(1)} async-done(((f32[16,16,128]{2,1,0:T(8,128)}), f32[16,16,128]{2,1,0:T(8,128)S(1)}, u32[]{:S(2)}, u32[]{:S(2)}) %all-to-all-start.1) | async-done | bytes 131104 | tf_op jit(solution)/shard_map/all_to_all | solution.py:710
  33.7 52.5 %shard_map.254 = (f32[16,192,256]{2,1,0:T(8,128)}, f32[16,8,256]{2,1,0:T(8,128)S(1)}, f32[16,8,256]{2,1,0:T(8,128)S(1)}, f32[16,8,256]{2,1,0:T(8,128)S(1)}, bf16[16,112,128]{2,1,0:T(8,128)(2,1)}) custom-call(s32[16]{0:T(128)S(1)} %copy-done.2, s32[1]{0:T(128)} %bitcast.refs_1_, bf16[16,64,128]{2,1,0:T(8,128)(2,1)} %copy-done.11, ...), custom_call_target="tpu_custom_call" | custom-call | flops 32000000000 | bytes 16000000 | tf_op jit(solution)/shard_map/pallas_call | solution.py:556
  86.3 3.6 %all-to-all-start.2 = ((bf16[16,112,128]{2,1,0:T(8,128)(2,1)}), bf16[16,112,128]{2,1,0:T(8,128)(2,1)S(1)}, u32[]{:S(2)}, u32[]{:S(2)}) async-start(bf16[16,112,128]{2,1,0:T(8,128)(2,1)} %get-tuple-element.26), calls=%async_computation.2 | async-start | bytes 917504 | tf_op jit(solution)/shard_map/all_to_all | solution.py:710
  89.9 2.2 %collective-permute-start.2 = (f32[16,8,256]{2,1,0:T(8,128)S(1)}, f32[16,8,256]{2,1,0:T(8,128)S(1)}, u32[]{:S(2)}, u32[]{:S(2)}) collective-permute-start(f32[16,8,256]{2,1,0:T(8,128)S(1)} %get-tuple-element.27), channel_id=1, source_target_pairs={{0,1},{1,2},{2,3},{3,4},{4,5},{5,6},{6,7},{7,8},{8,9},{9,10},{10,1... | collective-permute-start | bytes 393224 | tf_op jit(solution)/shard_map/ppermute | solution.py:794
  92.1 1.3 %collective-permute-start.3 = (f32[16,8,256]{2,1,0:T(8,128)S(1)}, f32[16,8,256]{2,1,0:T(8,128)S(1)}, u32[]{:S(2)}, u32[]{:S(2)}) collective-permute-start(f32[16,8,256]{2,1,0:T(8,128)S(1)} %get-tuple-element.28), channel_id=1, source_target_pairs={{1,0},{2,1},{3,2},{4,3},{5,4},{6,5},{7,6},{8,7},{9,8},{10,9},{11,1... | collective-permute-start | bytes 393224 | tf_op jit(solution)/shard_map/ppermute | solution.py:795
  93.4 9.7 %all-to-all-done.2 = bf16[16,112,128]{2,1,0:T(8,128)(2,1)S(1)} async-done(((bf16[16,112,128]{2,1,0:T(8,128)(2,1)}), bf16[16,112,128]{2,1,0:T(8,128)(2,1)S(1)}, u32[]{:S(2)}, u32[]{:S(2)}) %all-to-all-start.2) | async-done | bytes 458784 | tf_op jit(solution)/shard_map/all_to_all | solution.py:710
  103.1 0.1 convert_element_type.15
  103.2 0.3 select_reduce_fusion
  103.6 0.1 broadcast_in_dim.41
  103.7 17.7 %all_to_all.20.refs_0_ = bf16[16,112,128]{2,1,0:T(8,128)(2,1)S(1)} all-to-all(bf16[16,112,128]{2,1,0:T(8,128)(2,1)S(1)} %pad_maximum_fusion), channel_id=1, replica_groups=mesh['groups'=2,'tile'=16] {'tile'}, dimensions={0} | all-to-all | bytes 917504 | tf_op jit(solution)/shard_map/all_to_all | solution.py:710
  121.4 1.6 %shard_map.255 = (bf16[16,192,256]{2,1,0:T(8,128)(2,1)}, f32[1152,128]{1,0:T(8,128)}, f32[128,128]{1,0:T(8,128)}, f32[4,6,4,128]{3,2,1,0:T(4,128)}, f32[3,4,4,128]{3,2,1,0:T(4,128)}, /*index=5*/f32[3,3,3,128]{3,2,1,0:T(4,128)}) custom-call(bf16[16,112,128]{2,1,0:T(8,128)(2,1)S(1)} %all_to_all.20.refs_0_, f32[16,192,256]{2,1,0:T(8,128)S(1)} %copy-done, ...), custom_call_target="tpu_custom_call" | custom-call | tf_op jit(solution)/shard_map/pallas_call | solution.py:696
  (38 shorter events, 0.3 us)
Async XLA Ops:
  0.6 14.3 %copy-start.10 = (bf16[3,3,128,128]{3,2,1,0:T(8,128)(2,1)S(1)}, bf16[3,3,128,128]{3,2,1,0:T(8,128)(2,1)}, u32[]{:S(2)}) copy-start(bf16[3,3,128,128]{3,2,1,0:T(8,128)(2,1)} %param.28) | copy-start | bytes 884740
  3.8 17.5 %all-to-all-start = ((bf16[16,64,128]{2,1,0:T(8,128)(2,1)}), bf16[16,64,128]{2,1,0:T(8,128)(2,1)S(1)}, u32[]{:S(2)}, u32[]{:S(2)}) async-start(bf16[16,64,128]{2,1,0:T(8,128)(2,1)} %get-tuple-element.23), calls=%async_computation | async-start | bytes 524288 | tf_op jit(solution)/shard_map/all_to_all | solution.py:710
  11.1 15.5 %copy-start.14 = (bf16[3,3,3,128]{3,2,1,0:T(4,128)(2,1)S(1)}, bf16[3,3,3,128]{3,2,1,0:T(4,128)(2,1)}, u32[]{:S(2)}) copy-start(bf16[3,3,3,128]{3,2,1,0:T(4,128)(2,1)} %param.27) | copy-start | bytes 20740
  11.2 15.7 %copy-start.13 = (bf16[3,4,4,128]{3,2,1,0:T(4,128)(2,1)S(1)}, bf16[3,4,4,128]{3,2,1,0:T(4,128)(2,1)}, u32[]{:S(2)}) copy-start(bf16[3,4,4,128]{3,2,1,0:T(4,128)(2,1)} %param.30) | copy-start | bytes 36868
  11.2 15.8 %copy-start.12 = (bf16[4,4,6,128]{3,1,2,0:T(4,128)(2,1)S(1)}, bf16[4,4,6,128]{3,1,2,0:T(4,128)(2,1)}, u32[]{:S(2)}) copy-start(bf16[4,4,6,128]{3,1,2,0:T(4,128)(2,1)} %param.31) | copy-start | bytes 73732
  11.2 16.1 %collective-permute-start = (bf16[16,16,256]{2,1,0:T(8,128)(2,1)}, bf16[16,16,256]{2,1,0:T(8,128)(2,1)S(1)}, u32[]{:S(2)}, u32[]{:S(2)}) collective-permute-start(bf16[16,16,256]{2,1,0:T(8,128)(2,1)} %get-tuple-element.24), channel_id=1, source_target_pairs={{0,1},{1,2},{2,3},{3,4},{4,5},{5,6},{6,7},{7,8},{8,9},{9,10},{10,1... | collective-permute-start | bytes 393224 | tf_op jit(solution)/shard_map/ppermute | solution.py:745
  13.6 13.6 %collective-permute-start.1 = (bf16[16,16,256]{2,1,0:T(8,128)(2,1)}, bf16[16,16,256]{2,1,0:T(8,128)(2,1)S(1)}, u32[]{:S(2)}, u32[]{:S(2)}) collective-permute-start(bf16[16,16,256]{2,1,0:T(8,128)(2,1)} %get-tuple-element.25), channel_id=1, source_target_pairs={{1,0},{2,1},{3,2},{4,3},{5,4},{6,5},{7,6},{8,7},{9,8},{10,9},{11,1... | collective-permute-start | bytes 393224 | tf_op jit(solution)/shard_map/ppermute | solution.py:746
  14.9 12.2 %copy-start.1 = (bf16[128,128]{1,0:T(8,128)(2,1)S(1)}, bf16[128,128]{1,0:T(8,128)(2,1)}, u32[]{:S(2)}) copy-start(bf16[128,128]{1,0:T(8,128)(2,1)} %refs_25_.1) | copy-start | bytes 98308
  15.0 18.7 %copy-start.2 = (s32[16]{0:T(128)S(1)}, s32[16]{0:T(128)}, u32[]{:S(2)}) copy-start(s32[16]{0:T(128)} %refs_0_.3) | copy-start | bytes 196
  15.0 18.7 %copy-start.3 = (bf16[384,256]{1,0:T(8,128)(2,1)S(1)}, bf16[384,256]{1,0:T(8,128)(2,1)}, u32[]{:S(2)}) copy-start(bf16[384,256]{1,0:T(8,128)(2,1)} %constant.44.clone.refs_21_) | copy-start | bytes 589828
  15.0 18.7 %copy-start.4 = (bf16[768,32]{1,0:T(8,128)(2,1)S(1)}, bf16[768,32]{1,0:T(8,128)(2,1)}, u32[]{:S(2)}) copy-start(bf16[768,32]{1,0:T(8,128)(2,1)} %constant.42.clone.refs_19_) | copy-start | bytes 147460
  15.0 18.7 %copy-start.5 = (bf16[96,1024]{1,0:T(8,128)(2,1)S(1)}, bf16[96,1024]{1,0:T(8,128)(2,1)}, u32[]{:S(2)}) copy-start(bf16[96,1024]{1,0:T(8,128)(2,1)} %constant.41.clone.refs_18_) | copy-start | bytes 589828
  15.0 18.7 %copy-start.6 = (bf16[512,48]{1,0:T(8,128)(2,1)S(1)}, bf16[512,48]{1,0:T(8,128)(2,1)}, u32[]{:S(2)}) copy-start(bf16[512,48]{1,0:T(8,128)(2,1)} %constant.38.clone.refs_15_) | copy-start | bytes 147460
  15.0 18.7 %copy-start.7 = (bf16[256,256]{1,0:T(8,128)(2,1)S(1)}, bf16[256,256]{1,0:T(8,128)(2,1)}, u32[]{:S(2)}) copy-start(bf16[256,256]{1,0:T(8,128)(2,1)} %constant.35.clone.refs_12_) | copy-start | bytes 393220
  15.0 18.7 %copy-start.8 = (bf16[48,512]{1,0:T(8,128)(2,1)S(1)}, bf16[48,512]{1,0:T(8,128)(2,1)}, u32[]{:S(2)}) copy-start(bf16[48,512]{1,0:T(8,128)(2,1)} %constant.40.clone.refs_17_) | copy-start | bytes 147460
  15.0 18.7 %copy-start.9 = (bf16[32,80]{1,0:T(8,128)(2,1)S(1)}, bf16[32,80]{1,0:T(8,128)(2,1)}, u32[]{:S(2)}) copy-start(bf16[32,80]{1,0:T(8,128)(2,1)} %constant.43.clone.refs_20_) | copy-start | bytes 15364
  21.2 12.5 %copy-start.11 = (bf16[16,64,128]{2,1,0:T(8,128)(2,1)}, bf16[16,64,128]{2,1,0:T(8,128)(2,1)S(1)}, u32[]{:S(2)}) copy-start(bf16[16,64,128]{2,1,0:T(8,128)(2,1)S(1)} %all-to-all-done.refs_2_.refs_3_.refs_4_.refs_5_.refs_6_) | copy-start | bytes 786436
  22.3 11.4 %all-to-all-start.1 = ((f32[16,16,128]{2,1,0:T(8,128)}), f32[16,16,128]{2,1,0:T(8,128)S(1)}, u32[]{:S(2)}, u32[]{:S(2)}) async-start(f32[16,16,128]{2,1,0:T(8,128)} %select_reduce_fusion.1), calls=%async_computation.1 | async-start | bytes 262144 | tf_op jit(solution)/shard_map/all_to_all | solution.py:710
  86.3 16.8 %all-to-all-start.2 = ((bf16[16,112,128]{2,1,0:T(8,128)(2,1)}), bf16[16,112,128]{2,1,0:T(8,128)(2,1)S(1)}, u32[]{:S(2)}, u32[]{:S(2)}) async-start(bf16[16,112,128]{2,1,0:T(8,128)(2,1)} %get-tuple-element.26), calls=%async_computation.2 | async-start | bytes 917504 | tf_op jit(solution)/shard_map/all_to_all | solution.py:710
  89.9 13.3 %collective-permute-start.2 = (f32[16,8,256]{2,1,0:T(8,128)S(1)}, f32[16,8,256]{2,1,0:T(8,128)S(1)}, u32[]{:S(2)}, u32[]{:S(2)}) collective-permute-start(f32[16,8,256]{2,1,0:T(8,128)S(1)} %get-tuple-element.27), channel_id=1, source_target_pairs={{0,1},{1,2},{2,3},{3,4},{4,5},{5,6},{6,7},{7,8},{8,9},{9,10},{10,1... | collective-permute-start | bytes 393224 | tf_op jit(solution)/shard_map/ppermute | solution.py:794
  92.1 11.1 %collective-permute-start.3 = (f32[16,8,256]{2,1,0:T(8,128)S(1)}, f32[16,8,256]{2,1,0:T(8,128)S(1)}, u32[]{:S(2)}, u32[]{:S(2)}) collective-permute-start(f32[16,8,256]{2,1,0:T(8,128)S(1)} %get-tuple-element.28), channel_id=1, source_target_pairs={{1,0},{2,1},{3,2},{4,3},{5,4},{6,5},{7,6},{8,7},{9,8},{10,9},{11,1... | collective-permute-start | bytes 393224 | tf_op jit(solution)/shard_map/ppermute | solution.py:795
  103.1 18.3 %copy-start = (f32[16,192,256]{2,1,0:T(8,128)S(1)}, f32[16,192,256]{2,1,0:T(8,128)}, u32[]{:S(2)}) copy-start(f32[16,192,256]{2,1,0:T(8,128)} %get-tuple-element.30.refs_1_) | copy-start | bytes 9437188

commit v9 on v8

--- a/solution.py
+++ b/solution.py
@@ -564,7 +564,7 @@
     )(ids, tile, *[coarse] * (PER_STEP + 1), fine, cot, before, after, later, *fixed, *weights)
 
 
-EARLY_SLOTS = 8
+EARLY_SLOTS = 16
 
 
 def early_kernel(

time: 124 us -> 124 us (level)
  no operation moved by 1% of the time
where the time goes in v9:
time: 124 us; the launch traced here: 123 us
  Pallas kernels  57.5 us (46%)
  starting transfers between devices  21.7 us (18%)
  waiting for transfers between devices  21.7 us (18%)
  blocking collectives  17.7 us (14%)
  local copies, waits for them, and re-layouts  2.07 us (2%)
  other arithmetic  1.52 us (1%)
    pallas_call x1, Pallas kernels, run_slots(): pl.pallas_call(body, grid_spec=grid_spec, out_shape=out_shape, compiler_p...  52.5 us
    all_to_all x3, waiting for transfers between devices, exchanged(): lax.all_to_all(value, 'tile', split_axis=0, concat_axis=0, tiled=True)  21.7 us
    all_to_all x1, blocking collectives, exchanged(): lax.all_to_all(value, 'tile', split_axis=0, concat_axis=0, tiled=True)  17.7 us
    all_to_all x3, starting transfers between devices, exchanged(): lax.all_to_all(value, 'tile', split_axis=0, concat_axis=0, tiled=True)  14.5 us
    pallas_call x1, Pallas kernels, run_early(): pl.pallas_call(body, grid=(slots // EARLY_SLOTS,), in_specs=[whole(soluti...  3.42 us
  transfers between devices with their start and end apart: 7, of which 3 were waited for; matrix products, arithmetic and copies ran while one was open for 2% of the time, Pallas kernels for 0%

profile of v9, /device:TPU:0, one launch (start us, length us, event | category | flops | bytes accessed | tf_op | source)
XLA Modules:
  0.0 123.3 jit_solution(7966755288699759533)
XLA Ops:
  0.6 3.4 %shard_map.253 = (bf16[16,64,128]{2,1,0:T(8,128)(2,1)}, bf16[16,16,256]{2,1,0:T(8,128)(2,1)}, bf16[16,16,256]{2,1,0:T(8,128)(2,1)}) custom-call(bf16[1,2,4096]{2,1,0:T(2,128)(2,1)} %refs_0_.2, s32[1,4096]{1,0:T(1,128)} %refs_1_.1, bf16[16,192,256]{2,1,0:T(8,128)(2,1)} %bitcast.25, bf16[16,192,256]{2,1,0:T(8,128)(2,1)} %bitcast.27, ...), custom_call_target="tpu_custom_call" | custom-call | tf_op jit(solution)/shard_map/pallas_call | solution.py:627
  4.1 7.4 %all-to-all-start = ((bf16[16,64,128]{2,1,0:T(8,128)(2,1)}), bf16[16,64,128]{2,1,0:T(8,128)(2,1)S(1)}, u32[]{:S(2)}, u32[]{:S(2)}) async-start(bf16[16,64,128]{2,1,0:T(8,128)(2,1)} %get-tuple-element.23), calls=%async_computation | async-start | bytes 524288 | tf_op jit(solution)/shard_map/all_to_all | solution.py:710
  11.5 2.4 %collective-permute-start = (bf16[16,16,256]{2,1,0:T(8,128)(2,1)}, bf16[16,16,256]{2,1,0:T(8,128)(2,1)S(1)}, u32[]{:S(2)}, u32[]{:S(2)}) collective-permute-start(bf16[16,16,256]{2,1,0:T(8,128)(2,1)} %get-tuple-element.24), channel_id=1, source_target_pairs={{0,1},{1,2},{2,3},{3,4},{4,5},{5,6},{6,7},{7,8},{8,9},{9,10},{10,1... | collective-permute-start | bytes 393224 | tf_op jit(solution)/shard_map/ppermute | solution.py:745
  13.9 1.3 %collective-permute-start.1 = (bf16[16,16,256]{2,1,0:T(8,128)(2,1)}, bf16[16,16,256]{2,1,0:T(8,128)(2,1)S(1)}, u32[]{:S(2)}, u32[]{:S(2)}) collective-permute-start(bf16[16,16,256]{2,1,0:T(8,128)(2,1)} %get-tuple-element.25), channel_id=1, source_target_pairs={{1,0},{2,1},{3,2},{4,3},{5,4},{6,5},{7,6},{8,7},{9,8},{10,9},{11,1... | collective-permute-start | bytes 393224 | tf_op jit(solution)/shard_map/ppermute | solution.py:746
  15.3 0.0 copy-start.3
  15.3 0.0 copy-start.4
  15.3 0.0 copy-start.5
  15.3 0.0 copy-start.6
  15.3 0.0 copy-start.7
  15.3 0.0 copy-start.8
  15.4 0.0 copy-start.9
  15.4 0.2 copy.43
  15.6 0.3 copy.44
  15.9 5.6 %all-to-all-done.refs_2_.refs_3_.refs_4_.refs_5_.refs_6_ = bf16[16,64,128]{2,1,0:T(8,128)(2,1)S(1)} async-done(((bf16[16,64,128]{2,1,0:T(8,128)(2,1)}), bf16[16,64,128]{2,1,0:T(8,128)(2,1)S(1)}, u32[]{:S(2)}, u32[]{:S(2)}) %all-to-all-start) | async-done | bytes 262176 | tf_op jit(solution)/shard_map/all_to_all | solution.py:710
  21.6 1.0 select_reduce_fusion.1
  22.6 3.5 %all-to-all-start.1 = ((f32[16,16,128]{2,1,0:T(8,128)}), f32[16,16,128]{2,1,0:T(8,128)S(1)}, u32[]{:S(2)}, u32[]{:S(2)}) async-start(f32[16,16,128]{2,1,0:T(8,128)} %select_reduce_fusion.1), calls=%async_computation.1 | async-start | bytes 262144 | tf_op jit(solution)/shard_map/all_to_all | solution.py:710
  26.1 0.9 copy_bitcast_fusion
  27.0 0.1 copy.42
  27.1 0.1 copy.46
  27.3 0.1 copy.48
  27.4 0.1 copy.45
  27.6 6.4 %all-to-all-done.1.refs_11_ = f32[16,16,128]{2,1,0:T(8,128)S(1)} async-done(((f32[16,16,128]{2,1,0:T(8,128)}), f32[16,16,128]{2,1,0:T(8,128)S(1)}, u32[]{:S(2)}, u32[]{:S(2)}) %all-to-all-start.1) | async-done | bytes 131104 | tf_op jit(solution)/shard_map/all_to_all | solution.py:710
  34.1 52.5 %shard_map.254 = (f32[16,192,256]{2,1,0:T(8,128)}, f32[16,8,256]{2,1,0:T(8,128)S(1)}, f32[16,8,256]{2,1,0:T(8,128)S(1)}, f32[16,8,256]{2,1,0:T(8,128)S(1)}, bf16[16,112,128]{2,1,0:T(8,128)(2,1)}) custom-call(s32[16]{0:T(128)S(1)} %copy-done.2, s32[1]{0:T(128)} %bitcast.refs_1_, bf16[16,64,128]{2,1,0:T(8,128)(2,1)} %copy-done.11, ...), custom_call_target="tpu_custom_call" | custom-call | flops 32000000000 | bytes 16000000 | tf_op jit(solution)/shard_map/pallas_call | solution.py:556
  86.6 3.6 %all-to-all-start.2 = ((bf16[16,112,128]{2,1,0:T(8,128)(2,1)}), bf16[16,112,128]{2,1,0:T(8,128)(2,1)S(1)}, u32[]{:S(2)}, u32[]{:S(2)}) async-start(bf16[16,112,128]{2,1,0:T(8,128)(2,1)} %get-tuple-element.26), calls=%async_computation.2 | async-start | bytes 917504 | tf_op jit(solution)/shard_map/all_to_all | solution.py:710
  90.2 2.2 %collective-permute-start.2 = (f32[16,8,256]{2,1,0:T(8,128)S(1)}, f32[16,8,256]{2,1,0:T(8,128)S(1)}, u32[]{:S(2)}, u32[]{:S(2)}) collective-permute-start(f32[16,8,256]{2,1,0:T(8,128)S(1)} %get-tuple-element.27), channel_id=1, source_target_pairs={{0,1},{1,2},{2,3},{3,4},{4,5},{5,6},{6,7},{7,8},{8,9},{9,10},{10,1... | collective-permute-start | bytes 393224 | tf_op jit(solution)/shard_map/ppermute | solution.py:794
  92.4 1.3 %collective-permute-start.3 = (f32[16,8,256]{2,1,0:T(8,128)S(1)}, f32[16,8,256]{2,1,0:T(8,128)S(1)}, u32[]{:S(2)}, u32[]{:S(2)}) collective-permute-start(f32[16,8,256]{2,1,0:T(8,128)S(1)} %get-tuple-element.28), channel_id=1, source_target_pairs={{1,0},{2,1},{3,2},{4,3},{5,4},{6,5},{7,6},{8,7},{9,8},{10,9},{11,1... | collective-permute-start | bytes 393224 | tf_op jit(solution)/shard_map/ppermute | solution.py:795
  93.7 9.7 %all-to-all-done.2 = bf16[16,112,128]{2,1,0:T(8,128)(2,1)S(1)} async-done(((bf16[16,112,128]{2,1,0:T(8,128)(2,1)}), bf16[16,112,128]{2,1,0:T(8,128)(2,1)S(1)}, u32[]{:S(2)}, u32[]{:S(2)}) %all-to-all-start.2) | async-done | bytes 458784 | tf_op jit(solution)/shard_map/all_to_all | solution.py:710
  103.4 0.1 convert_element_type.15
  103.5 0.3 select_reduce_fusion
  103.9 0.1 broadcast_in_dim.41
  104.0 17.7 %all_to_all.20.refs_0_ = bf16[16,112,128]{2,1,0:T(8,128)(2,1)S(1)} all-to-all(bf16[16,112,128]{2,1,0:T(8,128)(2,1)S(1)} %pad_maximum_fusion), channel_id=1, replica_groups=mesh['groups'=2,'tile'=16] {'tile'}, dimensions={0} | all-to-all | bytes 917504 | tf_op jit(solution)/shard_map/all_to_all | solution.py:710
  121.7 1.6 %shard_map.255 = (bf16[16,192,256]{2,1,0:T(8,128)(2,1)}, f32[1152,128]{1,0:T(8,128)}, f32[128,128]{1,0:T(8,128)}, f32[4,6,4,128]{3,2,1,0:T(4,128)}, f32[3,4,4,128]{3,2,1,0:T(4,128)}, /*index=5*/f32[3,3,3,128]{3,2,1,0:T(4,128)}) custom-call(bf16[16,112,128]{2,1,0:T(8,128)(2,1)S(1)} %all_to_all.20.refs_0_, f32[16,192,256]{2,1,0:T(8,128)S(1)} %copy-done, ...), custom_call_target="tpu_custom_call" | custom-call | tf_op jit(solution)/shard_map/pallas_call | solution.py:696
  (38 shorter events, 0.3 us)
Async XLA Ops:
  0.6 14.6 %copy-start.10 = (bf16[3,3,128,128]{3,2,1,0:T(8,128)(2,1)S(1)}, bf16[3,3,128,128]{3,2,1,0:T(8,128)(2,1)}, u32[]{:S(2)}) copy-start(bf16[3,3,128,128]{3,2,1,0:T(8,128)(2,1)} %param.28) | copy-start | bytes 884740
  4.1 17.5 %all-to-all-start = ((bf16[16,64,128]{2,1,0:T(8,128)(2,1)}), bf16[16,64,128]{2,1,0:T(8,128)(2,1)S(1)}, u32[]{:S(2)}, u32[]{:S(2)}) async-start(bf16[16,64,128]{2,1,0:T(8,128)(2,1)} %get-tuple-element.23), calls=%async_computation | async-start | bytes 524288 | tf_op jit(solution)/shard_map/all_to_all | solution.py:710
  11.5 15.5 %copy-start.14 = (bf16[3,3,3,128]{3,2,1,0:T(4,128)(2,1)S(1)}, bf16[3,3,3,128]{3,2,1,0:T(4,128)(2,1)}, u32[]{:S(2)}) copy-start(bf16[3,3,3,128]{3,2,1,0:T(4,128)(2,1)} %param.27) | copy-start | bytes 20740
  11.5 15.7 %copy-start.13 = (bf16[3,4,4,128]{3,2,1,0:T(4,128)(2,1)S(1)}, bf16[3,4,4,128]{3,2,1,0:T(4,128)(2,1)}, u32[]{:S(2)}) copy-start(bf16[3,4,4,128]{3,2,1,0:T(4,128)(2,1)} %param.30) | copy-start | bytes 36868
  11.5 15.8 %copy-start.12 = (bf16[4,4,6,128]{3,1,2,0:T(4,128)(2,1)S(1)}, bf16[4,4,6,128]{3,1,2,0:T(4,128)(2,1)}, u32[]{:S(2)}) copy-start(bf16[4,4,6,128]{3,1,2,0:T(4,128)(2,1)} %param.31) | copy-start | bytes 73732
  11.5 16.1 %collective-permute-start = (bf16[16,16,256]{2,1,0:T(8,128)(2,1)}, bf16[16,16,256]{2,1,0:T(8,128)(2,1)S(1)}, u32[]{:S(2)}, u32[]{:S(2)}) collective-permute-start(bf16[16,16,256]{2,1,0:T(8,128)(2,1)} %get-tuple-element.24), channel_id=1, source_target_pairs={{0,1},{1,2},{2,3},{3,4},{4,5},{5,6},{6,7},{7,8},{8,9},{9,10},{10,1... | collective-permute-start | bytes 393224 | tf_op jit(solution)/shard_map/ppermute | solution.py:745
  13.9 13.6 %collective-permute-start.1 = (bf16[16,16,256]{2,1,0:T(8,128)(2,1)}, bf16[16,16,256]{2,1,0:T(8,128)(2,1)S(1)}, u32[]{:S(2)}, u32[]{:S(2)}) collective-permute-start(bf16[16,16,256]{2,1,0:T(8,128)(2,1)} %get-tuple-element.25), channel_id=1, source_target_pairs={{1,0},{2,1},{3,2},{4,3},{5,4},{6,5},{7,6},{8,7},{9,8},{10,9},{11,1... | collective-permute-start | bytes 393224 | tf_op jit(solution)/shard_map/ppermute | solution.py:746
  15.3 12.2 %copy-start.1 = (bf16[128,128]{1,0:T(8,128)(2,1)S(1)}, bf16[128,128]{1,0:T(8,128)(2,1)}, u32[]{:S(2)}) copy-start(bf16[128,128]{1,0:T(8,128)(2,1)} %refs_25_.1) | copy-start | bytes 98308
  15.3 18.7 %copy-start.2 = (s32[16]{0:T(128)S(1)}, s32[16]{0:T(128)}, u32[]{:S(2)}) copy-start(s32[16]{0:T(128)} %refs_0_.3) | copy-start | bytes 196
  15.3 18.7 %copy-start.3 = (bf16[384,256]{1,0:T(8,128)(2,1)S(1)}, bf16[384,256]{1,0:T(8,128)(2,1)}, u32[]{:S(2)}) copy-start(bf16[384,256]{1,0:T(8,128)(2,1)} %constant.44.clone.refs_21_) | copy-start | bytes 589828
  15.3 18.7 %copy-start.4 = (bf16[768,32]{1,0:T(8,128)(2,1)S(1)}, bf16[768,32]{1,0:T(8,128)(2,1)}, u32[]{:S(2)}) copy-start(bf16[768,32]{1,0:T(8,128)(2,1)} %constant.42.clone.refs_19_) | copy-start | bytes 147460
  15.3 18.7 %copy-start.5 = (bf16[96,1024]{1,0:T(8,128)(2,1)S(1)}, bf16[96,1024]{1,0:T(8,128)(2,1)}, u32[]{:S(2)}) copy-start(bf16[96,1024]{1,0:T(8,128)(2,1)} %constant.41.clone.refs_18_) | copy-start | bytes 589828
  15.3 18.7 %copy-start.6 = (bf16[512,48]{1,0:T(8,128)(2,1)S(1)}, bf16[512,48]{1,0:T(8,128)(2,1)}, u32[]{:S(2)}) copy-start(bf16[512,48]{1,0:T(8,128)(2,1)} %constant.38.clone.refs_15_) | copy-start | bytes 147460
  15.3 18.7 %copy-start.7 = (bf16[256,256]{1,0:T(8,128)(2,1)S(1)}, bf16[256,256]{1,0:T(8,128)(2,1)}, u32[]{:S(2)}) copy-start(bf16[256,256]{1,0:T(8,128)(2,1)} %constant.35.clone.refs_12_) | copy-start | bytes 393220
  15.3 18.7 %copy-start.8 = (bf16[48,512]{1,0:T(8,128)(2,1)S(1)}, bf16[48,512]{1,0:T(8,128)(2,1)}, u32[]{:S(2)}) copy-start(bf16[48,512]{1,0:T(8,128)(2,1)} %constant.40.clone.refs_17_) | copy-start | bytes 147460
  15.4 18.7 %copy-start.9 = (bf16[32,80]{1,0:T(8,128)(2,1)S(1)}, bf16[32,80]{1,0:T(8,128)(2,1)}, u32[]{:S(2)}) copy-start(bf16[32,80]{1,0:T(8,128)(2,1)} %constant.43.clone.refs_20_) | copy-start | bytes 15364
  21.5 12.5 %copy-start.11 = (bf16[16,64,128]{2,1,0:T(8,128)(2,1)}, bf16[16,64,128]{2,1,0:T(8,128)(2,1)S(1)}, u32[]{:S(2)}) copy-start(bf16[16,64,128]{2,1,0:T(8,128)(2,1)S(1)} %all-to-all-done.refs_2_.refs_3_.refs_4_.refs_5_.refs_6_) | copy-start | bytes 786436
  22.6 11.4 %all-to-all-start.1 = ((f32[16,16,128]{2,1,0:T(8,128)}), f32[16,16,128]{2,1,0:T(8,128)S(1)}, u32[]{:S(2)}, u32[]{:S(2)}) async-start(f32[16,16,128]{2,1,0:T(8,128)} %select_reduce_fusion.1), calls=%async_computation.1 | async-start | bytes 262144 | tf_op jit(solution)/shard_map/all_to_all | solution.py:710
  86.6 16.8 %all-to-all-start.2 = ((bf16[16,112,128]{2,1,0:T(8,128)(2,1)}), bf16[16,112,128]{2,1,0:T(8,128)(2,1)S(1)}, u32[]{:S(2)}, u32[]{:S(2)}) async-start(bf16[16,112,128]{2,1,0:T(8,128)(2,1)} %get-tuple-element.26), calls=%async_computation.2 | async-start | bytes 917504 | tf_op jit(solution)/shard_map/all_to_all | solution.py:710
  90.2 13.3 %collective-permute-start.2 = (f32[16,8,256]{2,1,0:T(8,128)S(1)}, f32[16,8,256]{2,1,0:T(8,128)S(1)}, u32[]{:S(2)}, u32[]{:S(2)}) collective-permute-start(f32[16,8,256]{2,1,0:T(8,128)S(1)} %get-tuple-element.27), channel_id=1, source_target_pairs={{0,1},{1,2},{2,3},{3,4},{4,5},{5,6},{6,7},{7,8},{8,9},{9,10},{10,1... | collective-permute-start | bytes 393224 | tf_op jit(solution)/shard_map/ppermute | solution.py:794
  92.4 11.1 %collective-permute-start.3 = (f32[16,8,256]{2,1,0:T(8,128)S(1)}, f32[16,8,256]{2,1,0:T(8,128)S(1)}, u32[]{:S(2)}, u32[]{:S(2)}) collective-permute-start(f32[16,8,256]{2,1,0:T(8,128)S(1)} %get-tuple-element.28), channel_id=1, source_target_pairs={{1,0},{2,1},{3,2},{4,3},{5,4},{6,5},{7,6},{8,7},{9,8},{10,9},{11,1... | collective-permute-start | bytes 393224 | tf_op jit(solution)/shard_map/ppermute | solution.py:795
  103.4 18.3 %copy-start = (f32[16,192,256]{2,1,0:T(8,128)S(1)}, f32[16,192,256]{2,1,0:T(8,128)}, u32[]{:S(2)}) copy-start(f32[16,192,256]{2,1,0:T(8,128)} %get-tuple-element.30.refs_1_) | copy-start | bytes 9437188
